TPU v7x, 32 devices: a whole 2x2x4 slice. The times are simulated.
32 devices in a mesh: dp: 4 (over x, core), fsdp: 8 (over z, y).
Axes of the slice: x: 2, y: 2, z: 4, core: 2. Of those that a mesh axis runs over, the one named last changes fastest.
Arguments:
- latents: bfloat16 [128, 64, 1536], P(('dp', 'fsdp')), may hold values from -6 to 6
- media: bfloat16 [576, 48, 1536], P(('dp', 'fsdp')), may hold values from -6 to 6
- frame_counts: int32 [128], P(('dp', 'fsdp')), may hold values from 1 to 8, as said below
- cotangent: bfloat16 [128, 64, 1536], P(('dp', 'fsdp')), may hold values from -6 to 6
- w_qkv: float32 [1536, 3, 1536], P(('dp', 'fsdp')), may hold values from -0.15625 to 0.15625
- m_qkv: float32 [1536, 3, 1536], P(('dp', 'fsdp')), may hold values from -0.00012207031 to 0.00012207031
- v_qkv: float32 [1536, 3, 1536], P(('dp', 'fsdp')), may hold values from 3.532127e-11 to 1.4128508e-10
- w_out: float32 [1536, 1536], P(('dp', 'fsdp')), may hold values from -1.25 to 1.25
- m_out: float32 [1536, 1536], P(('dp', 'fsdp')), may hold values from -0.00012207031 to 0.00012207031
- v_out: float32 [1536, 1536], P(('dp', 'fsdp')), may hold values from 7.064254e-12 to 2.8257017e-11
- w_up: float32 [1536, 6144], P(('dp', 'fsdp')), may hold values from -0.15625 to 0.15625
- m_up: float32 [1536, 6144], P(('dp', 'fsdp')), may hold values from -0.00012207031 to 0.00012207031
- v_up: float32 [1536, 6144], P(('dp', 'fsdp')), may hold values from 3.532127e-11 to 1.4128508e-10
- w_down: float32 [6144, 1536], P(('dp', 'fsdp')), may hold values from -0.078125 to 0.078125
- m_down: float32 [6144, 1536], P(('dp', 'fsdp')), may hold values from -0.00012207031 to 0.00012207031
- v_down: float32 [6144, 1536], P(('dp', 'fsdp')), may hold values from 3.532127e-11 to 1.4128508e-10
- time_table: float32 [1536, 8], P(('dp', 'fsdp')), may hold values from -3 to 3
- m_time: float32 [1536, 8], P(('dp', 'fsdp')), may hold values from -0.00036621094 to 0.00036621094
- v_time: float32 [1536, 8], P(('dp', 'fsdp')), may hold values from 3.1789144e-10 to 1.2715657e-09
- gains: float32 [1536, 3], P(('dp', 'fsdp')), may hold values from 0.3 to 2.5, as said below
- m_gains: float32 [1536, 3], P(('dp', 'fsdp')), may hold values from -0.00036621094 to 0.00036621094
- v_gains: float32 [1536, 3], P(('dp', 'fsdp')), may hold values from 3.1789144e-10 to 1.2715657e-09
Outputs:
- new_latents: bfloat16 [128, 64, 1536], P(('dp', 'fsdp'))
- d_latents: float32 [128, 64, 1536], P(('dp', 'fsdp'))
- grad_norm: float32 [], replicated
- new_w_qkv: float32 [1536, 3, 1536], P(('dp', 'fsdp'))
- new_m_qkv: float32 [1536, 3, 1536], P(('dp', 'fsdp'))
- new_v_qkv: float32 [1536, 3, 1536], P(('dp', 'fsdp'))
- new_w_out: float32 [1536, 1536], P(('dp', 'fsdp'))
- new_m_out: float32 [1536, 1536], P(('dp', 'fsdp'))
- new_v_out: float32 [1536, 1536], P(('dp', 'fsdp'))
- new_w_up: float32 [1536, 6144], P(('dp', 'fsdp'))
- new_m_up: float32 [1536, 6144], P(('dp', 'fsdp'))
- new_v_up: float32 [1536, 6144], P(('dp', 'fsdp'))
- new_w_down: float32 [6144, 1536], P(('dp', 'fsdp'))
- new_m_down: float32 [6144, 1536], P(('dp', 'fsdp'))
- new_v_down: float32 [6144, 1536], P(('dp', 'fsdp'))
- new_time_table: float32 [1536, 8], P(('dp', 'fsdp'))
- new_m_time: float32 [1536, 8], P(('dp', 'fsdp'))
- new_v_time: float32 [1536, 8], P(('dp', 'fsdp'))
- new_gains: float32 [1536, 3], P(('dp', 'fsdp'))
- new_m_gains: float32 [1536, 3], P(('dp', 'fsdp'))
- new_v_gains: float32 [1536, 3], P(('dp', 'fsdp'))
Inputs may be any that keep to these rules, and one draw needn't show every extreme that they name: `frame_counts`: each item slot holds one image of 1 frame or one clip of 8 frames; the frames of one device's 4 slots never exceed 18, and on some device of every draw they fill all 18. Positive gains.
All inputs are finite; a program needn't handle non-finite values.
Results may differ from a plain program's by a relative error of at most 0.022.
Values may be sent and summed in bfloat16 or wider, within the bound.
A program may use at most 320 MiB of HBM per device.

v0:
```python
import jax
import jax.numpy as jnp
from jax import lax
from jax.sharding import PartitionSpec as P

HEADS = 16
STEP = 10


highest = lax.Precision.HIGHEST
norm_eps = 1e-05
clip_limit = 1.0
beta_one = 0.9
beta_two = 0.999
adam_eps = 1e-08
decay_rate = 0.1


def layer_norm(values_in, gain):
    mean_row = jnp.mean(values_in, axis=-1, keepdims=True)
    centered = values_in - mean_row
    var_row = jnp.mean(centered * centered, axis=-1, keepdims=True)
    return centered * lax.rsqrt(var_row + norm_eps) * gain


def exact_gelu(values_in):
    return jax.nn.gelu(values_in, approximate=False)


def frame_tables(counts, frame_slots, time_len):
    slot_total = counts.shape[0]
    slot_ends = jnp.cumsum(counts)
    slot_starts = slot_ends - counts
    frame_ids = jnp.arange(frame_slots, dtype=jnp.int32)
    frame_owner = jnp.sum((frame_ids[:, None] >= slot_ends[None, :]).astype(jnp.int32), axis=1)
    slot_ids = jnp.arange(slot_total, dtype=jnp.int32)
    start_of = jnp.sum(
        jnp.where(frame_owner[:, None] == slot_ids[None, :], slot_starts[None, :], 0), axis=1
    )
    time_index = frame_ids - start_of
    live_frame = frame_owner < slot_total
    time_ids = jnp.arange(time_len, dtype=jnp.int32)
    time_hot = ((time_index[:, None] == time_ids[None, :]) & live_frame[:, None]).astype(
        jnp.float32
    )
    return (frame_owner, time_hot)


def gather_params(part_qkv, part_out, part_up, part_down, part_time, part_gains):
    inner_part = (
        lax.all_gather(part_qkv, "fsdp", axis=0, tiled=True),
        lax.all_gather(part_out, "fsdp", axis=0, tiled=True),
        lax.all_gather(part_up, "fsdp", axis=0, tiled=True),
        lax.all_gather(part_down, "fsdp", axis=0, tiled=True),
        lax.all_gather(part_time, "fsdp", axis=0, tiled=True),
        lax.all_gather(part_gains, "fsdp", axis=0, tiled=True),
    )
    return (
        lax.all_gather(inner_part[0], "dp", axis=0, tiled=True),
        lax.all_gather(inner_part[1], "dp", axis=0, tiled=True),
        lax.all_gather(inner_part[2], "dp", axis=0, tiled=True),
        lax.all_gather(inner_part[3], "dp", axis=0, tiled=True),
        lax.all_gather(inner_part[4], "dp", axis=0, tiled=True),
        lax.all_gather(inner_part[5], "dp", axis=0, tiled=True),
    )


def reduce_grads(grad_qkv, grad_out, grad_up, grad_down, grad_time, grad_gains):
    outer_part = (
        lax.psum_scatter(
            grad_qkv.astype(jnp.bfloat16), "dp", scatter_dimension=0, tiled=True
        ).astype(jnp.float32),
        lax.psum_scatter(
            grad_out.astype(jnp.bfloat16), "dp", scatter_dimension=0, tiled=True
        ).astype(jnp.float32),
        lax.psum_scatter(
            grad_up.astype(jnp.bfloat16), "dp", scatter_dimension=0, tiled=True
        ).astype(jnp.float32),
        lax.psum_scatter(
            grad_down.astype(jnp.bfloat16), "dp", scatter_dimension=0, tiled=True
        ).astype(jnp.float32),
        lax.psum_scatter(
            grad_time.astype(jnp.bfloat16), "dp", scatter_dimension=0, tiled=True
        ).astype(jnp.float32),
        lax.psum_scatter(
            grad_gains.astype(jnp.bfloat16), "dp", scatter_dimension=0, tiled=True
        ).astype(jnp.float32),
    )
    return (
        lax.psum_scatter(
            outer_part[0].astype(jnp.bfloat16), "fsdp", scatter_dimension=0, tiled=True
        ).astype(jnp.float32),
        lax.psum_scatter(
            outer_part[1].astype(jnp.bfloat16), "fsdp", scatter_dimension=0, tiled=True
        ).astype(jnp.float32),
        lax.psum_scatter(
            outer_part[2].astype(jnp.bfloat16), "fsdp", scatter_dimension=0, tiled=True
        ).astype(jnp.float32),
        lax.psum_scatter(
            outer_part[3].astype(jnp.bfloat16), "fsdp", scatter_dimension=0, tiled=True
        ).astype(jnp.float32),
        lax.psum_scatter(
            outer_part[4].astype(jnp.bfloat16), "fsdp", scatter_dimension=0, tiled=True
        ).astype(jnp.float32),
        lax.psum_scatter(
            outer_part[5].astype(jnp.bfloat16), "fsdp", scatter_dimension=0, tiled=True
        ).astype(jnp.float32),
    )


def masked_scores(q_heads, k_heads, allowed, score_scale):
    scores = (
        jnp.einsum("qhe,khe->hqk", q_heads, k_heads, preferred_element_type=jnp.float32)
        * score_scale
    )
    return jnp.where(allowed[None, :, :], scores, -1e30)


def adamw_step(weight, first, second, grad, factor, rate):
    clipped = grad * factor
    first_new = beta_one * first + (1.0 - beta_one) * clipped
    second_new = beta_two * second + (1.0 - beta_two) * clipped * clipped
    first_hat = first_new / (1.0 - beta_one**STEP)
    second_hat = second_new / (1.0 - beta_two**STEP)
    weight_new = weight - rate * (
        first_hat / (jnp.sqrt(second_hat) + adam_eps) + decay_rate * weight
    )
    return (weight_new, first_new, second_new)


def on_device(
    latents,
    media,
    frame_counts,
    cotangent,
    w_qkv,
    m_qkv,
    v_qkv,
    w_out,
    m_out,
    v_out,
    w_up,
    m_up,
    v_up,
    w_down,
    m_down,
    v_down,
    time_table,
    m_time,
    v_time,
    gains,
    m_gains,
    v_gains,
):
    low_qkv = w_qkv.astype(jnp.bfloat16)
    low_out = w_out.astype(jnp.bfloat16)
    low_up = w_up.astype(jnp.bfloat16)
    low_down = w_down.astype(jnp.bfloat16)
    low_time = time_table.astype(jnp.bfloat16)
    low_gains = gains.astype(jnp.bfloat16)
    full_qkv, full_out, full_up, full_down, full_time, full_gains = gather_params(
        low_qkv, low_out, low_up, low_down, low_time, low_gains
    )
    item_slots, lat_count, model_width = latents.shape
    frame_slots, patch_rows, unused_width = media.shape
    queries_n = item_slots * lat_count
    media_rows = frame_slots * patch_rows
    head_size = model_width // HEADS
    score_scale = 1.0 / head_size**0.5
    frame_owner, time_hot = frame_tables(frame_counts, frame_slots, full_time.shape[1])
    time_f32 = full_time.astype(jnp.float32)
    gains_f32 = full_gains.astype(jnp.float32)
    frame_time = jnp.dot(time_hot, time_f32.T, precision=highest)
    mixed = media.astype(jnp.float32) + frame_time[:, None, :]
    media_norm, media_back = jax.vjp(layer_norm, mixed, gains_f32[:, 0])
    media_low = media_norm.astype(jnp.bfloat16).reshape(media_rows, model_width)
    lat_rows = latents.reshape(queries_n, model_width).astype(jnp.float32)
    lat_norm, lat_back = jax.vjp(layer_norm, lat_rows, gains_f32[:, 1])
    lat_low = lat_norm.astype(jnp.bfloat16)
    keys_in = jnp.concatenate([media_low, lat_low], axis=0)
    key_rows = keys_in.shape[0]
    qkv_flat = full_qkv.reshape(model_width, 3 * model_width)
    queries = jnp.dot(
        lat_low, qkv_flat[:, :model_width], preferred_element_type=jnp.float32
    ).astype(jnp.bfloat16)
    key_value = jnp.dot(
        keys_in, qkv_flat[:, model_width:], preferred_element_type=jnp.float32
    ).astype(jnp.bfloat16)
    q_heads = queries.reshape(queries_n, HEADS, head_size)
    k_heads = key_value[:, :model_width].reshape(key_rows, HEADS, head_size)
    v_heads = key_value[:, model_width:].reshape(key_rows, HEADS, head_size)
    query_owner = jnp.arange(queries_n, dtype=jnp.int32) // lat_count
    key_owner = jnp.concatenate([jnp.repeat(frame_owner, patch_rows), query_owner], axis=0)
    allowed = query_owner[:, None] == key_owner[None, :]
    scores = masked_scores(q_heads, k_heads, allowed, score_scale)
    row_top = jnp.max(scores, axis=-1, keepdims=True)
    row_total = jnp.sum(jnp.exp(scores - row_top), axis=-1, keepdims=True)
    log_total = row_top + jnp.log(row_total)
    probs_low = jnp.exp(scores - log_total).astype(jnp.bfloat16)
    attended = jnp.einsum("hqk,khe->qhe", probs_low, v_heads, preferred_element_type=jnp.float32)
    attended = attended.reshape(queries_n, model_width).astype(jnp.bfloat16)
    middle = lat_rows + jnp.dot(attended, full_out, preferred_element_type=jnp.float32)
    hidden, ffn_back = jax.vjp(layer_norm, middle, gains_f32[:, 2])
    hidden_low = hidden.astype(jnp.bfloat16)
    pre_act = jnp.dot(hidden_low, full_up, preferred_element_type=jnp.float32)
    activated, gelu_back = jax.vjp(exact_gelu, pre_act)
    act_low = activated.astype(jnp.bfloat16)
    result = middle + jnp.dot(act_low, full_down, preferred_element_type=jnp.float32)
    new_latents = result.astype(jnp.bfloat16).reshape(item_slots, lat_count, model_width)
    back_qkv, back_out, back_up, back_down, back_time, back_gains = gather_params(
        low_qkv, low_out, low_up, low_down, low_time, low_gains
    )
    d_result = cotangent.reshape(queries_n, model_width)
    g_down = jnp.einsum("qf,qd->fd", act_low, d_result, preferred_element_type=jnp.float32)
    d_act = jnp.einsum("qd,fd->qf", d_result, back_down, preferred_element_type=jnp.float32)
    d_pre = gelu_back(d_act)[0].astype(jnp.bfloat16)
    g_up = jnp.einsum("qd,qf->df", hidden_low, d_pre, preferred_element_type=jnp.float32)
    d_hidden = jnp.einsum("qf,df->qd", d_pre, back_up, preferred_element_type=jnp.float32)
    d_middle_ln, g_gain_ffn = ffn_back(d_hidden)
    d_middle = d_result.astype(jnp.float32) + d_middle_ln
    d_branch = d_middle.astype(jnp.bfloat16)
    g_out = jnp.einsum("qe,qd->ed", attended, d_branch, preferred_element_type=jnp.float32)
    d_attended = jnp.einsum(
        "qd,ed->qe", d_branch, back_out, preferred_element_type=jnp.float32
    ).astype(jnp.bfloat16)
    scores_again = masked_scores(q_heads, k_heads, allowed, score_scale)
    probs = jnp.exp(scores_again - log_total)
    probs_again = probs.astype(jnp.bfloat16)
    d_att_heads = d_attended.reshape(queries_n, HEADS, head_size)
    d_probs = jnp.einsum("qhe,khe->hqk", d_att_heads, v_heads, preferred_element_type=jnp.float32)
    row_dot = jnp.sum(probs * d_probs, axis=-1, keepdims=True)
    d_scores = (probs * (d_probs - row_dot)).astype(jnp.bfloat16)
    d_queries = (
        (
            jnp.einsum("hqk,khe->qhe", d_scores, k_heads, preferred_element_type=jnp.float32)
            * score_scale
        )
        .reshape(queries_n, model_width)
        .astype(jnp.bfloat16)
    )
    d_keys = (
        (
            jnp.einsum("hqk,qhe->khe", d_scores, q_heads, preferred_element_type=jnp.float32)
            * score_scale
        )
        .reshape(key_rows, model_width)
        .astype(jnp.bfloat16)
    )
    d_values = (
        jnp.einsum("hqk,qhe->khe", probs_again, d_att_heads, preferred_element_type=jnp.float32)
        .reshape(key_rows, model_width)
        .astype(jnp.bfloat16)
    )
    g_query = jnp.einsum("qd,qe->de", lat_low, d_queries, preferred_element_type=jnp.float32)
    d_key_value = jnp.concatenate([d_keys, d_values], axis=1)
    g_key_value = jnp.einsum("kd,kx->dx", keys_in, d_key_value, preferred_element_type=jnp.float32)
    g_qkv = jnp.concatenate([g_query, g_key_value], axis=1).reshape(model_width, 3, model_width)
    back_flat = back_qkv.reshape(model_width, 3 * model_width)
    d_keys_in = jnp.einsum(
        "kx,dx->kd", d_key_value, back_flat[:, model_width:], preferred_element_type=jnp.float32
    )
    d_lat_norm = (
        jnp.einsum(
            "qe,de->qd", d_queries, back_flat[:, :model_width], preferred_element_type=jnp.float32
        )
        + d_keys_in[media_rows:]
    )
    d_lat_ln, g_gain_lat = lat_back(d_lat_norm)
    d_latents = (d_middle + d_lat_ln).reshape(item_slots, lat_count, model_width)
    d_mixed, g_gain_media = media_back(
        d_keys_in[:media_rows].reshape(frame_slots, patch_rows, model_width)
    )
    frame_grad = jnp.sum(d_mixed, axis=1)
    g_time = jnp.einsum("fd,ft->dt", frame_grad, time_hot, precision=highest)
    g_gains = jnp.stack([g_gain_media, g_gain_lat, g_gain_ffn], axis=1)
    reduced = reduce_grads(g_qkv, g_out, g_up, g_down, g_time, g_gains)
    local_sq = jnp.zeros((), jnp.float32)
    for grad in reduced:
        local_sq = local_sq + jnp.sum(grad * grad)
    grad_norm = jnp.sqrt(lax.psum(local_sq, ("dp", "fsdp")))
    factor = jnp.minimum(1.0, clip_limit / (grad_norm + 1e-06))
    masters = (w_qkv, w_out, w_up, w_down, time_table, gains)
    firsts = (m_qkv, m_out, m_up, m_down, m_time, m_gains)
    seconds = (v_qkv, v_out, v_up, v_down, v_time, v_gains)
    rates = (0.02, 0.1, 0.02, 0.01, 0.2, 0.5)
    updated = []
    for index in range(6):
        updated.extend(
            adamw_step(
                masters[index], firsts[index], seconds[index], reduced[index], factor, rates[index]
            )
        )
    return (
        new_latents,
        d_latents,
        grad_norm,
        updated[0],
        updated[1],
        updated[2],
        updated[3],
        updated[4],
        updated[5],
        updated[6],
        updated[7],
        updated[8],
        updated[9],
        updated[10],
        updated[11],
        updated[12],
        updated[13],
        updated[14],
        updated[15],
        updated[16],
        updated[17],
    )


def solution(mesh):
    placed = (
        P(("dp", "fsdp"), None, None),
        P(("dp", "fsdp"), None, None),
        P(("dp", "fsdp")),
        P(("dp", "fsdp"), None, None),
        P(("dp", "fsdp"), None, None),
        P(("dp", "fsdp"), None, None),
        P(("dp", "fsdp"), None, None),
        P(("dp", "fsdp"), None),
        P(("dp", "fsdp"), None),
        P(("dp", "fsdp"), None),
        P(("dp", "fsdp"), None),
        P(("dp", "fsdp"), None),
        P(("dp", "fsdp"), None),
        P(("dp", "fsdp"), None),
        P(("dp", "fsdp"), None),
        P(("dp", "fsdp"), None),
        P(("dp", "fsdp"), None),
        P(("dp", "fsdp"), None),
        P(("dp", "fsdp"), None),
        P(("dp", "fsdp"), None),
        P(("dp", "fsdp"), None),
        P(("dp", "fsdp"), None),
    )
    return jax.shard_map(
        on_device,
        mesh=mesh,
        in_specs=placed,
        out_specs=(
            P(("dp", "fsdp"), None, None),
            P(("dp", "fsdp"), None, None),
            P(),
            P(("dp", "fsdp"), None, None),
            P(("dp", "fsdp"), None, None),
            P(("dp", "fsdp"), None, None),
            P(("dp", "fsdp"), None),
            P(("dp", "fsdp"), None),
            P(("dp", "fsdp"), None),
            P(("dp", "fsdp"), None),
            P(("dp", "fsdp"), None),
            P(("dp", "fsdp"), None),
            P(("dp", "fsdp"), None),
            P(("dp", "fsdp"), None),
            P(("dp", "fsdp"), None),
            P(("dp", "fsdp"), None),
            P(("dp", "fsdp"), None),
            P(("dp", "fsdp"), None),
            P(("dp", "fsdp"), None),
            P(("dp", "fsdp"), None),
            P(("dp", "fsdp"), None),
        ),
        check_vma=False,
    )
```

profile of v0, /device:TPU:0, one launch (start us, length us, event | category | flops | bytes accessed | tf_op | source)
XLA Modules:
  0.0 1890.9 jit_solution(5706644227998352457)
XLA Ops:
  14.3 64.4 %all-gather.11.cloned.1.call-done = bf16[384,3,1536]{2,0,1:T(8,128)(2,1)} async-done(((bf16[48,3,1536]{2,0,1:T(8,128)(2,1)}), bf16[384,3,1536]{2,0,1:T(8,128)(2,1)}) %all-gather.11.cloned.1.call-update) | async-done | bytes 3538960 | tf_op jit(solution)/shard_map/all_gather | solution.py:51
  84.8 36.2 %all-gather.15.cloned.1.call-done = bf16[384,1536]{1,0:T(8,128)(2,1)} async-done(((bf16[48,1536]{1,0:T(8,128)(2,1)}), bf16[384,1536]{1,0:T(8,128)(2,1)}) %all-gather.15.cloned.1.call-update) | async-done | bytes 1179664 | tf_op jit(solution)/shard_map/all_gather | solution.py:52
  121.1 81.4 %all-gather.19.cloned.1.call-done = bf16[384,6144]{1,0:T(8,128)(2,1)} async-done(((bf16[48,6144]{1,0:T(8,128)(2,1)}), bf16[384,6144]{1,0:T(8,128)(2,1)}) %all-gather.19.cloned.1.call-update) | async-done | bytes 4718608 | tf_op jit(solution)/shard_map/all_gather | solution.py:53
  202.6 80.6 %all-gather.23.cloned.1.call-done = bf16[1536,1536]{1,0:T(8,128)(2,1)} async-done(((bf16[192,1536]{1,0:T(8,128)(2,1)}), bf16[1536,1536]{1,0:T(8,128)(2,1)}) %all-gather.23.cloned.1.call-update) | async-done | bytes 4718608 | tf_op jit(solution)/shard_map/all_gather | solution.py:54
  285.1 17.7 all-gather.1
  308.6 26.0 %all-gather = bf16[8,48,8]{1,2,0:T(8,128)(2,1)S(1)} all-gather(bf16[1,48,8]{1,2,0:T(8,128)(2,1)S(1)} %convert_bitcast_fusion), channel_id=1, replica_groups=mesh['dp'=4,'fsdp'=8] {'fsdp'}, dimensions={0}, use_global_device_ids=true | all-gather | bytes 6912 | tf_op jit(solution)/shard_map/all_gather | solution.py:55
  347.8 26.0 %all-gather.13.cloned.1.call-done = bf16[1536,3,1536]{0,2,1:T(8,128)(2,1)} async-done(((bf16[384,3,1536]{0,2,1:T(8,128)(2,1)}), bf16[1536,3,1536]{0,2,1:T(8,128)(2,1)}) %all-gather.13.cloned.1.call-update) | async-done | bytes 14155792 | tf_op jit(solution)/shard_map/all_gather | solution.py:59
  380.8 14.0 convolution_convert_fusion.3
  451.4 82.9 %all-gather.21.cloned.1.call-done = bf16[1536,6144]{1,0:T(8,128)(2,1)} async-done(((bf16[384,6144]{1,0:T(8,128)(2,1)}), bf16[1536,6144]{1,0:T(8,128)(2,1)}) %all-gather.21.cloned.1.call-update) | async-done | bytes 18874384 | tf_op jit(solution)/shard_map/all_gather | solution.py:61
  545.7 110.2 %all-gather.25.cloned.1.call-done = bf16[6144,1536]{1,0:T(8,128)(2,1)} async-done(((bf16[1536,1536]{1,0:T(8,128)(2,1)}), bf16[6144,1536]{1,0:T(8,128)(2,1)}) %all-gather.25.cloned.1.call-update) | async-done | bytes 18874384 | tf_op jit(solution)/shard_map/all_gather | solution.py:62
  655.9 23.4 %add_convert_fusion = (bf16[256,6144]{1,0:T(8,128)(2,1)}, f32[256,6144]{1,0:T(8,128)}) fusion(f32[256,6144]{1,0:T(8,128)} %fusion.72, bf16[256,1536]{1,0:T(8,128)(2,1)} %bitcast.108, bf16[6144,1536]{1,0:T(8,128)(2,1)} %all-gather.25.cloned.1.call-done), kind=kOutput, calls=%fused_computation.22 | convolution fusion | flops 4945084416 | bytes 35389440 | tf_op jit(solution)/shard_map/qd,fd->qf/dot_general | solution.py:215
  743.8 15.7 fusion.2
  789.8 18.2 convolution_convert_fusion.2
  852.3 16.1 reduce-scatter.22.cloned.1.call-done
  868.4 112.1 %reduce-scatter.34.cloned.1.call-done = bf16[384,4608]{1,0:T(8,128)(2,1)} async-done(((bf16[1536,4608]{1,0:T(8,128)(2,1)}), bf16[384,4608]{1,0:T(8,128)(2,1)}) %reduce-scatter.34.cloned.1.call-update) | async-done | bytes 3538960
  995.3 127.4 %reduce-scatter.26.cloned.1.call-done = bf16[384,6144]{1,0:T(8,128)(2,1)} async-done(((bf16[1536,6144]{1,0:T(8,128)(2,1)}), bf16[384,6144]{1,0:T(8,128)(2,1)}) %reduce-scatter.26.cloned.1.call-update) | async-done | bytes 4718608 | tf_op jit(solution)/shard_map/reduce_scatter | solution.py:76
  1122.9 141.9 %reduce-scatter.30.cloned.1.call-done = bf16[1536,1536]{1,0:T(8,128)(2,1)} async-done(((bf16[6144,1536]{1,0:T(8,128)(2,1)}), bf16[1536,1536]{1,0:T(8,128)(2,1)}) %reduce-scatter.30.cloned.1.call-update) | async-done | bytes 4718608 | tf_op jit(solution)/shard_map/reduce_scatter | solution.py:79
  1276.7 49.2 %reduce-scatter.42.cloned.1.call-done = bf16[48,3]{1,0:T(8,128)(2,1)} async-done(((bf16[384,3]{1,0:T(8,128)(2,1)}), bf16[48,3]{1,0:T(8,128)(2,1)}) %reduce-scatter.42.cloned.1.call-update) | async-done | bytes 304
  1327.3 58.7 %reduce-scatter.38.cloned.1.call-done = bf16[48,8]{1,0:T(8,128)(2,1)} async-done(((bf16[384,8]{1,0:T(8,128)(2,1)}), bf16[48,8]{1,0:T(8,128)(2,1)}) %reduce-scatter.38.cloned.1.call-update) | async-done | bytes 784
  1387.4 65.3 %reduce-scatter.24.cloned.1.call-done = bf16[48,1536]{1,0:T(8,128)(2,1)} async-done(((bf16[384,1536]{1,0:T(8,128)(2,1)}), bf16[48,1536]{1,0:T(8,128)(2,1)}) %reduce-scatter.24.cloned.1.call-update) | async-done | bytes 147472 | tf_op jit(solution)/shard_map/reduce_scatter | solution.py:93
  1454.3 171.0 %all-reduce.3.cloned.1.call-done = bf16[384,3,1536]{2,1,0:T(4,128)(2,1)} async-done(((bf16[384,3,1536]{2,1,0:T(4,128)(2,1)}), bf16[384,3,1536]{2,1,0:T(4,128)(2,1)}) %all-reduce.3.cloned.1.call-update) | async-done | bytes 3538960
  1628.7 95.0 %reduce-scatter.28.cloned.1.call-done = bf16[48,6144]{1,0:T(8,128)(2,1)} async-done(((bf16[384,6144]{1,0:T(8,128)(2,1)}), bf16[48,6144]{1,0:T(8,128)(2,1)}) %reduce-scatter.28.cloned.1.call-update) | async-done | bytes 589840 | tf_op jit(solution)/shard_map/reduce_scatter | solution.py:96
  1726.3 96.4 %reduce-scatter.32.cloned.1.call-done = bf16[192,1536]{1,0:T(8,128)(2,1)} async-done(((bf16[1536,1536]{1,0:T(8,128)(2,1)}), bf16[192,1536]{1,0:T(8,128)(2,1)}) %reduce-scatter.32.cloned.1.call-update) | async-done | bytes 589840 | tf_op jit(solution)/shard_map/reduce_scatter | solution.py:99
  1830.4 40.5 %psum.7 = f32[]{:T(128)} all-reduce(f32[]{:T(128)S(6)} %add.224), channel_id=1, replica_groups=mesh['dp'=4,'fsdp'=8] {'dp','fsdp'}, use_global_device_ids=true, to_apply=%region_40.41 | all-reduce | flops 1 | bytes 8 | tf_op jit(solution)/shard_map/psum | solution.py:280
  (327 shorter events, 298.6 us)
Async XLA Ops:
  7.2 71.5 %all-gather.11.cloned.1.call-start = ((), (), s32[]{:S(2)}) async-start(), calls=%async_computation.11 | async-start | bytes 3981312 | tf_op jit(solution)/shard_map/all_gather | solution.py:51
  9.3 111.7 %all-gather.15.cloned.1.call-start = ((), (), s32[]{:S(2)}) async-start(), calls=%async_computation.13 | async-start | bytes 1327104 | tf_op jit(solution)/shard_map/all_gather | solution.py:52
  11.1 191.4 %all-gather.19.cloned.1.call-start = ((), (), s32[]{:S(2)}) async-start(), calls=%async_computation.15 | async-start | bytes 5308416 | tf_op jit(solution)/shard_map/all_gather | solution.py:53
  13.3 269.9 %all-gather.23.cloned.1.call-start = ((), (), s32[]{:S(2)}) async-start(), calls=%async_computation.17 | async-start | bytes 5308416 | tf_op jit(solution)/shard_map/all_gather | solution.py:54
  14.2 359.5 %all-gather.13.cloned.1.call-start = ((), (), s32[]{:S(2)}) async-start(), calls=%async_computation.12 | async-start | bytes 17694720 | tf_op jit(solution)/shard_map/all_gather | solution.py:59
  84.8 359.6 %all-gather.17.cloned.1.call-start = ((), (), s32[]{:S(2)}) async-start(), calls=%async_computation.14 | async-start | bytes 5898240 | tf_op jit(solution)/shard_map/all_gather | solution.py:60
  121.1 413.2 %all-gather.21.cloned.1.call-start = ((), (), s32[]{:S(2)}) async-start(), calls=%async_computation.16 | async-start | bytes 23592960 | tf_op jit(solution)/shard_map/all_gather | solution.py:61
  202.5 453.4 %all-gather.25.cloned.1.call-start = ((), (), s32[]{:S(2)}) async-start(), calls=%async_computation.18 | async-start | bytes 23592960 | tf_op jit(solution)/shard_map/all_gather | solution.py:62
  283.2 567.9 %reduce-scatter.40.cloned.1.call-start = ((), (), s32[]{:S(2)}) async-start(), calls=%async_computation.28 | async-start | bytes 491520
  773.1 78.5 %reduce-scatter.36.cloned.1.call-start = ((), (), s32[]{:S(2)}) async-start(), calls=%async_computation.26 | async-start | bytes 491520
  774.7 93.7 %reduce-scatter.22.cloned.1.call-start = ((), (), s32[]{:S(2)}) async-start(), calls=%async_computation.19 | async-start | bytes 5898240 | tf_op jit(solution)/shard_map/reduce_scatter | solution.py:73
  778.3 202.2 %reduce-scatter.34.cloned.1.call-start = ((), (), s32[]{:S(2)}) async-start(), calls=%async_computation.25 | async-start | bytes 17694720
  820.6 302.2 %reduce-scatter.26.cloned.1.call-start = ((), (), s32[]{:S(2)}) async-start(), calls=%async_computation.21 | async-start | bytes 23592960 | tf_op jit(solution)/shard_map/reduce_scatter | solution.py:76
  834.2 430.5 %reduce-scatter.30.cloned.1.call-start = ((), (), s32[]{:S(2)}) async-start(), calls=%async_computation.23 | async-start | bytes 23592960 | tf_op jit(solution)/shard_map/reduce_scatter | solution.py:79
  851.0 474.8 %reduce-scatter.42.cloned.1.call-start = ((), (), s32[]{:S(2)}) async-start(), calls=%async_computation.29 | async-start | bytes 110592
  851.6 534.4 %reduce-scatter.38.cloned.1.call-start = ((), (), s32[]{:S(2)}) async-start(), calls=%async_computation.27 | async-start | bytes 110592
  852.2 600.5 %reduce-scatter.24.cloned.1.call-start = ((), (), s32[]{:S(2)}) async-start(), calls=%async_computation.20 | async-start | bytes 1327104 | tf_op jit(solution)/shard_map/reduce_scatter | solution.py:93
  868.4 756.9 %all-reduce.3.cloned.1.call-start = ((), (), s32[]{:S(2)}) async-start(), calls=%async_computation.30 | async-start | bytes 9437184
  995.3 728.4 %reduce-scatter.28.cloned.1.call-start = ((), (), s32[]{:S(2)}) async-start(), calls=%async_computation.22 | async-start | bytes 5308416 | tf_op jit(solution)/shard_map/reduce_scatter | solution.py:96
  1122.8 699.8 %reduce-scatter.32.cloned.1.call-start = ((), (), s32[]{:S(2)}) async-start(), calls=%async_computation.24 | async-start | bytes 5308416 | tf_op jit(solution)/shard_map/reduce_scatter | solution.py:99
  1266.0 560.5 %copy-start.65 = (f32[256]{0:T(256)S(1)}, f32[256]{0:T(256)}, u32[]{:S(2)}) copy-start(f32[256]{0:T(256)} %copy-done.64) | copy-start | bytes 3076
  1327.3 544.3 %copy-start.72 = (f32[48,3]{0,1:T(4,128)S(1)}, f32[48,3]{0,1:T(4,128)}, u32[]{:S(2)}) copy-start(f32[48,3]{0,1:T(4,128)} %param.41) | copy-start | bytes 1732
  1327.3 544.3 %copy-start.76 = (f32[48,3]{0,1:T(4,128)S(1)}, f32[48,3]{0,1:T(4,128)}, u32[]{:S(2)}) copy-start(f32[48,3]{0,1:T(4,128)} %param.42) | copy-start | bytes 1732
  1327.3 544.3 %copy-start.77 = (f32[48,3]{0,1:T(4,128)S(1)}, f32[48,3]{0,1:T(4,128)}, u32[]{:S(2)}) copy-start(f32[48,3]{0,1:T(4,128)} %param.43) | copy-start | bytes 1732
  (82 other events, 2904.6 us)
Sparse Core Ops, SparseCore 0:
  10.8 67.8 all-gather.10
  81.5 39.5 all-gather.14
  123.8 78.6 all-gather.18
  205.1 78.0 all-gather.22
  284.6 89.1 all-gather.12
  375.2 37.4 all-gather.16
  414.3 120.0 all-gather.20
  535.9 120.0 all-gather.24
  773.3 20.8 reduce-scatter.39
  797.1 20.8 reduce-scatter.35
  820.5 47.8 reduce-scatter.21
  871.0 109.4 reduce-scatter.33
  983.3 139.4 reduce-scatter.25
  1125.2 139.4 reduce-scatter.29
  1268.2 57.6 reduce-scatter.41
  1329.3 56.6 reduce-scatter.37
  1389.6 63.0 reduce-scatter.23
  1456.6 168.6 all-reduce.2
  1629.4 94.2 reduce-scatter.27
  1727.6 95.0 reduce-scatter.31
where the time goes:
time: 1900 us; the launch traced here: 1890 us
  waiting for transfers between devices  1420 us (75%)
  matrix products  203 us (11%)
  blocking collectives  94.9 us (5%)
  other arithmetic  91.2 us (5%)
  local copies, waits for them, and re-layouts  62.6 us (3%)
  between operations  22 us (1%)
    unnamed x26, waiting for transfers between devices  392 us
    reduce_scatter x1, waiting for transfers between devices, reduce_grads(): lax.psum_scatter(grad_down.astype(jnp.bfloat16), 'dp', scatter_dimension=...  142 us
    reduce_scatter x1, waiting for transfers between devices, reduce_grads(): lax.psum_scatter(grad_up.astype(jnp.bfloat16), 'dp', scatter_dimension=0,...  127 us
    all_gather x1, waiting for transfers between devices, gather_params(): lax.all_gather(inner_part[3], 'dp', axis=0, tiled=True)  110 us
    reduce_scatter x1, waiting for transfers between devices, reduce_grads(): lax.psum_scatter(outer_part[3].astype(jnp.bfloat16), 'fsdp', scatter_dime...  96.4 us
    reduce_scatter x1, waiting for transfers between devices, reduce_grads(): lax.psum_scatter(outer_part[2].astype(jnp.bfloat16), 'fsdp', scatter_dime...  95 us
    all_gather x1, waiting for transfers between devices, gather_params(): lax.all_gather(inner_part[2], 'dp', axis=0, tiled=True)  82.9 us
    all_gather x1, waiting for transfers between devices, gather_params(): lax.all_gather(part_up, 'fsdp', axis=0, tiled=True)  81.4 us
  transfers between devices with their start and end apart: 20, of which 17 were waited for; matrix products, arithmetic and copies ran while one was open for 11% of the time, Pallas kernels for 0%

commit v1 on v0

--- a/solution.py
+++ b/solution.py
@@ -1,6 +1,10 @@
+import functools
+
 import jax
 import jax.numpy as jnp
 from jax import lax
+from jax.experimental import pallas as pl
+from jax.experimental.pallas import tpu as pltpu
 from jax.sharding import PartitionSpec as P
 
 HEADS = 16
@@ -15,6 +19,283 @@
 adam_eps = 1e-08
 decay_rate = 0.1
 
+MESH=pl.DeviceIdType.MESH
+ANY=pl.ANY
+
+class Place:
+    def __init__(self, n_z):
+        dp = lax.axis_index("dp"); fs = lax.axis_index("fsdp")
+        self.n_z = n_z
+        self.at = {"x": dp // 2, "c": dp % 2, "z": fs // 2, "y": fs % 2}
+    def dev(self, **new):
+        p = {**self.at, **new}
+        return (p["x"] * 2 + p["c"], p["z"] * 2 + p["y"])
+    def other(self, ax):
+        return self.dev(**{ax: 1 - self.at[ax]})
+    def along_z(self, k):
+        return self.dev(z=(self.at["z"] + k) % self.n_z)
+    def partners(self):
+        return [self.other(a) for a in "cxy"] + [self.along_z(k) for k in range(1, self.n_z)]
+
+def greet(place):
+    bar = pltpu.get_barrier_semaphore()
+    others = place.partners()
+    for d in others:
+        pl.semaphore_signal(bar, inc=1, device_id=d, device_id_type=MESH)
+    pl.semaphore_wait(bar, len(others))
+
+def block_index(place, held):
+    return tuple(slice(None) if ax in held else place.at[ax] for ax in "xczy")
+
+class Gather:
+    def __init__(self, place, src, dst, rows, cols, order, sems, base):
+        self.place, self.src, self.dst = place, src, dst
+        self.sl = (pl.ds(*rows), pl.ds(*cols))
+        self.order, self.sems, self.base = order, sems, base
+        self.copies = {}
+    def region(self, held):
+        return self.dst.at[block_index(self.place, held) + self.sl]
+    def start(self, step):
+        p = self.place; ax = self.order[step]; held = self.order[:step]
+        ss, rs = self.sems
+        made = []
+        n = self.base
+        for s in range(step):
+            n += p.n_z - 1 if self.order[s] == "z" else 1
+        src = self.src.at[self.sl] if step == 0 else self.region(held)
+        dst = self.region(held)
+        for k in (range(1, p.n_z) if ax == "z" else (0,)):
+            to = p.along_z(k) if ax == "z" else p.other(ax)
+            d = pltpu.make_async_remote_copy(src_ref=src, dst_ref=dst, send_sem=ss.at[n], recv_sem=rs.at[n], device_id=to, device_id_type=MESH)
+            d.start(); made.append(d); n += 1
+        self.copies[step] = made
+    def arrive(self, step):
+        for d in self.copies[step]: d.wait_recv()
+    def finish(self):
+        for made in self.copies.values():
+            for d in made: d.wait_send()
+
+def n_sems(n_z): return n_z + 2
+
+def gather_kernel(n_z, plan, n_w, *refs):
+    ins, outs, (ss, rs, ls) = refs[:n_w], refs[n_w:2*n_w], refs[2*n_w:]
+    place = Place(n_z)
+    greet(place)
+    locals_ = []
+    for i in range(n_w):
+        d = pltpu.make_async_copy(ins[i], outs[i].at[block_index(place, ())], ls.at[i])
+        d.start(); locals_.append(d)
+    stages = [[Gather(place, ins[w], outs[w], rows, cols, order, (ss, rs), j * n_sems(n_z)) for (j, w, rows, cols, order) in stage] for stage in plan]
+    waited = set()
+    T, steps = len(stages), 4
+    for t in range(T + steps):
+        for back in range(steps + 1):
+            u = t - back
+            if not 0 <= u < T: continue
+            for g, (j, w, *_) in zip(stages[u], plan[u]):
+                if back == 1 and w not in waited:
+                    locals_[w].wait(); waited.add(w)
+                if back > 0: g.arrive(back - 1)
+                if back < steps: g.start(back)
+    for st in stages:
+        for g in st: g.finish()
+
+def number(plan):
+    j, out = 0, []
+    for stage in plan:
+        new = []
+        for piece in stage:
+            new.append((j,) + piece); j += 1
+        out.append(new)
+    return out, j
+
+def gather_all(shards, plan, n_z):
+    plan, count = number(plan)
+    n_w = len(shards)
+    return pl.pallas_call(
+        functools.partial(gather_kernel, n_z, plan, n_w),
+        out_shape=[jax.ShapeDtypeStruct((2, 2, n_z, 2) + s.shape, s.dtype) for s in shards],
+        in_specs=[pl.BlockSpec(memory_space=pltpu.VMEM)] * n_w,
+        out_specs=[pl.BlockSpec(memory_space=ANY)] * n_w,
+        scratch_shapes=[pltpu.SemaphoreType.DMA((count * n_sems(n_z),)), pltpu.SemaphoreType.DMA((count * n_sems(n_z),)), pltpu.SemaphoreType.DMA((n_w,))],
+        name="gather_weights",
+        compiler_params=pltpu.CompilerParams(collective_id=0, has_side_effects=True),
+    )(*shards)
+
+ZYX, ZXY = ("z", "y", "x", "c"), ("z", "x", "y", "c")
+
+SLOTS = 3
+
+class Scatter:
+    def __init__(self, place, src, out, rows, cols, order, piece, part, turn, sems, bufs):
+        self.p, self.src, self.out = place, src, out
+        self.rows, self.cols = pl.ds(*rows), pl.ds(*cols)
+        self.shape = (rows[1], cols[1])
+        self.order, self.piece = order, piece
+        self.ss, self.rs, self.ls = sems
+        self.part, self.slot, self.b = part, (turn % SLOTS) * 2 + part, bufs
+        self.sent = {}
+    def v(self, ref, *lead):
+        return ref.at[lead + (pl.ds(0, self.shape[0]), pl.ds(0, self.shape[1]))]
+    def send(self, src, dst, to, n):
+        n += self.piece * n_sems(self.p.n_z)
+        d = pltpu.make_async_remote_copy(src_ref=src, dst_ref=dst, send_sem=self.ss.at[n], recv_sem=self.rs.at[n], device_id=to, device_id_type=MESH)
+        d.start()
+        return d
+    def copy(self, src, dst, k):
+        d = pltpu.make_async_copy(src, dst, self.ls.at[self.slot, k])
+        d.start()
+        return d
+    def add(self, count, dst, a, b):
+        r, w = self.shape
+        def one(i, carry):
+            (da, di), (aa, ai), (ba, bi) = dst(i), a(i), b(i)
+            da[di + (slice(0, r), slice(0, w))] = aa[ai + (slice(0, r), slice(0, w))] + ba[bi + (slice(0, r), slice(0, w))]
+            return carry
+        lax.fori_loop(0, count, one, 0)
+    def free(self, step):
+        if step in self.sent:
+            for d in self.sent.pop(step): d.wait_send() if step < 4 else d.wait()
+    def step0(self):
+        p = self.p; c = p.at["c"]; A = slice(None)
+        self.sent[0] = [self.send(self.src.at[:, 1 - c, :, :, self.rows, self.cols], self.v(self.b["r0"], self.piece, A, A, A), p.other("c"), 0)]
+        self.mine = self.copy(self.src.at[:, c, :, :, self.rows, self.cols], self.v(self.b["s0"], self.slot, A, A, A), 0)
+        self.came = self.sent[0]
+    def step1(self):
+        p = self.p; A = slice(None); nz = p.n_z; b = self.b; sl, pt = self.slot, self.part
+        for d in self.came: d.wait_recv()
+        got = self.copy(self.v(b["r0"], self.piece, A, A, A), self.v(b["t0"], pt, A, A, A), 1)
+        self.mine.wait(); got.wait()
+        at = lambda i: (i // (nz * 2), (i // 2) % nz, i % 2)
+        self.add(4 * nz, lambda i: (b["s0"], (sl,) + at(i)), lambda i: (b["s0"], (sl,) + at(i)), lambda i: (b["t0"], (pt,) + at(i)))
+        ax = self.order[0]; o = 1 - p.at[ax]
+        src = self.v(b["s0"], sl, o, A, A) if ax == "x" else self.v(b["s0"], sl, A, A, o)
+        dst = self.v(b["r1"], self.piece, A, A)
+        if ax == "x":
+            dst = self.v(b["r1y"], self.piece, A, A)
+        self.sent[1] = self.came = [self.send(src, dst, p.other(ax), 1)]
+    def step2(self):
+        p = self.p; A = slice(None); nz = p.n_z; b = self.b; sl, pt = self.slot, self.part
+        for d in self.came: d.wait_recv()
+        ax = self.order[0]; m = p.at[ax]; o = 1 - p.at[self.order[1]]
+        if ax == "x":
+            got = self.copy(self.v(b["r1y"], self.piece, A, A), self.v(b["t1y"], A, A), 1); got.wait()
+            at = lambda i: (i // 2, i % 2)
+            self.add(2 * nz, lambda i: (b["s1y"], (sl // 2,) + at(i)), lambda i: (b["s0"], (sl, m) + at(i)), lambda i: (b["t1y"], at(i)))
+            src = self.v(b["s1y"], sl // 2, A, o)
+        else:
+            got = self.copy(self.v(b["r1"], self.piece, A, A), self.v(b["t1"], A, A), 1); got.wait()
+            at = lambda i: (i // nz, i % nz)
+            self.add(2 * nz, lambda i: (b["s1"], (sl // 2,) + at(i)), lambda i: (b["s0"], (sl,) + at(i) + (m,)), lambda i: (b["t1"], at(i)))
+            src = self.v(b["s1"], sl // 2, o, A)
+        self.sent[2] = self.came = [self.send(src, self.v(b["r2"], self.piece, A), p.other(self.order[1]), 2)]
+    def step3(self):
+        p = self.p; A = slice(None); nz = p.n_z; b = self.b; sl, pt = self.slot, self.part
+        for d in self.came: d.wait_recv()
+        got = self.copy(self.v(b["r2"], self.piece, A), self.v(b["t2"], pt, A), 1); got.wait()
+        m = p.at[self.order[1]]
+        mine = (lambda i: (b["s1y"], (sl // 2, i, m))) if self.order[0] == "x" else (lambda i: (b["s1"], (sl // 2, m, i)))
+        self.add(nz, lambda i: (b["s2"], (sl, i)), mine, lambda i: (b["t2"], (pt, i)))
+        self.sent[3] = self.came = [
+            self.send(self.v(b["s2"], sl, (p.at["z"] + k) % nz), self.v(b["r3"], self.piece, k - 1), p.along_z(k), 2 + k)
+            for k in range(1, nz)]
+    def step4(self):
+        p = self.p; A = slice(None); nz = p.n_z; b = self.b; sl, pt = self.slot, self.part
+        r, w = self.shape
+        for d in self.came: d.wait_recv()
+        got = self.copy(self.v(b["r3"], self.piece, A), self.v(b["t3"], pt, A), 1); got.wait()
+        total = b["s2"][sl, p.at["z"], 0:r, 0:w].astype(jnp.float32)
+        for k in range(nz - 1):
+            total = total + b["t3"][pt, k, 0:r, 0:w].astype(jnp.float32)
+        b["o"][sl, 0:r, 0:w] = total
+        b["sq"][0:r, 0:w] += total * total
+        self.sent[4] = [self.copy(self.v(b["o"], sl), self.out.at[self.rows, self.cols], 2)]
+
+def scatter_kernel(n_z, plan, n_w, names, *refs):
+    ins, outs = refs[:n_w], refs[n_w:2 * n_w]
+    norm_out = refs[2 * n_w]
+    rest = refs[2 * n_w + 1:]
+    bufs = dict(zip(names, rest))
+    ss, rs, ls, ns, nr = rest[len(names):]
+    place = Place(n_z)
+    greet(place)
+    bufs["sq"][...] = jnp.zeros_like(bufs["sq"])
+    stages = [[Scatter(place, ins[w], outs[w], rows, cols, order, j, part, t, (ss, rs, ls), bufs) for part, (j, w, rows, cols, order) in enumerate(stage)] for t, stage in enumerate(plan)]
+    T = len(stages)
+    for t in range(T + 4):
+        for back in range(5):
+            u = t - back
+            if not 0 <= u < T: continue
+            if u >= SLOTS:
+                for g in stages[u - SLOTS]:
+                    if back == 0: g.free(1)
+                    else: g.free(back)
+            for g in stages[u]: getattr(g, f"step{back}")()
+    for st in stages:
+        for g in st:
+            for k in range(5): g.free(k)
+    sq = bufs["sq"]
+    part = bufs["n"]
+    acc = jnp.zeros((8, 128), jnp.float32)
+    for i in range(sq.shape[0] // 8):
+        for j in range(sq.shape[1] // 128):
+            acc = acc + sq[i * 8:(i + 1) * 8, j * 128:(j + 1) * 128]
+    for q, ax in enumerate("cxy"):
+        part[2 * q] = acc
+        d = pltpu.make_async_remote_copy(src_ref=part.at[2 * q], dst_ref=part.at[2 * q + 1], send_sem=ns.at[q], recv_sem=nr.at[q], device_id=place.other(ax), device_id_type=MESH)
+        d.start(); d.wait()
+        acc = part[2 * q] + part[2 * q + 1]
+    zs = bufs["nz"]
+    z = place.at["z"]
+    zs[z] = acc
+    ds_ = []
+    for k in range(1, n_z):
+        d = pltpu.make_async_remote_copy(src_ref=zs.at[z], dst_ref=zs.at[z], send_sem=ns.at[2 + k], recv_sem=nr.at[2 + k], device_id=place.along_z(k), device_id_type=MESH)
+        d.start(); ds_.append(d)
+    for d in ds_: d.wait()
+    total = zs[0]
+    for k in range(1, n_z): total = total + zs[k]
+    norm_out[...] = total
+
+def scatter_all(grads, plan, n_z):
+    plan, count = number(plan)
+    n_w = len(grads)
+    R = max(p[2][1] for st in plan for p in st); W = max(p[3][1] for st in plan for p in st)
+    bf = jnp.bfloat16
+    hbm = {"r0": (count, 2, n_z, 2, R, W), "r1": (count, 2, n_z, R, W), "r1y": (count, n_z, 2, R, W), "r2": (count, n_z, R, W), "r3": (count, n_z - 1, R, W)}
+    vm = {"s0": ((2 * SLOTS, 2, n_z, 2, R, W), bf), "t0": ((2, 2, n_z, 2, R, W), bf), "s1": ((SLOTS, 2, n_z, R, W), bf), "s1y": ((SLOTS, n_z, 2, R, W), bf),
+          "t1": ((2, n_z, R, W), bf), "t1y": ((n_z, 2, R, W), bf), "s2": ((2 * SLOTS, n_z, R, W), bf), "t2": ((2, n_z, R, W), bf), "t3": ((2, n_z - 1, R, W), bf),
+          "o": ((2 * SLOTS, R, W), jnp.float32), "sq": ((R, W), jnp.float32), "n": ((6, 8, 128), jnp.float32), "nz": ((n_z, 8, 128), jnp.float32)}
+    names = list(hbm) + list(vm)
+    outs = pl.pallas_call(
+        functools.partial(scatter_kernel, n_z, plan, n_w, names),
+        out_shape=[jax.ShapeDtypeStruct(g.shape[4:], jnp.float32) for g in grads] + [jax.ShapeDtypeStruct((8, 128), jnp.float32)] + [jax.ShapeDtypeStruct(s, bf) for s in hbm.values()],
+        in_specs=[pl.BlockSpec(memory_space=ANY)] * n_w,
+        out_specs=[pl.BlockSpec(memory_space=ANY)] * n_w + [pl.BlockSpec(memory_space=pltpu.VMEM)] + [pl.BlockSpec(memory_space=ANY)] * len(hbm),
+        scratch_shapes=[pltpu.VMEM(s, d) for s, d in vm.values()] + [pltpu.SemaphoreType.DMA((count * n_sems(n_z),)), pltpu.SemaphoreType.DMA((count * n_sems(n_z),)), pltpu.SemaphoreType.DMA((2 * SLOTS, 3)), pltpu.SemaphoreType.DMA((n_z + 2,)), pltpu.SemaphoreType.DMA((n_z + 2,))],
+        name="scatter_grads",
+        compiler_params=pltpu.CompilerParams(collective_id=1, has_side_effects=True, vmem_limit_bytes=48 * 2**20),
+    )(*grads)
+    return outs[:n_w], outs[n_w]
+
+def weight_plan(shapes, width, tiny):
+    out = []
+    for w, rows, cols in shapes:
+        for r in range(0, rows, 48):
+            for k in range(0, cols, 2 * width):
+                out.append([(w, (r, 48), (k, width), 0), (w, (r, 48), (k + width, width), 1)])
+    return out
+
+
+def plan_with(orders, weights, width, tiny_first):
+    stages = [[(w, r, c, orders[o]) for (w, r, c, o) in st] for st in weight_plan(weights, width, None)]
+    tiny = [(4, (0, 16), (0, 128), orders[0])]
+    return [tiny] + stages if tiny_first else stages + [tiny]
+
+
+def fits_kernels(n_dp, n_fsdp, shards):
+    return n_dp == 4 and n_fsdp % 2 == 0 and all(s.shape[0] % 48 == 0 and s.shape[1] % 1536 == 0 for s in shards)
+
 
 def layer_norm(values_in, gain):
     mean_row = jnp.mean(values_in, axis=-1, keepdims=True)
@@ -29,7 +310,8 @@
 
 def frame_tables(counts, frame_slots, time_len):
     slot_total = counts.shape[0]
-    slot_ends = jnp.cumsum(counts)
+    order = jnp.arange(slot_total, dtype=jnp.int32)
+    slot_ends = jnp.sum(jnp.where(order[None, :] <= order[:, None], counts[None, :], 0), axis=1)
     slot_starts = slot_ends - counts
     frame_ids = jnp.arange(frame_slots, dtype=jnp.int32)
     frame_owner = jnp.sum((frame_ids[:, None] >= slot_ends[None, :]).astype(jnp.int32), axis=1)
@@ -158,9 +440,25 @@
     low_down = w_down.astype(jnp.bfloat16)
     low_time = time_table.astype(jnp.bfloat16)
     low_gains = gains.astype(jnp.bfloat16)
-    full_qkv, full_out, full_up, full_down, full_time, full_gains = gather_params(
-        low_qkv, low_out, low_up, low_down, low_time, low_gains
-    )
+    n_dp, n_fsdp = lax.axis_size("dp"), lax.axis_size("fsdp")
+    own_rows, model = w_qkv.shape[0], w_qkv.shape[2]
+    shards = [low_qkv.reshape(own_rows, -1), low_out, low_up, low_down]
+    kernels = fits_kernels(n_dp, n_fsdp, shards)
+    if kernels:
+        n_z = n_fsdp // 2
+        listed = [(w, shards[w].shape[0], shards[w].shape[1]) for w in range(4)]
+        time_len = low_time.shape[1]
+        tiny = jnp.concatenate([low_time.T, low_gains.T], axis=0)
+        tiny = jnp.pad(tiny, ((0, 16 - tiny.shape[0]), (0, 128 - own_rows)))
+        full = gather_all(shards + [tiny], plan_with((ZYX, ZXY), listed, 768, True), n_z)
+        full_qkv, full_out, full_up, full_down = (f.reshape(-1, f.shape[-1]) for f in full[:4])
+        full_qkv = full_qkv.reshape(model, 3, model)
+        tiny_all = full[4].reshape(n_dp * n_fsdp, 16, 128)[:, :, :own_rows].transpose(1, 0, 2).reshape(16, model)
+        full_time, full_gains = tiny_all[:time_len].T, tiny_all[time_len : time_len + 3].T
+    else:
+        full_qkv, full_out, full_up, full_down, full_time, full_gains = gather_params(
+            low_qkv, low_out, low_up, low_down, low_time, low_gains
+        )
     item_slots, lat_count, model_width = latents.shape
     frame_slots, patch_rows, unused_width = media.shape
     queries_n = item_slots * lat_count
@@ -207,21 +505,18 @@
     act_low = activated.astype(jnp.bfloat16)
     result = middle + jnp.dot(act_low, full_down, preferred_element_type=jnp.float32)
     new_latents = result.astype(jnp.bfloat16).reshape(item_slots, lat_count, model_width)
-    back_qkv, back_out, back_up, back_down, back_time, back_gains = gather_params(
-        low_qkv, low_out, low_up, low_down, low_time, low_gains
-    )
     d_result = cotangent.reshape(queries_n, model_width)
     g_down = jnp.einsum("qf,qd->fd", act_low, d_result, preferred_element_type=jnp.float32)
-    d_act = jnp.einsum("qd,fd->qf", d_result, back_down, preferred_element_type=jnp.float32)
+    d_act = jnp.einsum("qd,fd->qf", d_result, full_down, preferred_element_type=jnp.float32)
     d_pre = gelu_back(d_act)[0].astype(jnp.bfloat16)
     g_up = jnp.einsum("qd,qf->df", hidden_low, d_pre, preferred_element_type=jnp.float32)
-    d_hidden = jnp.einsum("qf,df->qd", d_pre, back_up, preferred_element_type=jnp.float32)
+    d_hidden = jnp.einsum("qf,df->qd", d_pre, full_up, preferred_element_type=jnp.float32)
     d_middle_ln, g_gain_ffn = ffn_back(d_hidden)
     d_middle = d_result.astype(jnp.float32) + d_middle_ln
     d_branch = d_middle.astype(jnp.bfloat16)
     g_out = jnp.einsum("qe,qd->ed", attended, d_branch, preferred_element_type=jnp.float32)
     d_attended = jnp.einsum(
-        "qd,ed->qe", d_branch, back_out, preferred_element_type=jnp.float32
+        "qd,ed->qe", d_branch, full_out, preferred_element_type=jnp.float32
     ).astype(jnp.bfloat16)
     scores_again = masked_scores(q_heads, k_heads, allowed, score_scale)
     probs = jnp.exp(scores_again - log_total)
@@ -255,7 +550,7 @@
     d_key_value = jnp.concatenate([d_keys, d_values], axis=1)
     g_key_value = jnp.einsum("kd,kx->dx", keys_in, d_key_value, preferred_element_type=jnp.float32)
     g_qkv = jnp.concatenate([g_query, g_key_value], axis=1).reshape(model_width, 3, model_width)
-    back_flat = back_qkv.reshape(model_width, 3 * model_width)
+    back_flat = full_qkv.reshape(model_width, 3 * model_width)
     d_keys_in = jnp.einsum(
         "kx,dx->kd", d_key_value, back_flat[:, model_width:], preferred_element_type=jnp.float32
     )
@@ -273,11 +568,24 @@
     frame_grad = jnp.sum(d_mixed, axis=1)
     g_time = jnp.einsum("fd,ft->dt", frame_grad, time_hot, precision=highest)
     g_gains = jnp.stack([g_gain_media, g_gain_lat, g_gain_ffn], axis=1)
-    reduced = reduce_grads(g_qkv, g_out, g_up, g_down, g_time, g_gains)
-    local_sq = jnp.zeros((), jnp.float32)
-    for grad in reduced:
-        local_sq = local_sq + jnp.sum(grad * grad)
-    grad_norm = jnp.sqrt(lax.psum(local_sq, ("dp", "fsdp")))
+    if kernels:
+        def blocks(g, rows):
+            return g.astype(jnp.bfloat16).reshape(2, 2, n_z, 2, rows, -1)
+
+        tiny_g = jnp.concatenate([g_time, g_gains], axis=1).T.reshape(time_len + 3, -1, own_rows).transpose(1, 0, 2)
+        tiny_g = jnp.pad(tiny_g, ((0, 0), (0, 16 - tiny_g.shape[1]), (0, 128 - own_rows)))
+        grads = [blocks(g, s.shape[0]) for g, s in zip((g_qkv, g_out, g_up, g_down), shards)] + [blocks(tiny_g, 16)]
+        orders = (("x", "y", "z"), ("y", "x", "z"))
+        own, squares = scatter_all(grads, plan_with(orders, listed[::-1], 768, False), n_z)
+        own_tiny = own[4][: time_len + 3, :own_rows].T
+        reduced = (own[0].reshape(w_qkv.shape), own[1], own[2], own[3], own_tiny[:, :time_len], own_tiny[:, time_len:])
+        grad_norm = jnp.sqrt(jnp.sum(squares))
+    else:
+        reduced = reduce_grads(g_qkv, g_out, g_up, g_down, g_time, g_gains)
+        local_sq = jnp.zeros((), jnp.float32)
+        for grad in reduced:
+            local_sq = local_sq + jnp.sum(grad * grad)
+        grad_norm = jnp.sqrt(lax.psum(local_sq, ("dp", "fsdp")))
     factor = jnp.minimum(1.0, clip_limit / (grad_norm + 1e-06))
     masters = (w_qkv, w_out, w_up, w_down, time_table, gains)
     firsts = (m_qkv, m_out, m_up, m_down, m_time, m_gains)

time: 1900 us -> 885 us (0.47)
  waiting for transfers between devices: 1420 us -> 0 us
  Pallas kernels: 0 us -> 544 us
  blocking collectives: 94.9 us -> 0 us
  local copies, waits for them, and re-layouts: 62.6 us -> 37.9 us
    pallas_call x0 -> x2, Pallas kernels: none -> 544 us  [the longest x1 276 us: scatter_all(): pl.pallas_call(functools.partial(scatter_kernel, n_z, plan, n_w, names),...]
    reduce_scatter x6 -> x0, waiting for transfers between devices: 542 us -> none  [the longest x1 142 us: reduce_grads(): lax.psum_scatter(grad_down.astype(jnp.bfloat16), 'dp', scatter_dimension=...]
    all_gather x8 -> x0, waiting for transfers between devices: 482 us -> none  [the longest x1 110 us: gather_params(): lax.all_gather(inner_part[3], 'dp', axis=0, tiled=True)]
    unnamed x26 -> x0, waiting for transfers between devices: 392 us -> none
    all_gather x4 -> x0, blocking collectives: 54.4 us -> none  [the longest x1 26 us: gather_params(): lax.all_gather(part_time, 'fsdp', axis=0, tiled=True)]
    psum x1 -> x0, blocking collectives: 40.5 us -> none  [on_device(): grad_norm = jnp.sqrt(lax.psum(local_sq, ('dp', 'fsdp')))]
  transfers between devices with their start and end apart: 20 -> 0, of which waited for: 17 -> 0; matrix products, arithmetic and copies ran while one was open for 11% -> 0% of each run, Pallas kernels for 0% -> 0%
where the time goes in v1:
time: 885 us; the launch traced here: 874 us
  Pallas kernels  544 us (61%)
  matrix products  212 us (24%)
  other arithmetic  76.7 us (9%)
  local copies, waits for them, and re-layouts  37.9 us (4%)
    pallas_call x1, Pallas kernels, scatter_all(): pl.pallas_call(functools.partial(scatter_kernel, n_z, plan, n_w, names),...  276 us
    pallas_call x1, Pallas kernels, gather_all(): pl.pallas_call(functools.partial(gather_kernel, n_z, plan, n_w), out_shap...  268 us
    dot_general x1, matrix products, on_device(): pre_act = jnp.dot(hidden_low, full_up, preferred_element_type=jnp.float32)  22.7 us
    dot_general x1, matrix products, on_device(): jnp.einsum('qd,fd->qf', d_result, full_down, preferred_element_type=jnp.f...  21.6 us

profile of v1, /device:TPU:0, one launch (start us, length us, event | category | flops | bytes accessed | tf_op | source)
XLA Modules:
  0.0 874.4 jit_solution(13320018407976376914)
XLA Ops:
  18.6 267.8 %gather_weights.1 = (bf16[2,2,4,2,48,4608]{5,4,3,2,1,0:T(8,128)(2,1)}, bf16[2,2,4,2,48,1536]{5,4,3,2,1,0:T(8,128)(2,1)}, bf16[2,2,4,2,48,6144]{5,4,3,2,1,0:T(8,1...) custom-call(bf16[48,4608]{1,0:T(8,128)(2,1)} %bitcast.151, ...), custom_call_target="tpu_custom_call" | custom-call | tf_op jit(solution)/shard_map/gather_weights/pallas_call | solution.py:115
  294.0 4.6 fusion.22
  303.0 14.3 %convolution_convert_fusion.3 = bf16[1120,3072]{1,0:T(8,128)(2,1)S(1)} fusion(bf16[1536,4608]{1,0:T(8,128)(2,1)} %bitcast.163, bf16[256,1536]{1,0:T(8,128)(2,1)S(1)} %copy-done.31, bf16[864,1536]{1,0:T(8,128)(2,1)S(1)} %bitcast.149), kind=kOutput, calls=%fused_computation.11 | convolution fusion | flops 10579968000 | bytes 19759104 | tf_op jit(solution)/shard_map/dot_general | solution.py:484
  325.0 5.7 copy.92
  330.8 10.7 %fusion.72 = (f32[16,256]{1,0:T(8,128)S(1)}, f32[16,256,1120]{1,2,0:T(8,128)}) fusion(bf16[256,16,96]{0,2,1:T(8,128)(2,1)} %bitcast.141, bf16[1120,16,96]{0,2,1:T(8,128)(2,1)S(1)} %bitcast.119, pred[256,1120]{0,1:T(8,128)(4,1)} %broadcast_compare_fusion), kind=kOutput, calls=%fused_computation.171 | convolution fusion | flops 894562304 | bytes 22880256 | tf_op jit(solution)/shard_map/qhe,khe->hqk/dot_general | solution.py:395
  342.0 9.2 %exponential_reduce_fusion = f32[16,256]{1,0:T(8,128)} fusion(f32[16,256,1120]{1,2,0:T(8,128)} %get-tuple-element.121, f32[16,256]{1,0:T(8,128)S(1)} %get-tuple-element.120), kind=kLoop, calls=%fused_computation.7 | loop fusion | flops 9170944 | bytes 18382848 | tf_op jit(solution)/shard_map/reduce_sum | solution.py:495
  352.0 10.4 %fusion.29 = bf16[16,96,256]{2,1,0:T(8,128)(2,1)S(1)} fusion(bf16[1120,16,96]{0,2,1:T(8,128)(2,1)} %bitcast.122, f32[16,256,1120]{1,2,0:T(8,128)} %get-tuple-element.121, f32[16,256]{1,0:T(8,128)S(1)} %log_add_fusion), kind=kOutput, calls=%fused_computation.80 | convolution fusion | flops 890372096 | bytes 22593536 | tf_op jit(solution)/shard_map/hqk,khe->qhe/dot_general | solution.py:498
  366.9 22.7 %multiply_convert_fusion.2 = (bf16[256,6144]{1,0:T(8,128)(2,1)}, f32[256,6144]{1,0:T(8,128)S(1)}, f32[256,6144]{1,0:T(8,128)}) fusion(bf16[1536,6144]{1,0:T(8,128)(2,1)} %bitcast.158, f32[256,1536]{1,0:T(8,128)S(1)} %get-tuple-element.123, f32[1536]{0:T(1024)S(1)} %copy-done.36, f32[256]{0:T(256)S(1)} %fusion.55, f32[256]{0:T(256)S(1)} %broadcast_multiply_fusion.3), kind=kOutput, calls=%fused_computation.24 | convolution fusion | flops 4935647232 | bytes 36184064 | tf_op jit(solution)/shard_map/dot_general | solution.py:503
  389.6 21.6 %add_convert_fusion = bf16[256,6144]{1,0:T(8,128)(2,1)} fusion(f32[256,6144]{1,0:T(8,128)S(1)} %get-tuple-element.115, bf16[6144,1536]{1,0:T(8,128)(2,1)} %bitcast.160, bf16[256,1536]{1,0:T(8,128)(2,1)S(1)} %bitcast.137, f32[256,6144]{1,0:T(8,128)} %get-tuple-element.124), kind=kOutput, calls=%fused_computation.23 | convolution fusion | flops 4853858304 | bytes 35389440 | tf_op jit(solution)/shard_map/qd,fd->qf/dot_general | solution.py:510
  411.2 10.8 %fusion.21 = bf16[256,1536]{1,0:T(8,128)(2,1)} fusion(f32[256,1536]{1,0:T(8,128)S(1)} %get-tuple-element.123, bf16[256,6144]{1,0:T(8,128)(2,1)} %get-tuple-element.114, bf16[6144,1536]{1,0:T(8,128)(2,1)} %bitcast.161), kind=kOutput, calls=%fused_computation.56 | convolution fusion | flops 4832624640 | bytes 24379392 | tf_op jit(solution)/shard_map/dot_general | solution.py:506
  421.9 11.2 %multiply_reduce_fusion.4 = (bf16[1536]{0:T(1024)(128)(2,1)S(1)}, f32[256]{0:T(256)S(1)}, f32[256,1536]{1,0:T(8,128)}) fusion(f32[256,1536]{1,0:T(8,128)S(1)} %get-tuple-element.123, f32[256]{0:T(256)S(1)} %fusion.55, f32[256]{0:T(256)S(1)} %broadcast_multiply_fusion.3, f32[1536]{0:T(1024)S(1)} %copy-done.36, bf16[256,6144]{1,0:T(8,128)(2,1)} %add_convert_fusion, ...), kind=kOutput, calls=%fused_computation.67 | convolution fusion | flops 4834588672 | bytes 25178112 | tf_op jit(solution)/shard_map/qf,df->qd/dot_general | solution.py:513
  443.2 5.0 convolution_convert_fusion.5
  448.1 11.0 %convolution_convert_fusion.6 = bf16[16,96,1120]{2,1,0:T(8,128)(2,1)} fusion(bf16[256,16,96]{0,2,1:T(8,128)(2,1)S(1)} %bitcast.139, f32[16,256,1120]{1,2,0:T(8,128)} %get-tuple-element.121, f32[16,256]{1,0:T(8,128)S(1)} %log_add_fusion), kind=kOutput, calls=%fused_computation.47 | convolution fusion | flops 891699200 | bytes 22593536 | tf_op jit(solution)/shard_map/hqk,qhe->khe/dot_general | solution.py:545
  459.2 13.3 %multiply_reduce_fusion = (f32[16,256]{1,0:T(8,128)S(1)}, f32[16,256,1120]{1,2,0:T(8,128)}) fusion(f32[16,256,1120]{1,2,0:T(8,128)} %get-tuple-element.121, f32[16,256]{1,0:T(8,128)S(1)} %log_add_fusion, bf16[256,16,96]{0,2,1:T(8,128)(2,1)S(1)} %bitcast.140, bf16[1120,16,96]{0,2,1:T(8,128)(2,1)} %bitcast.123), kind=kOutput, calls=%fused_computation.5 | convolution fusion | flops 894562304 | bytes 40960000 | tf_op jit(solution)/shard_map/qhe,khe->hqk/dot_general | solution.py:525
  472.5 13.1 %multiply_convert_fusion = bf16[16,256,1120]{1,2,0:T(8,128)(2,1)S(1)} fusion(f32[16,256,1120]{1,2,0:T(8,128)} %get-tuple-element.127, f32[16,256,1120]{1,2,0:T(8,128)} %get-tuple-element.121, f32[16,256]{1,0:T(8,128)S(1)} %get-tuple-element.126, f32[16,256]{1,0:T(8,128)S(1)} %log_add_fusion), kind=kLoop, calls=%fused_computation.4 | loop fusion | flops 18350080 | bytes 45907968 | tf_op jit(solution)/shard_map/convert_element_type | solution.py:527
  487.3 4.5 multiply_convert_fusion.1
  495.4 6.8 copy.97
  502.1 17.5 %convolution_convert_fusion.2 = bf16[1536,3072]{1,0:T(8,128)(2,1)} fusion(bf16[1120,1536]{0,1:T(8,128)(2,1)S(1)} %bitcast.143, bf16[1120,1536]{0,1:T(8,128)(2,1)} %bitcast.145, bf16[256,1536]{1,0:T(8,128)(2,1)} %copy-done.30, bf16[864,1536]{1,0:T(8,128)(2,1)} %bitcast.150), kind=kOutput, calls=%fused_computation.10 | convolution fusion | flops 10595008512 | bytes 19759104 | tf_op jit(solution)/shard_map/kd,kx->dx/dot_general | solution.py:551
  519.7 16.8 %fusion.2 = f32[1120,1536]{1,0:T(8,128)} fusion(bf16[1536,4608]{1,0:T(8,128)(2,1)} %bitcast.164, bf16[1120,1536]{0,1:T(8,128)(2,1)S(1)} %bitcast.144, bf16[1120,1536]{0,1:T(8,128)(2,1)} %bitcast.146), kind=kOutput, calls=%fused_computation.13 | convolution fusion | flops 10583408640 | bytes 23298048 | tf_op jit(solution)/shard_map/kx,dx->kd/dot_general | solution.py:554
  536.6 4.7 multiply_reduce_fusion.6
  544.4 6.7 pad_maximum_fusion
  560.8 11.5 %convolution_convert_fusion.1 = bf16[1536,6144]{1,0:T(8,128)(2,1)} fusion(bf16[256,6144]{1,0:T(8,128)(2,1)} %add_convert_fusion, f32[256,1536]{1,0:T(8,128)S(1)} %copy-done.6, f32[1536]{0:T(1024)S(1)} %copy-done.37, f32[256]{0:T(256)S(1)} %copy-done.50, f32[256]{0:T(256)S(1)} %copy-done.46), kind=kOutput, calls=%fused_computation.1 | convolution fusion | flops 4842848256 | bytes 23601152 | tf_op jit(solution)/shard_map/qd,qf->df/dot_general | solution.py:512
  572.3 9.0 %convolution_convert_fusion = bf16[6144,1536]{1,0:T(8,128)(2,1)} fusion(bf16[256,6144]{1,0:T(8,128)(2,1)S(1)} %copy-done.18, bf16[256,1536]{1,0:T(8,128)(2,1)S(1)} %bitcast.138), kind=kOutput, calls=%fused_computation | convolution fusion | flops 4841275392 | bytes 22806528 | tf_op jit(solution)/shard_map/qf,qd->fd/dot_general | solution.py:509
  581.3 276.0 %scatter_grads.1 = (f32[48,4608]{1,0:T(8,128)S(1)}, f32[48,1536]{1,0:T(8,128)S(1)}, f32[48,6144]{1,0:T(8,128)S(1)}, f32[192,1536]{1,0:T(8,128)S(1)}, f32[16,128]...) custom-call(bf16[2,2,4,2,48,4608]{5,4,3,2,1,0:T(8,128)(2,1)} %bitcas, ...), custom_call_target="tpu_custom_call" | custom-call | tf_op jit(solution)/shard_map/scatter_grads/pallas_call | solution.py:270
  (228 shorter events, 86.0 us)
Async XLA Ops:
  5.3 284.6 %copy-start = (bf16[18,48,1536]{2,1,0:T(8,128)(2,1)S(1)}, bf16[18,48,1536]{2,1,0:T(8,128)(2,1)}, u32[]{:S(2)}) copy-start(bf16[18,48,1536]{2,1,0:T(8,128)(2,1)} %param.23) | copy-start | bytes 7962628
  17.7 273.8 %copy-start.2 = (bf16[4,64,1536]{2,1,0:T(8,128)(2,1)S(1)}, bf16[4,64,1536]{2,1,0:T(8,128)(2,1)}, u32[]{:S(2)}) copy-start(bf16[4,64,1536]{2,1,0:T(8,128)(2,1)} %param.22) | copy-start | bytes 2359300
  288.9 12.1 %copy-start.38 = (f32[1536]{0:T(1024)}, f32[1536]{0:T(1024)S(1)}, u32[]{:S(2)}) copy-start(f32[1536]{0:T(1024)S(1)} %get-tuple-element.93) | copy-start | bytes 18436
  290.5 10.5 %copy-start.32 = (f32[18,48]{1,0:T(8,128)}, f32[18,48]{1,0:T(8,128)S(1)}, u32[]{:S(2)}) copy-start(f32[18,48]{1,0:T(8,128)S(1)} %broadcast_multiply_fusion.1) | copy-start | bytes 10372
  291.6 9.4 %copy-start.40 = (f32[18,48]{1,0:T(8,128)}, f32[18,48]{1,0:T(8,128)S(1)}, u32[]{:S(2)}) copy-start(f32[18,48]{1,0:T(8,128)S(1)} %fusion.42) | copy-start | bytes 10372
  302.9 14.4 %copy-start.25 = (bf16[18,48,1536]{2,1,0:T(8,128)(2,1)}, bf16[18,48,1536]{2,1,0:T(8,128)(2,1)S(1)}, u32[]{:S(2)}) copy-start(bf16[18,48,1536]{2,1,0:T(8,128)(2,1)S(1)} %multiply_convert_fusion.3) | copy-start | bytes 7962628
  352.0 10.4 %copy-start.3 = (bf16[4,64,1536]{2,1,0:T(8,128)(2,1)S(1)}, bf16[4,64,1536]{2,1,0:T(8,128)(2,1)}, u32[]{:S(2)}) copy-start(bf16[4,64,1536]{2,1,0:T(8,128)(2,1)} %param.22) | copy-start | bytes 2359300
  366.5 66.6 %copy-start.5 = (f32[256,1536]{1,0:T(8,128)}, f32[256,1536]{1,0:T(8,128)S(1)}, u32[]{:S(2)}) copy-start(f32[256,1536]{1,0:T(8,128)S(1)} %get-tuple-element.123) | copy-start | bytes 4718596
  366.6 66.6 %copy-start.45 = (f32[256]{0:T(256)}, f32[256]{0:T(256)S(1)}, u32[]{:S(2)}) copy-start(f32[256]{0:T(256)S(1)} %broadcast_multiply_fusion.3) | copy-start | bytes 3076
  366.9 66.3 %copy-start.49 = (f32[256]{0:T(256)}, f32[256]{0:T(256)S(1)}, u32[]{:S(2)}) copy-start(f32[256]{0:T(256)S(1)} %fusion.55) | copy-start | bytes 3076
  366.9 22.7 %copy-start.14 = (bf16[4,64,1536]{2,1,0:T(8,128)(2,1)S(1)}, bf16[4,64,1536]{2,1,0:T(8,128)(2,1)}, u32[]{:S(2)}) copy-start(bf16[4,64,1536]{2,1,0:T(8,128)(2,1)} %param.25) | copy-start | bytes 2359300
  411.2 27.3 %slice-start.2 = ((s8[4718592]{0:T(1024)(128)(4,1)}), s8[4194304]{0:T(1024)(128)(4,1)S(1)}, s32[]{:S(2)}) async-start(s8[4718592]{0:T(1024)(128)(4,1)} %bitcast.128), calls=%async_computation.2 | async-start | bytes 8388608
  421.9 16.6 %slice-start.3 = ((s8[4718592]{0:T(1024)(128)(4,1)}), s8[524288]{0:T(1024)(128)(4,1)S(1)}, s32[]{:S(2)}) async-start(s8[4718592]{0:T(1024)(128)(4,1)} %bitcast.128), calls=%async_computation.3 | async-start | bytes 1048576
  502.1 42.1 %slice-start = ((s8[4718592]{0:T(1024)(128)(4,1)}), s8[524288]{0:T(1024)(128)(4,1)S(1)}, s32[]{:S(2)}) async-start(s8[4718592]{0:T(1024)(128)(4,1)} %bitcast.125), calls=%async_computation | async-start | bytes 1048576
  519.7 16.9 %copy-start.4 = (bf16[4,64,1536]{2,1,0:T(8,128)(2,1)S(1)}, bf16[4,64,1536]{2,1,0:T(8,128)(2,1)}, u32[]{:S(2)}) copy-start(bf16[4,64,1536]{2,1,0:T(8,128)(2,1)} %param.22) | copy-start | bytes 2359300
  519.7 16.9 %copy-start.11 = (bf16[16,96,256]{2,1,0:T(8,128)(2,1)S(1)}, bf16[16,96,256]{2,1,0:T(8,128)(2,1)}, u32[]{:S(2)}) copy-start(bf16[16,96,256]{2,1,0:T(8,128)(2,1)} %copy-done.10) | copy-start | bytes 2359300
  519.7 16.9 %copy-start.35 = (f32[1536]{0:T(1024)S(1)}, f32[1536]{0:T(1024)}, u32[]{:S(2)}) copy-start(f32[1536]{0:T(1024)} %copy-done.34) | copy-start | bytes 18436
  519.7 16.9 %copy-start.53 = (f32[256]{0:T(256)S(1)}, f32[256]{0:T(256)}, u32[]{:S(2)}) copy-start(f32[256]{0:T(256)} %div.162) | copy-start | bytes 3076
  519.7 24.6 %slice-start.1 = ((s8[4718592]{0:T(1024)(128)(4,1)}), s8[4194304]{0:T(1024)(128)(4,1)S(1)}, s32[]{:S(2)}) async-start(s8[4718592]{0:T(1024)(128)(4,1)} %bitcast.125), calls=%async_computation.1 | async-start | bytes 8388608
  560.8 11.5 %copy-start.18 = (bf16[256,6144]{1,0:T(8,128)(2,1)S(1)}, bf16[256,6144]{1,0:T(8,128)(2,1)}, u32[]{:S(2)}) copy-start(bf16[256,6144]{1,0:T(8,128)(2,1)} %get-tuple-element.114) | copy-start | bytes 9437188
  581.3 278.9 %copy-start.56 = (f32[48,8]{0,1:T(8,128)S(1)}, f32[48,8]{0,1:T(8,128)}, u32[]{:S(2)}) copy-start(f32[48,8]{0,1:T(8,128)} %param.38) | copy-start | bytes 4612
  858.6 8.8 %copy-start.20 = (f32[192,1536]{1,0:T(8,128)S(1)}, f32[192,1536]{1,0:T(8,128)}, u32[]{:S(2)}) copy-start(f32[192,1536]{1,0:T(8,128)} %param.35) | copy-start | bytes 3538948
  858.6 8.8 %copy-start.26 = (f32[192,1536]{1,0:T(8,128)S(1)}, f32[192,1536]{1,0:T(8,128)}, u32[]{:S(2)}) copy-start(f32[192,1536]{1,0:T(8,128)} %param.36) | copy-start | bytes 3538948
  858.6 8.8 %copy-start.27 = (f32[192,1536]{1,0:T(8,128)S(1)}, f32[192,1536]{1,0:T(8,128)}, u32[]{:S(2)}) copy-start(f32[192,1536]{1,0:T(8,128)} %param.37) | copy-start | bytes 3538948
  (47 other events, 173.2 us)

commit v2 on v1

--- a/solution.py
+++ b/solution.py
@@ -1,4 +1,5 @@
 import functools
+import math
 
 import jax
 import jax.numpy as jnp
@@ -77,29 +78,6 @@
 
 def n_sems(n_z): return n_z + 2
 
-def gather_kernel(n_z, plan, n_w, *refs):
-    ins, outs, (ss, rs, ls) = refs[:n_w], refs[n_w:2*n_w], refs[2*n_w:]
-    place = Place(n_z)
-    greet(place)
-    locals_ = []
-    for i in range(n_w):
-        d = pltpu.make_async_copy(ins[i], outs[i].at[block_index(place, ())], ls.at[i])
-        d.start(); locals_.append(d)
-    stages = [[Gather(place, ins[w], outs[w], rows, cols, order, (ss, rs), j * n_sems(n_z)) for (j, w, rows, cols, order) in stage] for stage in plan]
-    waited = set()
-    T, steps = len(stages), 4
-    for t in range(T + steps):
-        for back in range(steps + 1):
-            u = t - back
-            if not 0 <= u < T: continue
-            for g, (j, w, *_) in zip(stages[u], plan[u]):
-                if back == 1 and w not in waited:
-                    locals_[w].wait(); waited.add(w)
-                if back > 0: g.arrive(back - 1)
-                if back < steps: g.start(back)
-    for st in stages:
-        for g in st: g.finish()
-
 def number(plan):
     j, out = 0, []
     for stage in plan:
@@ -108,19 +86,6 @@
             new.append((j,) + piece); j += 1
         out.append(new)
     return out, j
-
-def gather_all(shards, plan, n_z):
-    plan, count = number(plan)
-    n_w = len(shards)
-    return pl.pallas_call(
-        functools.partial(gather_kernel, n_z, plan, n_w),
-        out_shape=[jax.ShapeDtypeStruct((2, 2, n_z, 2) + s.shape, s.dtype) for s in shards],
-        in_specs=[pl.BlockSpec(memory_space=pltpu.VMEM)] * n_w,
-        out_specs=[pl.BlockSpec(memory_space=ANY)] * n_w,
-        scratch_shapes=[pltpu.SemaphoreType.DMA((count * n_sems(n_z),)), pltpu.SemaphoreType.DMA((count * n_sems(n_z),)), pltpu.SemaphoreType.DMA((n_w,))],
-        name="gather_weights",
-        compiler_params=pltpu.CompilerParams(collective_id=0, has_side_effects=True),
-    )(*shards)
 
 ZYX, ZXY = ("z", "y", "x", "c"), ("z", "x", "y", "c")
 
@@ -297,6 +262,262 @@
     return n_dp == 4 and n_fsdp % 2 == 0 and all(s.shape[0] % 48 == 0 and s.shape[1] % 1536 == 0 for s in shards)
 
 
+def out_copies(pairs, sems, at, running):
+    for src, dst in pairs:
+        d = pltpu.make_async_copy(src, dst, sems.at[len(running)])
+        d.start()
+        running.append(d)
+
+
+def dot(a, b, contract=((1,), (0,))):
+    return lax.dot_general(a, b, (contract, ((), ())), preferred_element_type=jnp.float32)
+
+
+def head_windows(head):
+    group = 128 // math.gcd(head, 128)
+    out = []
+    for j in range(group):
+        first, last = j * head // 128, ((j + 1) * head - 1) // 128
+        out.append((first, last + 1, j * head - first * 128))
+    return out, group * head
+
+
+def lanes_of(rows, tiles, start, head):
+    lane = lax.broadcasted_iota(jnp.int32, (rows, tiles * 128), 1)
+    return (lane >= start) & (lane < start + head)
+
+
+def normed(rows_in, gain):
+    centered = rows_in - jnp.mean(rows_in, axis=-1, keepdims=True)
+    var_row = jnp.mean(centered * centered, axis=-1, keepdims=True)
+    return centered * lax.rsqrt(var_row + norm_eps) * gain
+
+
+def forward_kernel(n_z, plan, needs, *refs):
+    (sh, (lat, media, cot, hot, bias), full, outs, scratch) = refs[:5], refs[5:10], refs[10:15], refs[15:26], refs[26:]
+    o_keys, o_q, o_k, o_v, o_att, o_hid, o_act, o_dpre, o_mid, o_new, o_lse = outs
+    keys, q, k, v, att, hid, act, slope, dact, mid, new, tiny, tiny_t, lse, wbuf, wdown, ss, rs, ls, os_, ws = scratch
+    f_qkv, f_out, f_up, f_down, f_tiny = full
+    place = Place(n_z)
+    greet(place)
+    queries_n, model = lat.shape
+    media_rows = media.shape[0]
+    key_rows = media_rows + queries_n
+    hidden_n = act.shape[1]
+    head = model // HEADS
+    windows, group_width = head_windows(head)
+    scale = 1.0 / head**0.5
+    written = []
+
+    def load(src, dst):
+        d = pltpu.make_async_copy(src, dst, ws.at[0])
+        d.start()
+        d.wait()
+
+    def write(*pairs):
+        out_copies(pairs, os_, 0, written)
+
+    def norms():
+        load(f_tiny, tiny)
+        tiny_t[...] = tiny[...].reshape(model, 128).astype(jnp.float32).T
+        keys[media_rows:key_rows, :] = normed(lat[...].astype(jnp.float32), tiny_t[9:10, :]).astype(jnp.bfloat16)
+
+        def frame(i, carry):
+            rows = pl.ds(pl.multiple_of(i * 48, 48), 48)
+            mixed = media[rows, :].astype(jnp.float32) + dot(hot[rows, :], tiny_t[...].astype(jnp.bfloat16))
+            keys[rows, :] = normed(mixed, tiny_t[8:9, :]).astype(jnp.bfloat16)
+            return carry
+
+        lax.fori_loop(0, media_rows // 48, frame, 0)
+        write((keys, o_keys))
+
+    def project(i, dst, first):
+        load(f_qkv.at[:, :, :, :, :, pl.ds(i * model, model)], wbuf)
+
+        def tile(n, carry):
+            cols = pl.ds(pl.multiple_of(n * 256, 256), 256)
+            w = wbuf[:, :, :, :, :, cols].reshape(model, 256)
+            dst[:, cols] = dot(keys[first:key_rows, :], w).astype(jnp.bfloat16)
+            return carry
+
+        lax.fori_loop(0, model // 256, tile, 0)
+
+    def project_q():
+        project(0, q, media_rows)
+        write((q, o_q))
+
+    def project_k():
+        project(1, k, 0)
+        write((k, o_k))
+
+    def project_v():
+        project(2, v, 0)
+        write((v, o_v))
+
+    def attend(g):
+        base = g * group_width
+        tiles = [jnp.zeros((queries_n, 128), jnp.float32) for _ in range(group_width // 128)]
+        for j, (t0, t1, start) in enumerate(windows):
+            cols = slice(base + t0 * 128, base + t1 * 128)
+            qh = q[:, cols]
+            qh = jnp.where(lanes_of(queries_n, t1 - t0, start, head), qh, jnp.zeros_like(qh))
+            s = dot(k[:, cols], qh, ((1,), (1,))) * scale + bias[...]
+            top = jnp.max(s, axis=0, keepdims=True)
+            e = jnp.exp(s - top)
+            total = jnp.sum(e, axis=0, keepdims=True)
+            p = (e * (1.0 / total)).astype(jnp.bfloat16)
+            lse[g * len(windows) + j : g * len(windows) + j + 1, :] = top + jnp.log(total)
+            vh = v[:, cols]
+            vh = jnp.where(lanes_of(key_rows, t1 - t0, start, head), vh, jnp.zeros_like(vh))
+            got = dot(p, vh, ((0,), (0,)))
+            for t in range(t0, t1):
+                tiles[t] = tiles[t] + got[:, (t - t0) * 128 : (t - t0 + 1) * 128]
+        for t, tile in enumerate(tiles):
+            att[:, base + t * 128 : base + (t + 1) * 128] = tile.astype(jnp.bfloat16)
+
+    def project_out():
+        write((att, o_att), (lse, o_lse))
+        load(f_out, wbuf)
+
+        def tile(n, carry):
+            cols = pl.ds(pl.multiple_of(n * 256, 256), 256)
+            w = wbuf[:, :, :, :, :, cols].reshape(model, 256)
+            mid[:, cols] = lat[:, cols].astype(jnp.float32) + dot(att[...], w)
+            return carry
+
+        lax.fori_loop(0, model // 256, tile, 0)
+        hid[...] = normed(mid[...], tiny_t[10:11, :]).astype(jnp.bfloat16)
+        write((mid, o_mid), (hid, o_hid))
+
+    def up(i):
+        load(f_up.at[:, :, :, :, :, pl.ds(i * model, model)], wbuf)
+
+        def tile(n, carry):
+            cols = pl.ds(pl.multiple_of(n * 256, 256), 256)
+            into = pl.ds(pl.multiple_of(i * model + n * 256, 256), 256)
+            w = wbuf[:, :, :, :, :, cols].reshape(model, 256)
+            x = dot(hid[...], w)
+            cdf = 0.5 + 0.5 * lax.erf(x * 0.7071067811865476)
+            act[:, into] = (x * cdf).astype(jnp.bfloat16)
+            slope[:, into] = cdf + x * (jnp.exp(-0.5 * x * x) * 0.3989422804014327)
+            return carry
+
+        lax.fori_loop(0, model // 256, tile, 0)
+        if (i + 1) * model == hidden_n:
+            write((act, o_act))
+
+    def down(i, width):
+        cols = slice(i * width, (i + 1) * width)
+        load(f_down.at[:, :, :, :, :, pl.ds(i * width, width)], wdown)
+        per = hidden_n // 4
+        got = jnp.zeros((queries_n, width), jnp.float32)
+        for b in range(4):
+            w = wdown[b // 2, b % 2].reshape(per, width)
+            got = got + dot(act[:, b * per : (b + 1) * per], w)
+            back = dot(cot[:, cols], w, ((1,), (1,)))
+            if i == 0:
+                dact[:, b * per : (b + 1) * per] = back
+            else:
+                dact[:, b * per : (b + 1) * per] += back
+        new[:, cols] = (mid[:, cols] + got).astype(jnp.bfloat16)
+
+    def finish():
+        for d in written:
+            d.wait()
+        written.clear()
+
+        def tile(n, carry):
+            cols = pl.ds(pl.multiple_of(n * 512, 512), 512)
+            act[:, cols] = (dact[:, cols] * slope[:, cols]).astype(jnp.bfloat16)
+            return carry
+
+        lax.fori_loop(0, hidden_n // 512, tile, 0)
+        write((act, o_dpre), (new, o_new))
+        for d in written:
+            d.wait()
+
+    work = [(needs["tiny"], 8, norms), (needs["q"], 4, project_q), (needs["k"], 8, project_k), (needs["v"], 8, project_v)]
+    work += [(needs["v"], 7, functools.partial(attend, g)) for g in range(model // group_width)]
+    work += [(needs["out"], 5, project_out)]
+    work += [(s, 6, functools.partial(up, i)) for i, s in enumerate(needs["up"])]
+    work += [(s, 5, functools.partial(down, i, model // len(needs["down"]))) for i, s in enumerate(needs["down"])]
+    work += [(needs["down"][-1], 5, finish)]
+    locals_ = []
+    for i in range(5):
+        d = pltpu.make_async_copy(sh[i], full[i].at[block_index(place, ())], ls.at[i])
+        d.start()
+        locals_.append(d)
+    stages = [[Gather(place, sh[w], full[w], rows, cols, order, (ss, rs), j * n_sems(n_z)) for (j, w, rows, cols, order) in stage] for stage in plan]
+    waited = set()
+    total, steps = len(stages), 4
+    for t in range(total + steps):
+        for back in range(steps + 1):
+            u = t - back
+            if not 0 <= u < total:
+                continue
+            for g, (j, w, *_) in zip(stages[u], plan[u]):
+                if back == 1 and w not in waited:
+                    locals_[w].wait()
+                    waited.add(w)
+                if back > 0:
+                    g.arrive(back - 1)
+                if back < steps:
+                    g.start(back)
+        room = 14
+        while work and work[0][0] <= t - steps and (room > 0 or t == total + steps - 1):
+            need, cost, piece = work.pop(0)
+            room -= cost
+            piece()
+    for st in stages:
+        for g in st:
+            g.finish()
+
+
+def forward_plan(shards, model):
+    two = lambda w, rows, first, width: [(w, (0, rows), (first, width), ZYX), (w, (0, rows), (first + width, width), ZXY)]
+    rows, half = shards[1].shape[0], model // 2
+    stages, needs = [[(4, (0, rows), (0, 128), ZYX)]], {"tiny": 0}
+    for i, name in enumerate("qkv"):
+        needs[name] = len(stages)
+        stages.append(two(0, rows, i * model, half))
+    needs["out"] = len(stages)
+    stages.append(two(1, rows, 0, half))
+    needs["up"], needs["down"] = [], []
+    for i in range(shards[2].shape[1] // model):
+        needs["up"].append(len(stages))
+        stages.append(two(2, rows, i * model, half))
+    for i in range(model // 256):
+        needs["down"].append(len(stages))
+        stages.append(two(3, shards[3].shape[0], i * 256, 128))
+    return stages, needs
+
+
+def forward_all(shards, lat, media, cot, hot, bias, n_z):
+    model, hidden_n = lat.shape[1], shards[2].shape[1]
+    stages, needs = forward_plan(shards, model)
+    plan, count = number(stages)
+    queries_n, media_rows = lat.shape[0], media.shape[0]
+    key_rows = queries_n + media_rows
+    bf, f32 = jnp.bfloat16, jnp.float32
+    rows = shards[1].shape[0]
+    made = [((key_rows, model), bf), ((queries_n, model), bf), ((key_rows, model), bf), ((key_rows, model), bf), ((queries_n, model), bf),
+            ((queries_n, model), bf), ((queries_n, hidden_n), bf), ((queries_n, hidden_n), bf), ((queries_n, model), f32), ((queries_n, model), bf), ((HEADS, queries_n), f32)]
+    vm = made[:7] + [((queries_n, hidden_n), f32), ((queries_n, hidden_n), f32), ((queries_n, model), f32), ((queries_n, model), bf),
+                     ((2, 2, n_z, 2, rows, 128), bf), ((128, model), f32), ((HEADS, queries_n), f32), ((2, 2, n_z, 2, rows, model), bf), ((2, 2, n_z, 2, shards[3].shape[0], 256), bf)]
+    sem = pltpu.SemaphoreType.DMA
+    in_vmem, in_any = pl.BlockSpec(memory_space=pltpu.VMEM), pl.BlockSpec(memory_space=ANY)
+    out = pl.pallas_call(
+        functools.partial(forward_kernel, n_z, plan, needs),
+        out_shape=[jax.ShapeDtypeStruct((2, 2, n_z, 2) + s.shape, s.dtype) for s in shards] + [jax.ShapeDtypeStruct(*m) for m in made],
+        in_specs=[in_vmem] * 10,
+        out_specs=[in_any] * (5 + len(made)),
+        scratch_shapes=[pltpu.VMEM(*m) for m in vm] + [sem((count * n_sems(n_z),)), sem((count * n_sems(n_z),)), sem((5,)), sem((16,)), sem((1,))],
+        name="gather_and_forward",
+        compiler_params=pltpu.CompilerParams(collective_id=0, has_side_effects=True, vmem_limit_bytes=60 * 2**20),
+    )(*shards, lat, media, cot, hot, bias)
+    return out[:5], out[5:]
+
+
 def layer_norm(values_in, gain):
     mean_row = jnp.mean(values_in, axis=-1, keepdims=True)
     centered = values_in - mean_row
@@ -444,18 +665,7 @@
     own_rows, model = w_qkv.shape[0], w_qkv.shape[2]
     shards = [low_qkv.reshape(own_rows, -1), low_out, low_up, low_down]
     kernels = fits_kernels(n_dp, n_fsdp, shards)
-    if kernels:
-        n_z = n_fsdp // 2
-        listed = [(w, shards[w].shape[0], shards[w].shape[1]) for w in range(4)]
-        time_len = low_time.shape[1]
-        tiny = jnp.concatenate([low_time.T, low_gains.T], axis=0)
-        tiny = jnp.pad(tiny, ((0, 16 - tiny.shape[0]), (0, 128 - own_rows)))
-        full = gather_all(shards + [tiny], plan_with((ZYX, ZXY), listed, 768, True), n_z)
-        full_qkv, full_out, full_up, full_down = (f.reshape(-1, f.shape[-1]) for f in full[:4])
-        full_qkv = full_qkv.reshape(model, 3, model)
-        tiny_all = full[4].reshape(n_dp * n_fsdp, 16, 128)[:, :, :own_rows].transpose(1, 0, 2).reshape(16, model)
-        full_time, full_gains = tiny_all[:time_len].T, tiny_all[time_len : time_len + 3].T
-    else:
+    if not kernels:
         full_qkv, full_out, full_up, full_down, full_time, full_gains = gather_params(
             low_qkv, low_out, low_up, low_down, low_time, low_gains
         )
@@ -465,50 +675,68 @@
     media_rows = frame_slots * patch_rows
     head_size = model_width // HEADS
     score_scale = 1.0 / head_size**0.5
-    frame_owner, time_hot = frame_tables(frame_counts, frame_slots, full_time.shape[1])
+    frame_owner, time_hot = frame_tables(frame_counts, frame_slots, low_time.shape[1])
+    query_owner = jnp.arange(queries_n, dtype=jnp.int32) // lat_count
+    key_owner = jnp.concatenate([jnp.repeat(frame_owner, patch_rows), query_owner], axis=0)
+    allowed = query_owner[:, None] == key_owner[None, :]
+    lat_flat = latents.reshape(queries_n, model_width)
+    lat_rows = lat_flat.astype(jnp.float32)
+    key_rows = media_rows + queries_n
+    if kernels:
+        n_z = n_fsdp // 2
+        time_len = low_time.shape[1]
+        tiny = jnp.concatenate([low_time, low_gains], axis=1)
+        tiny = jnp.pad(tiny, ((0, 0), (0, 128 - tiny.shape[1])))
+        hot = jnp.pad(jnp.repeat(time_hot, patch_rows, axis=0), ((0, 0), (0, 128 - time_len))).astype(jnp.bfloat16)
+        bias = jnp.where(allowed.T, 0.0, -1e30).astype(jnp.float32)
+        full, made = forward_all(
+            shards + [tiny], lat_flat, media.reshape(media_rows, model_width), cotangent.reshape(queries_n, model_width), hot, bias, n_z
+        )
+        full_qkv, full_out, full_up, full_down, full_tiny = (f.reshape(-1, f.shape[-1]) for f in full)
+        full_qkv = full_qkv.reshape(model, 3, model)
+        full_time, full_gains = full_tiny[:, :time_len], full_tiny[:, time_len : time_len + 3]
+        keys_in, queries, keys_all, values_all, attended, hidden_low, act_low, d_pre, middle, new_rows, log_total = made
+        log_total = log_total[:, :, None]
     time_f32 = full_time.astype(jnp.float32)
     gains_f32 = full_gains.astype(jnp.float32)
     frame_time = jnp.dot(time_hot, time_f32.T, precision=highest)
     mixed = media.astype(jnp.float32) + frame_time[:, None, :]
     media_norm, media_back = jax.vjp(layer_norm, mixed, gains_f32[:, 0])
-    media_low = media_norm.astype(jnp.bfloat16).reshape(media_rows, model_width)
-    lat_rows = latents.reshape(queries_n, model_width).astype(jnp.float32)
     lat_norm, lat_back = jax.vjp(layer_norm, lat_rows, gains_f32[:, 1])
-    lat_low = lat_norm.astype(jnp.bfloat16)
-    keys_in = jnp.concatenate([media_low, lat_low], axis=0)
-    key_rows = keys_in.shape[0]
-    qkv_flat = full_qkv.reshape(model_width, 3 * model_width)
-    queries = jnp.dot(
-        lat_low, qkv_flat[:, :model_width], preferred_element_type=jnp.float32
-    ).astype(jnp.bfloat16)
-    key_value = jnp.dot(
-        keys_in, qkv_flat[:, model_width:], preferred_element_type=jnp.float32
-    ).astype(jnp.bfloat16)
+    if not kernels:
+        lat_low = lat_norm.astype(jnp.bfloat16)
+        media_low = media_norm.astype(jnp.bfloat16).reshape(media_rows, model_width)
+        keys_in = jnp.concatenate([media_low, lat_low], axis=0)
+        qkv_flat = full_qkv.reshape(model_width, 3 * model_width)
+        queries = jnp.dot(lat_low, qkv_flat[:, :model_width], preferred_element_type=jnp.float32).astype(jnp.bfloat16)
+        key_value = jnp.dot(keys_in, qkv_flat[:, model_width:], preferred_element_type=jnp.float32).astype(jnp.bfloat16)
+        keys_all, values_all = key_value[:, :model_width], key_value[:, model_width:]
+    lat_low = keys_in[media_rows:]
     q_heads = queries.reshape(queries_n, HEADS, head_size)
-    k_heads = key_value[:, :model_width].reshape(key_rows, HEADS, head_size)
-    v_heads = key_value[:, model_width:].reshape(key_rows, HEADS, head_size)
-    query_owner = jnp.arange(queries_n, dtype=jnp.int32) // lat_count
-    key_owner = jnp.concatenate([jnp.repeat(frame_owner, patch_rows), query_owner], axis=0)
-    allowed = query_owner[:, None] == key_owner[None, :]
-    scores = masked_scores(q_heads, k_heads, allowed, score_scale)
-    row_top = jnp.max(scores, axis=-1, keepdims=True)
-    row_total = jnp.sum(jnp.exp(scores - row_top), axis=-1, keepdims=True)
-    log_total = row_top + jnp.log(row_total)
-    probs_low = jnp.exp(scores - log_total).astype(jnp.bfloat16)
-    attended = jnp.einsum("hqk,khe->qhe", probs_low, v_heads, preferred_element_type=jnp.float32)
-    attended = attended.reshape(queries_n, model_width).astype(jnp.bfloat16)
-    middle = lat_rows + jnp.dot(attended, full_out, preferred_element_type=jnp.float32)
+    k_heads = keys_all.reshape(key_rows, HEADS, head_size)
+    v_heads = values_all.reshape(key_rows, HEADS, head_size)
+    if not kernels:
+        scores = masked_scores(q_heads, k_heads, allowed, score_scale)
+        row_top = jnp.max(scores, axis=-1, keepdims=True)
+        row_total = jnp.sum(jnp.exp(scores - row_top), axis=-1, keepdims=True)
+        log_total = row_top + jnp.log(row_total)
+        probs_low = jnp.exp(scores - log_total).astype(jnp.bfloat16)
+        attended = jnp.einsum("hqk,khe->qhe", probs_low, v_heads, preferred_element_type=jnp.float32)
+        attended = attended.reshape(queries_n, model_width).astype(jnp.bfloat16)
+        middle = lat_rows + jnp.dot(attended, full_out, preferred_element_type=jnp.float32)
     hidden, ffn_back = jax.vjp(layer_norm, middle, gains_f32[:, 2])
-    hidden_low = hidden.astype(jnp.bfloat16)
-    pre_act = jnp.dot(hidden_low, full_up, preferred_element_type=jnp.float32)
-    activated, gelu_back = jax.vjp(exact_gelu, pre_act)
-    act_low = activated.astype(jnp.bfloat16)
-    result = middle + jnp.dot(act_low, full_down, preferred_element_type=jnp.float32)
-    new_latents = result.astype(jnp.bfloat16).reshape(item_slots, lat_count, model_width)
+    if not kernels:
+        hidden_low = hidden.astype(jnp.bfloat16)
+        pre_act = jnp.dot(hidden_low, full_up, preferred_element_type=jnp.float32)
+        activated, gelu_back = jax.vjp(exact_gelu, pre_act)
+        act_low = activated.astype(jnp.bfloat16)
+        new_rows = (middle + jnp.dot(act_low, full_down, preferred_element_type=jnp.float32)).astype(jnp.bfloat16)
+    new_latents = new_rows.reshape(item_slots, lat_count, model_width)
     d_result = cotangent.reshape(queries_n, model_width)
     g_down = jnp.einsum("qf,qd->fd", act_low, d_result, preferred_element_type=jnp.float32)
-    d_act = jnp.einsum("qd,fd->qf", d_result, full_down, preferred_element_type=jnp.float32)
-    d_pre = gelu_back(d_act)[0].astype(jnp.bfloat16)
+    if not kernels:
+        d_act = jnp.einsum("qd,fd->qf", d_result, full_down, preferred_element_type=jnp.float32)
+        d_pre = gelu_back(d_act)[0].astype(jnp.bfloat16)
     g_up = jnp.einsum("qd,qf->df", hidden_low, d_pre, preferred_element_type=jnp.float32)
     d_hidden = jnp.einsum("qf,df->qd", d_pre, full_up, preferred_element_type=jnp.float32)
     d_middle_ln, g_gain_ffn = ffn_back(d_hidden)
@@ -575,6 +803,7 @@
         tiny_g = jnp.concatenate([g_time, g_gains], axis=1).T.reshape(time_len + 3, -1, own_rows).transpose(1, 0, 2)
         tiny_g = jnp.pad(tiny_g, ((0, 0), (0, 16 - tiny_g.shape[1]), (0, 128 - own_rows)))
         grads = [blocks(g, s.shape[0]) for g, s in zip((g_qkv, g_out, g_up, g_down), shards)] + [blocks(tiny_g, 16)]
+        listed = [(w, shards[w].shape[0], shards[w].shape[1]) for w in range(4)]
         orders = (("x", "y", "z"), ("y", "x", "z"))
         own, squares = scatter_all(grads, plan_with(orders, listed[::-1], 768, False), n_z)
         own_tiny = own[4][: time_len + 3, :own_rows].T

time: 885 us -> 795 us (0.90)
  matrix products: 212 us -> 132 us
  other arithmetic: 76.7 us -> 64.9 us
  Pallas kernels: 544 us -> 553 us
    dot_general x7 -> x0, matrix products: 88.4 us -> none  [the longest x1 22.7 us: on_device(): pre_act = jnp.dot(hidden_low, full_up, preferred_element_type=jnp.float32)]
    slice x6 -> x2, local copies, waits for them, and re-layouts: 14.8 us -> 0.26 us  [the longest x1 0.2 us: on_device(): full_tiny[:, time_len:time_len + 3]]
    pallas_call x0 -> x3, local copies, waits for them, and re-layouts: none -> 13.7 us  [forward_all(): pl.pallas_call(functools.partial(forward_kernel, n_z, plan, needs), out_s...]
    pallas_call x1, Pallas kernels: 268 us -> 277 us  [forward_all(): pl.pallas_call(functools.partial(forward_kernel, n_z, plan, needs), out_s...]
    reduce_sum x1 -> x0, other arithmetic: 9.23 us -> none  [on_device(): row_total = jnp.sum(jnp.exp(scores - row_top), axis=-1, keepdims=True)]
where the time goes in v2:
time: 795 us; the launch traced here: 786 us
  Pallas kernels  553 us (70%)
  matrix products  132 us (17%)
  other arithmetic  64.9 us (8%)
  local copies, waits for them, and re-layouts  32.2 us (4%)
    pallas_call x1, Pallas kernels, forward_all(): pl.pallas_call(functools.partial(forward_kernel, n_z, plan, needs), out_s...  277 us
    pallas_call x1, Pallas kernels, scatter_all(): pl.pallas_call(functools.partial(scatter_kernel, n_z, plan, n_w, names),...  276 us
    dot_general x1, matrix products, on_device(): jnp.einsum('kd,kx->dx', keys_in, d_key_value, preferred_element_type=jnp....  19.1 us
    convert_element_type x1, other arithmetic, on_device(): d_scores = (probs * (d_probs - row_dot)).astype(jnp.bfloat16)  16.2 us

profile of v2, /device:TPU:0, one launch (start us, length us, event | category | flops | bytes accessed | tf_op | source)
XLA Modules:
  0.0 785.6 jit_solution(906513341193031160)
XLA Ops:
  14.4 277.0 %gather_and_forward.1 = (bf16[2,2,4,2,48,4608]{5,4,3,2,1,0:T(8,128)(2,1)}, bf16[2,2,4,2,48,1536]{5,4,3,2,1,0:T(8,128)(2,1)}, bf16[2,2,4,2,48,6144]{5,4,3,2,1,0:T...) custom-call(bf16[48,4608]{1,0:T(8,128)(2,1)} %bitcast.109, ...), custom_call_target="tpu_custom_call" | custom-call | tf_op jit(solution)/shard_map/gather_and_forward/pallas_call | solution.py:509
  295.6 10.3 %multiply_reduce_fusion.4 = (bf16[1536]{0:T(1024)(128)(2,1)S(1)}, f32[256]{0:T(256)S(1)}, f32[256,1536]{1,0:T(8,128)S(1)}) fusion(f32[256,1536]{1,0:T(8,128)S(1)} %copy-done.2, f32[256]{0:T(256)S(1)} %fusion.39, f32[256]{0:T(256)S(1)} %broadcast_multiply_fusion.3, f32[1536]{0:T(1024)S(1)} %get-tuple-element.136, bf16[256,6144]{1,0:T(8,128)(2,1)} %get-tuple-element.43, ...), kind=kOutput, calls=%fused_computation.41 | convolution fusion | flops 4834588672 | bytes 25178112 | tf_op jit(solution)/shard_map/qf,df->qd/dot_general | solution.py:741
  310.0 4.7 convolution_convert_fusion.5
  319.2 4.9 convolution_convert_fusion.4
  324.2 5.7 copy.110
  329.9 5.7 copy.113
  335.6 11.3 %fusion.51 = f32[16,256,1120]{1,2,0:T(8,128)} fusion(bf16[256,16,96]{0,2,1:T(8,128)(2,1)} %bitcast.100, bf16[1120,16,96]{0,2,1:T(8,128)(2,1)} %bitcast.95), kind=kOutput, calls=%fused_computation.128 | convolution fusion | flops 880803840 | bytes 22577152 | tf_op jit(solution)/shard_map/qhe,khe->hqk/dot_general | solution.py:753
  346.9 9.5 %convolution_convert_fusion.1 = bf16[1536,6144]{1,0:T(8,128)(2,1)} fusion(bf16[256,1536]{1,0:T(8,128)(2,1)S(1)} %copy-done.28, bf16[256,6144]{1,0:T(8,128)(2,1)S(1)} %copy-done.20), kind=kOutput, calls=%fused_computation.1 | convolution fusion | flops 4841275392 | bytes 22806528 | tf_op jit(solution)/shard_map/qd,qf->df/dot_general | solution.py:740
  356.4 14.7 %multiply_reduce_fusion = (f32[16,256]{1,0:T(8,128)S(1)}, f32[16,256,1120]{1,2,0:T(8,128)}) fusion(f32[16,256,1120]{1,2,0:T(8,128)} %fusion.51, f32[16,256]{1,0:T(8,128)S(1)} %copy-done.30, bf16[256,16,96]{0,2,1:T(8,128)(2,1)S(1)} %bitcast.102, bf16[1120,16,96]{0,2,1:T(8,128)(2,1)} %bitcast.89, pred[256,1120]{0,1:T(8,128)(4,1)S(1)} %broadcast_compare_fusion), kind=kOutput, calls=%fused_computation.6 | convolution fusion | flops 903737344 | bytes 41246720 | tf_op jit(solution)/shard_map/qhe,khe->hqk/dot_general | solution.py:616
  371.1 16.2 %multiply_convert_fusion = bf16[16,256,1120]{1,2,0:T(8,128)(2,1)} fusion(f32[16,256,1120]{1,2,0:T(8,128)} %get-tuple-element.163, f32[16,256,1120]{1,2,0:T(8,128)} %fusion.51, f32[16,256]{1,0:T(8,128)S(1)} %get-tuple-element.162), kind=kLoop, calls=%fused_computation.5 | loop fusion | flops 13762560 | bytes 45891584 | tf_op jit(solution)/shard_map/convert_element_type | solution.py:755
  387.3 11.1 %fusion.11 = bf16[16,96,1120]{2,1,0:T(8,128)(2,1)} fusion(bf16[256,16,96]{0,2,1:T(8,128)(2,1)} %bitcast.101, f32[16,256,1120]{1,2,0:T(8,128)} %get-tuple-element.163), kind=kOutput, calls=%fused_computation.28 | convolution fusion | flops 887111680 | bytes 22577152 | tf_op jit(solution)/shard_map/hqk,qhe->khe/dot_general | solution.py:773
  398.4 6.4 multiply_convert_fusion.2
  404.9 4.6 multiply_convert_fusion.1
  409.5 4.7 convolution_convert_fusion.3
  414.1 6.6 copy.114
  420.8 19.1 %convolution_convert_fusion.2 = bf16[1536,3072]{1,0:T(8,128)(2,1)} fusion(bf16[1120,1536]{1,0:T(8,128)(2,1)} %get-tuple-element.53, bf16[1120,1536]{0,1:T(8,128)(2,1)} %bitcast.107, bf16[1120,1536]{0,1:T(8,128)(2,1)} %bitcast.104), kind=kOutput, calls=%fused_computation.9 | convolution fusion | flops 10588127232 | bytes 19759104 | tf_op jit(solution)/shard_map/kd,kx->dx/dot_general | solution.py:779
  439.9 15.6 %fusion.3 = f32[1120,1536]{1,0:T(8,128)S(1)} fusion(bf16[1536,4608]{1,0:T(8,128)(2,1)} %bitcast.117, bf16[1120,1536]{0,1:T(8,128)(2,1)} %bitcast.108, bf16[1120,1536]{0,1:T(8,128)(2,1)S(1)} %bitcast.105), kind=kOutput, calls=%fused_computation.10 | convolution fusion | flops 10583408640 | bytes 23298048 | tf_op jit(solution)/shard_map/kx,dx->kd/dot_general | solution.py:782
  455.5 4.1 multiply_reduce_fusion.6
  460.0 10.7 %pad_maximum_fusion = bf16[1536,4608]{1,0:T(8,128)(2,1)} fusion(bf16[1536,3072]{1,0:T(8,128)(2,1)} %convolution_convert_fusion.2, bf16[1536,1536]{1,0:T(8,128)(2,1)S(1)} %bitcast.94), kind=kLoop, calls=%fused_computation.8 | loop fusion | flops 28311552 | bytes 28311552 | tf_op jit(solution)/shard_map/concatenate | solution.py:780
  478.0 3.0 add_reduce_fusion
  481.6 10.6 %convolution_convert_fusion = bf16[6144,1536]{1,0:T(8,128)(2,1)} fusion(bf16[256,6144]{1,0:T(8,128)(2,1)} %get-tuple-element.56, bf16[256,1536]{1,0:T(8,128)(2,1)} %bitcast.97), kind=kOutput, calls=%fused_computation | convolution fusion | flops 4841275392 | bytes 22806528 | tf_op jit(solution)/shard_map/qf,qd->fd/dot_general | solution.py:736
  492.2 276.0 %scatter_grads.1 = (f32[48,4608]{1,0:T(8,128)S(1)}, f32[48,1536]{1,0:T(8,128)S(1)}, f32[48,6144]{1,0:T(8,128)S(1)}, f32[192,1536]{1,0:T(8,128)S(1)}, f32[16,128]...) custom-call(bf16[2,2,4,2,48,4608]{5,4,3,2,1,0:T(8,128)(2,1)} %bitcas, ...), custom_call_target="tpu_custom_call" | custom-call | tf_op jit(solution)/shard_map/scatter_grads/pallas_call | solution.py:235
  777.7 2.4 multiply_subtract_fusion
  780.9 2.4 multiply_subtract_fusion.1
  (157 shorter events, 44.9 us)
Async XLA Ops:
  0.7 10.8 %copy-start.14 = (f32[48,6144]{1,0:T(8,128)S(1)}, f32[48,6144]{1,0:T(8,128)}, u32[]{:S(2)}) copy-start(f32[48,6144]{1,0:T(8,128)} %param.32) | copy-start | bytes 3538948
  0.7 9.9 %copy-start.17 = (f32[48,3,1536]{2,0,1:T(8,128)S(1)}, f32[48,3,1536]{2,0,1:T(8,128)}, u32[]{:S(2)}) copy-start(f32[48,3,1536]{2,0,1:T(8,128)} %param.26) | copy-start | bytes 2654212
  2.4 292.5 %copy-start.32 = (s32[18]{0:T(128)}, s32[18]{0:T(128)S(1)}, u32[]{:S(2)}) copy-start(s32[18]{0:T(128)S(1)} %iota_subtract_fusion) | copy-start | bytes 220
  2.5 292.5 %copy-start.34 = (pred[18]{0:T(512)(128)(4,1)}, pred[18]{0:T(512)(128)(4,1)S(1)}, u32[]{:S(2)}) copy-start(pred[18]{0:T(512)(128)(4,1)S(1)} %broadcast_compare_fusion.1) | copy-start | bytes 58
  5.2 7.1 copy-start.12
  295.6 10.3 %copy-start.3 = (f32[256,1536]{1,0:T(8,128)S(1)}, f32[256,1536]{1,0:T(8,128)}, u32[]{:S(2)}) copy-start(f32[256,1536]{1,0:T(8,128)} %get-tuple-element.46) | copy-start | bytes 4718596
  335.6 11.3 %copy-start.20 = (bf16[256,6144]{1,0:T(8,128)(2,1)S(1)}, bf16[256,6144]{1,0:T(8,128)(2,1)}, u32[]{:S(2)}) copy-start(bf16[256,6144]{1,0:T(8,128)(2,1)} %get-tuple-element.43) | copy-start | bytes 9437188
  335.6 11.3 %copy-start.28 = (bf16[256,1536]{1,0:T(8,128)(2,1)S(1)}, bf16[256,1536]{1,0:T(8,128)(2,1)}, u32[]{:S(2)}) copy-start(bf16[256,1536]{1,0:T(8,128)(2,1)} %get-tuple-element.55) | copy-start | bytes 2359300
  346.9 9.5 %copy-start.10 = (bf16[256,1536]{0,1:T(8,128)(2,1)S(1)}, bf16[256,1536]{0,1:T(8,128)(2,1)}, u32[]{:S(2)}) copy-start(bf16[256,1536]{0,1:T(8,128)(2,1)} %copy.111) | copy-start | bytes 2359300
  346.9 9.5 %copy-start.30 = (f32[16,256]{1,0:T(8,128)S(1)}, f32[16,256]{1,0:T(8,128)}, u32[]{:S(2)}) copy-start(f32[16,256]{1,0:T(8,128)} %get-tuple-element.49) | copy-start | bytes 49156
  387.3 17.6 %slice-start = ((s8[9175040]{0:T(1024)(128)(4,1)}), s8[786432]{0:T(1024)(128)(4,1)S(1)}, s32[]{:S(2)}) async-start(s8[9175040]{0:T(1024)(128)(4,1)} %bitcast.80), calls=%async_computation | async-start | bytes 1572864
  387.3 17.6 %slice-start.1 = ((s8[9175040]{0:T(1024)(128)(4,1)}), s8[4194304]{0:T(1024)(128)(4,1)S(1)}, s32[]{:S(2)}) async-start(s8[9175040]{0:T(1024)(128)(4,1)} %bitcast.80), calls=%async_computation.1 | async-start | bytes 8388608
  398.4 6.4 slice-start.2
  398.4 6.5 copy-start.11
  420.8 19.1 %copy-start.16 = (bf16[16,96,1120]{2,1,0:T(8,128)(2,1)S(1)}, bf16[16,96,1120]{2,1,0:T(8,128)(2,1)}, u32[]{:S(2)}) copy-start(bf16[16,96,1120]{2,1,0:T(8,128)(2,1)} %multiply_convert_fusion.1) | copy-start | bytes 10321924
  420.8 39.2 %slice-start.3 = ((s8[4718592]{0:T(1024)(128)(4,1)}), s8[524288]{0:T(1024)(128)(4,1)S(1)}, s32[]{:S(2)}) async-start(s8[4718592]{0:T(1024)(128)(4,1)} %bitcast.93), calls=%async_computation.3 | async-start | bytes 1048576
  439.9 15.6 %copy-start.1 = (bf16[4,64,1536]{2,1,0:T(8,128)(2,1)S(1)}, bf16[4,64,1536]{2,1,0:T(8,128)(2,1)}, u32[]{:S(2)}) copy-start(bf16[4,64,1536]{2,1,0:T(8,128)(2,1)} %param.22) | copy-start | bytes 2359300
  439.9 15.6 %copy-start.9 = (bf16[16,96,256]{2,1,0:T(8,128)(2,1)S(1)}, bf16[16,96,256]{2,1,0:T(8,128)(2,1)}, u32[]{:S(2)}) copy-start(bf16[16,96,256]{2,1,0:T(8,128)(2,1)} %copy-done.8) | copy-start | bytes 2359300
  439.9 20.1 %slice-start.4 = ((s8[4718592]{0:T(1024)(128)(4,1)}), s8[4194304]{0:T(1024)(128)(4,1)S(1)}, s32[]{:S(2)}) async-start(s8[4718592]{0:T(1024)(128)(4,1)} %bitcast.93), calls=%async_computation.4 | async-start | bytes 8388608
  460.0 11.5 %copy-start.7 = (bf16[4,64,1536]{2,1,0:T(8,128)(2,1)S(1)}, bf16[4,64,1536]{2,1,0:T(8,128)(2,1)}, u32[]{:S(2)}) copy-start(bf16[4,64,1536]{2,1,0:T(8,128)(2,1)} %param.25) | copy-start | bytes 2359300
  492.2 279.0 %copy-start.31 = (f32[48,8]{0,1:T(8,128)S(1)}, f32[48,8]{0,1:T(8,128)}, u32[]{:S(2)}) copy-start(f32[48,8]{0,1:T(8,128)} %param.38) | copy-start | bytes 4612
  769.6 5.1 copy-start.18
  769.6 5.1 copy-start.26
  769.6 5.1 copy-start.27
  (17 other events, 46.0 us)

commit v3 on v2

v3 whole, which is shorter than its diff:
```python
import functools
import math
import types

import jax
import jax.numpy as jnp
from jax import lax
from jax.experimental import pallas as pl
from jax.experimental.pallas import tpu as pltpu
from jax.sharding import PartitionSpec as P

DP, FSDP = "dp", "fsdp"
HEADS = 16
STEP = 10


highest = lax.Precision.HIGHEST
norm_eps = 1e-05
clip_limit = 1.0
beta_one = 0.9
beta_two = 0.999
adam_eps = 1e-08
decay_rate = 0.1

MESH=pl.DeviceIdType.MESH
ANY=pl.ANY

class Place:
    def __init__(self, n_z):
        dp = lax.axis_index(DP); fs = lax.axis_index(FSDP)
        self.n_z = n_z
        self.at = {"x": dp // 2, "c": dp % 2, "z": fs // 2, "y": fs % 2}
    def dev(self, **new):
        p = {**self.at, **new}
        return (p["x"] * 2 + p["c"], p["z"] * 2 + p["y"])
    def other(self, ax):
        return self.dev(**{ax: 1 - self.at[ax]})
    def along_z(self, k):
        return self.dev(z=(self.at["z"] + k) % self.n_z)
    def partners(self):
        return [self.other(a) for a in "cxy"] + [self.along_z(k) for k in range(1, self.n_z)]

def greet(place):
    bar = pltpu.get_barrier_semaphore()
    others = place.partners()
    for d in others:
        pl.semaphore_signal(bar, inc=1, device_id=d, device_id_type=MESH)
    pl.semaphore_wait(bar, len(others))

def block_index(place, held):
    return tuple(slice(None) if ax in held else place.at[ax] for ax in "xczy")

class Gather:
    def __init__(self, place, src, dst, rows, cols, order, sems, base):
        self.place, self.src, self.dst = place, src, dst
        self.sl = (pl.ds(*rows), pl.ds(*cols))
        self.order, self.sems, self.base = order, sems, base
        self.copies = {}
    def region(self, held):
        return self.dst.at[block_index(self.place, held) + self.sl]
    def start(self, step):
        p = self.place; ax = self.order[step]; held = self.order[:step]
        ss, rs = self.sems
        made = []
        n = self.base
        for s in range(step):
            n += p.n_z - 1 if self.order[s] == "z" else 1
        src = self.src.at[self.sl] if step == 0 else self.region(held)
        dst = self.region(held)
        for k in (range(1, p.n_z) if ax == "z" else (0,)):
            to = p.along_z(k) if ax == "z" else p.other(ax)
            d = pltpu.make_async_remote_copy(src_ref=src, dst_ref=dst, send_sem=ss.at[n], recv_sem=rs.at[n], device_id=to, device_id_type=MESH)
            d.start(); made.append(d); n += 1
        self.copies[step] = made
    def arrive(self, step):
        for d in self.copies[step]: d.wait_recv()
    def finish(self):
        for made in self.copies.values():
            for d in made: d.wait_send()

def n_sems(n_z): return n_z + 2

def number(plan):
    j, out = 0, []
    for stage in plan:
        new = []
        for piece in stage:
            new.append((j,) + piece); j += 1
        out.append(new)
    return out, j

ZYX, ZXY = ("z", "y", "x", "c"), ("z", "x", "y", "c")

SLOTS = 4


class Scatter:
    def __init__(self, place, out, rows, cols, order, piece, part, turn, sems, bufs):
        self.p, self.out, self.order, self.piece = place, out, order, piece
        self.rows, self.cols, self.width = pl.ds(*rows), pl.ds(*cols), cols[1]
        self.ss, self.rs, self.ls = sems
        self.part, self.b = part, bufs
        self.here = (turn % SLOTS) * 2 + part
        self.sent = {}

    def v(self, ref, *lead):
        return ref.at[lead + (slice(None), pl.ds(0, self.width))]

    def send(self, src, dst, to, n):
        n += self.piece * (self.p.n_z + 1)
        d = pltpu.make_async_remote_copy(src_ref=src, dst_ref=dst, send_sem=self.ss.at[n], recv_sem=self.rs.at[n], device_id=to, device_id_type=MESH)
        d.start()
        return d

    def add(self, count, dst, a, b):
        w = slice(0, self.width)

        def one(i, carry):
            (da, di), (aa, ai), (ba, bi) = dst(i), a(i), b(i)
            da[di + (slice(None), w)] = aa[ai + (slice(None), w)] + ba[bi + (slice(None), w)]
            return carry

        lax.fori_loop(0, count, one, 0)

    def free(self, step):
        for d in self.sent.pop(step, ()):
            d.wait_send() if step < 3 else d.wait()

    def step0(self, fill):
        p, b, A, h = self.p, self.b, slice(None), self.here
        fill(b.s0, h, self)
        ax = self.order[0]
        o = 1 - p.at[ax]
        if ax == "x":
            pair = self.v(b.s0, h, o, A, A), self.v(b.r1y, h // 2, A, A)
        else:
            pair = self.v(b.s0, h, A, A, o), self.v(b.r1x, h // 2, A, A)
        self.sent[0] = [self.send(*pair, p.other(ax), 0)]

    def step1(self):
        p, b, A, h, nz = self.p, self.b, slice(None), self.here, self.p.n_z
        for d in self.sent[0]:
            d.wait_recv()
        ax, nxt = self.order[0], self.order[1]
        m, o = p.at[ax], 1 - p.at[nxt]
        if ax == "x":
            at = lambda i: (i // 2, i % 2)
            self.add(2 * nz, lambda i: (b.s1y, (h // 2,) + at(i)), lambda i: (b.s0, (h, m) + at(i)), lambda i: (b.r1y, (h // 2,) + at(i)))
            src = self.v(b.s1y, h // 2, A, o)
        else:
            at = lambda i: (i // nz, i % nz)
            self.add(2 * nz, lambda i: (b.s1x, (h // 2,) + at(i)), lambda i: (b.s0, (h,) + at(i) + (m,)), lambda i: (b.r1x, (h // 2,) + at(i)))
            src = self.v(b.s1x, h // 2, o, A)
        self.sent[1] = [self.send(src, self.v(b.r2, h, A), p.other(nxt), 1)]

    def step2(self):
        p, b, h, nz = self.p, self.b, self.here, self.p.n_z
        for d in self.sent[1]:
            d.wait_recv()
        m = p.at[self.order[1]]
        mine = (lambda i: (b.s1y, (h // 2, i, m))) if self.order[0] == "x" else (lambda i: (b.s1x, (h // 2, m, i)))
        self.add(nz, lambda i: (b.s2, (h, i)), mine, lambda i: (b.r2, (h, i)))
        self.sent[2] = [
            self.send(self.v(b.s2, h, (p.at["z"] + k) % nz), self.v(b.r3, h, k - 1), p.along_z(k), 1 + k) for k in range(1, nz)
        ]

    def step3(self):
        p, b, h, nz, w = self.p, self.b, self.here, self.p.n_z, self.width
        for d in self.sent[2]:
            d.wait_recv()
        total = b.s2[h, p.at["z"], :, 0:w].astype(jnp.float32)
        for k in range(nz - 1):
            total = total + b.r3[h, k, :, 0:w].astype(jnp.float32)
        b.o[h, :, 0:w] = total
        b.sq[:, 0:w] += total * total
        d = pltpu.make_async_copy(self.v(b.o, h), self.out.at[self.rows, self.cols], self.ls.at[h])
        d.start()
        self.sent[3] = [d]


def sum_squares(place, n_z, bufs, sems, out):
    ns, nr = sems
    sq, part, zs = bufs.sq, bufs.n, bufs.nz
    acc = jnp.zeros((8, 128), jnp.float32)
    for i in range(sq.shape[0] // 8):
        for j in range(sq.shape[1] // 128):
            acc = acc + sq[i * 8 : (i + 1) * 8, j * 128 : (j + 1) * 128]
    for n, ax in enumerate("cxy"):
        part[2 * n] = acc
        d = pltpu.make_async_remote_copy(src_ref=part.at[2 * n], dst_ref=part.at[2 * n + 1], send_sem=ns.at[n], recv_sem=nr.at[n], device_id=place.other(ax), device_id_type=MESH)
        d.start()
        d.wait()
        acc = part[2 * n] + part[2 * n + 1]
    z = place.at["z"]
    zs[z] = acc
    made = []
    for k in range(1, n_z):
        d = pltpu.make_async_remote_copy(src_ref=zs.at[z], dst_ref=zs.at[z], send_sem=ns.at[2 + k], recv_sem=nr.at[2 + k], device_id=place.along_z(k), device_id_type=MESH)
        d.start()
        made.append(d)
    for d in made:
        d.wait()
    total = zs[0]
    for k in range(1, n_z):
        total = total + zs[k]
    out[...] = total


def backward_kernel(n_z, plan, names, *refs):
    b = types.SimpleNamespace(**dict(zip(names, refs)))
    ss, rs, ls, ns, nr, ws, ps, pr, lt_sem, rhs_sem, out_sem = refs[len(names) :]
    own_grads = (b.g_qkv, b.g_out, b.g_up, b.g_down, b.g_tiny)
    place = Place(n_z)
    greet(place)
    core, A = place.at["c"], slice(None)
    queries_n, model = b.q.shape
    key_rows = b.keys.shape[0]
    media_rows = key_rows - queries_n
    hidden_n = b.dpre.shape[1]
    head = model // HEADS
    windows, group_width = head_windows(head)
    scale = 1.0 / head**0.5
    f32, bf = jnp.float32, jnp.bfloat16
    b.sq[...] = jnp.zeros_like(b.sq)
    given = {}

    def give(src, dst):
        n = len(given)
        d = pltpu.make_async_remote_copy(src_ref=src, dst_ref=dst, send_sem=ps.at[n], recv_sem=pr.at[n], device_id=place.other("c"), device_id_type=MESH)
        d.start()
        given[id(dst)] = [d, False]

    def got(dst):
        held_copy = given[id(dst)]
        if not held_copy[1]:
            held_copy[0].wait_recv()
            held_copy[1] = True

    give(b.dpre, b.x_dpre)
    keys_in = pltpu.make_async_copy(b.keys, b.k, out_sem.at[1])
    keys_in.start()

    wbuf = b.wbuf

    def fetch(src, slot):
        d = pltpu.make_async_copy(src, wbuf.at[slot], ws.at[slot])
        d.start()
        return d

    def tiles_of(jobs, use):
        ahead = fetch(jobs[0], 0)
        for i in range(len(jobs)):
            now = ahead
            if i + 1 < len(jobs):
                ahead = fetch(jobs[i + 1], (i + 1) % 2)
            now.wait()
            use(i, wbuf[i % 2].reshape(384, model))

    def hidden_part(i):
        d = pltpu.make_async_copy(b.dpre.at[:, pl.ds(i * model, model)], b.dpart, ws.at[4])
        d.start()
        d.wait()

        def use(n, w):
            got_ = dot(b.dpart[...], w, ((1,), (1,)))
            cols = slice(n * 384, (n + 1) * 384)
            if i == 0:
                b.dmid[:, cols] = got_
            else:
                b.dmid[:, cols] += got_

        tiles_of([b.f_up.at[x, c, :, :, :, pl.ds(i * model, model)] for x in range(2) for c in range(2)], use)

    def norm_back(rows_in, grad, gain):
        centered = rows_in - jnp.mean(rows_in, axis=-1, keepdims=True)
        inv = lax.rsqrt(jnp.mean(centered * centered, axis=-1, keepdims=True) + norm_eps)
        hat = centered * inv
        scaled = grad * gain
        back = inv * (scaled - jnp.mean(scaled, axis=-1, keepdims=True) - hat * jnp.mean(scaled * hat, axis=-1, keepdims=True))
        return back, jnp.sum(grad * hat, axis=0, keepdims=True)

    def ffn_norm():
        d = pltpu.make_async_copy(b.f_tiny, b.tiny, ws.at[3])
        d.start()
        e = pltpu.make_async_copy(b.p_cot.at[core], b.dbranch, ws.at[4])
        e.start()
        d.wait()
        e.wait()
        b.tiny_t[...] = b.tiny[...].reshape(model, 128).astype(f32).T
        b.gsmall[...] = jnp.zeros_like(b.gsmall)

        def rows(i, carry):
            at = pl.ds(pl.multiple_of(i * 64, 64), 64)
            back, gain = norm_back(b.mid[at, :], b.dmid[at, :], b.tiny_t[10:11, :])
            total = b.dbranch[at, :].astype(f32) + back
            b.dmid[at, :] = total
            b.dbranch[at, :] = total.astype(bf)
            b.gsmall[10:11, :] += gain
            return carry

        lax.fori_loop(0, queries_n // 64, rows, 0)
        give(b.dbranch, b.x_branch)

    def attended_back():
        def use(n, w):
            b.datt[:, n * 384 : (n + 1) * 384] = dot(b.dbranch[...], w, ((1,), (1,))).astype(bf)

        tiles_of([b.f_out.at[x, c] for x in range(2) for c in range(2)], use)

    def attend_back(g):
        if g == 0:
            keys_in.wait()
        base = g * group_width
        n_tiles = group_width // 128
        last = {t: max(j for j, (t0, t1, _) in enumerate(windows) if t0 <= t < t1) for t in range(n_tiles)}
        sums = {}
        for j, (t0, t1, start) in enumerate(windows):
            cols = slice(base + t0 * 128, base + t1 * 128)
            q_in, k_in = lanes_of(queries_n, t1 - t0, start, head), lanes_of(key_rows, t1 - t0, start, head)
            qh = b.q[:, cols]
            qh = jnp.where(q_in, qh, jnp.zeros_like(qh))
            dah = b.datt[:, cols]
            dah = jnp.where(q_in, dah, jnp.zeros_like(dah))
            kw = b.k[:, cols]
            h = g * len(windows) + j
            p = jnp.exp(dot(kw, qh, ((1,), (1,))) * scale + b.bias[...] - b.lse[h : h + 1, :])
            dp = dot(b.v[:, cols], dah, ((1,), (1,)))
            row_dot = jnp.sum(p * dp, axis=0, keepdims=True)
            ds = (p * (dp - row_dot)).astype(bf)
            kh = jnp.where(k_in, kw, jnp.zeros_like(kw))
            parts = ((b.dv, dot(p.astype(bf), dah)), (b.dk, dot(ds, qh) * scale), (b.dq, dot(ds, kh, ((0,), (0,))) * scale))
            for n, (into, part) in enumerate(parts):
                for t in range(t0, t1):
                    new = part[:, (t - t0) * 128 : (t - t0 + 1) * 128]
                    sums[n, t] = sums[n, t] + new if (n, t) in sums else new
                    if last[t] == j:
                        into[:, base + t * 128 : base + (t + 1) * 128] = sums.pop((n, t)).astype(bf)
        if g == model // group_width - 1:
            give(b.dq, b.x_dq)
            give(b.dk, b.x_dk)
            give(b.dv, b.x_dv)

    def keys_back(n):
        x, c = n // 2, n % 2
        made = [fetch(b.f_qkv.at[x, c, :, :, :, pl.ds(i * model, model)], i) for i in range(3)]
        for d in made:
            d.wait()
        w = [wbuf[i].reshape(384, model) for i in range(3)]
        cols = slice(n * 384, (n + 1) * 384)
        lat_rows = slice(media_rows, key_rows)
        tail = dot(b.dq[...], w[0], ((1,), (1,))) + dot(b.dk[lat_rows, :], w[1], ((1,), (1,))) + dot(b.dv[lat_rows, :], w[2], ((1,), (1,)))
        b.k[lat_rows, cols] = tail.astype(bf)
        step = media_rows // 3
        for i in range(3):
            rows = slice(i * step, (i + 1) * step)
            b.k[rows, cols] = (dot(b.dk[rows, :], w[1], ((1,), (1,))) + dot(b.dv[rows, :], w[2], ((1,), (1,)))).astype(bf)

    def latents_back():
        def rows(i, carry):
            at = pl.ds(pl.multiple_of(i * 64, 64), 64)
            grad = b.k[pl.ds(pl.multiple_of(media_rows + i * 64, 16), 64), :].astype(f32)
            back, gain = norm_back(b.lat[at, :].astype(f32), grad, b.tiny_t[9:10, :])
            b.dmid[at, :] = b.dmid[at, :] + back
            b.gsmall[9:10, :] += gain
            return carry

        lax.fori_loop(0, queries_n // 64, rows, 0)
        d = pltpu.make_async_copy(b.dmid, b.d_lat, out_sem.at[0])
        d.start()
        late.append(d)

    late = []

    def media_back(part):
        step = media_rows // 3
        frames = step // 48
        d = pltpu.make_async_copy(b.media.at[pl.ds(part * step, step)], b.mrows, ws.at[3])
        d.start()
        d.wait()

        def frame(i, carry):
            at = pl.ds(pl.multiple_of(i * 48, 48), 48)
            whole = pl.ds(pl.multiple_of(part * step + i * 48, 48), 48)
            mixed = b.mrows[at, :].astype(f32) + dot(b.hot[whole, :], b.tiny_t[...].astype(bf))
            back, gain = norm_back(mixed, b.k[whole, :].astype(f32), b.tiny_t[8:9, :])
            b.gsmall[8:9, :] += gain
            b.gsmall[0:8, :] += b.hotc[part * frames + i][:, 0:1] * jnp.sum(back, axis=0, keepdims=True)
            return carry

        lax.fori_loop(0, frames, frame, 0)

    def small():
        b.gblocks[...] = b.gsmall[...].T.astype(bf).reshape(b.gblocks.shape)
        give(b.gblocks.at[:, 1 - core], b.x_tiny)

    held = [None]

    def left(src):
        if held[0] is src:
            return
        held[0] = src
        if src is b.p_keys:
            into = b.ltk
        elif src is b.p_act:
            into = b.lt
        else:
            into = b.lt.at[:, :, pl.ds(0, 2 * n_z)]
        d = pltpu.make_async_copy(src, into, lt_sem.at[0])
        d.start()
        d.wait()

    def right(own, sibling, cols, part):
        made = [pltpu.make_async_copy(r.at[:, pl.ds(*cols)], b.rhs.at[part, i], rhs_sem.at[part, i]) for i, r in enumerate((own, sibling))]
        for d in made:
            d.start()
        for d in made:
            d.wait()

    def blocks(x, k, group):
        if group == 1:
            return [b.lt[s, x, 0 : 2 * n_z].reshape(96 * n_z, queries_n) for s in (core, 1 - core)]
        return [jnp.concatenate([b.lt[s, x, i * group + k] for i in range(2 * n_z)], axis=0) for s in (core, 1 - core)]

    def filler(w, rows, cols):
        first, width = cols
        wide = pl.ds(first, width)

        def fill(dst, here, g):
            if w == 4:
                got(b.x_tiny)
                d = pltpu.make_async_copy(b.x_tiny, b.tiny2, ws.at[3])
                d.start()
                d.wait()

                def one(i, carry):
                    x, z, y = i // (2 * n_z), (i // 2) % n_z, i % 2
                    dst[here, x, z, y, :, 0:width] = b.gblocks[x, core, z, y] + b.tiny2[x, z, y]
                    return carry

                lax.fori_loop(0, 4 * n_z, one, 0)
                return
            keyed = w == 0 and first >= model
            if keyed:
                left(b.p_keys)
                mine, theirs = (b.dk, b.x_dk) if first < 2 * model else (b.dv, b.x_dv)
                got(theirs)
                at = pl.ds(first % model, width)
                d = pltpu.make_async_copy(theirs.at[:, at], b.rhsk.at[g.part], rhs_sem.at[g.part, 0])
                d.start()
                d.wait()
                r = [mine[:, at], b.rhsk[g.part]]
            elif w == 3:
                left(b.p_act)
                right(b.p_cot.at[core], b.p_cot.at[1 - core], cols, g.part)
            elif w == 2:
                left(b.p_hid)
                got(b.x_dpre)
                right(b.dpre, b.x_dpre, cols, g.part)
            else:
                mine, theirs, act = (b.dbranch, b.x_branch, b.p_att) if w == 1 else (b.dq, b.x_dq, b.p_lat)
                left(act)
                got(theirs)
                at = pl.ds(first % model, width)
                d = pltpu.make_async_copy(theirs.at[:, at], b.rhs.at[g.part, 1], rhs_sem.at[g.part, 1])
                d.start()
                d.wait()
            if w in (2, 3):
                r = [b.rhs[g.part, 0], b.rhs[g.part, 1]]
            elif not keyed:
                r = [mine[:, at], b.rhs[g.part, 1]]
            for x in range(2):
                if keyed:
                    l = [b.ltk[s, x].reshape(96 * n_z, key_rows) for s in (core, 1 - core)]
                else:
                    l = blocks(x, rows[0] // 48, 4 if w == 3 else 1)
                total = dot(l[0], r[0]) + dot(l[1], r[1])
                dst[here, x, :, :, :, 0:width] = total.astype(bf).reshape(n_z, 2, 48, width)

        return fill

    parts = 3
    work = [(3, 5, functools.partial(hidden_part, i)) for i in range(hidden_n // model)] + [(0, 3, ffn_norm), (0, 4, attended_back)]
    work += [(0, 9, functools.partial(attend_back, g)) for g in range(model // group_width)]
    work += [(0, 5, functools.partial(keys_back, n)) for n in range(4)] + [(0, 3, latents_back)]
    work += [(0, 4, functools.partial(media_back, i)) for i in range(parts)] + [(0, 2, small)]

    def run_until(dst):
        while id(dst) not in given:
            work.pop(0)[2]()

    stages = [
        [Scatter(place, own_grads[w], rows, cols, order, j, part, t, (ss, rs, ls), b) for part, (j, w, rows, cols, order) in enumerate(stage)]
        for t, stage in enumerate(plan)
    ]
    total = len(stages)
    for t in range(total + 3):
        for back in range(4):
            u = t - back
            if not 0 <= u < total:
                continue
            if u >= SLOTS:
                for g in stages[u - SLOTS]:
                    g.free(back)
            for g, (j, w, rows, cols, order) in zip(stages[u], plan[u]):
                if back == 0:
                    need = (b.x_dv, b.x_branch, b.x_dpre, b.x_dpre, b.x_tiny)[w]
                    run_until(need)
                    g.step0(filler(w, rows, cols))
                else:
                    (g.step1, g.step2, g.step3)[back - 1]()
        room = 9
        while work and room > 0:
            _, cost, piece = work.pop(0)
            room -= cost
            piece()
    for st in stages:
        for g in st:
            for k in range(4):
                g.free(k)
    for d, done in given.values():
        d.wait_send()
    for d in late:
        d.wait()
    sum_squares(place, n_z, b, (ns, nr), b.norm)


def backward_plan(shards, model, width):
    orders = (("x", "y", "z"), ("y", "x", "z"))
    pieces = [(3, (k, 48), (c, width)) for k in range(0, shards[3].shape[0], 48) for c in range(0, model, width)]
    pieces += [(2, (0, 48), (c, width)) for c in range(0, shards[2].shape[1], width)]
    pieces += [(1, (0, 48), (c, width)) for c in range(0, model, width)] + [(4, (0, 48), (0, 128))]
    pieces += [(0, (0, 48), (c, width)) for c in range(0, 3 * model, width)]
    return [[p + (orders[i],) for i, p in enumerate(pieces[n : n + 2])] for n in range(0, len(pieces), 2)]


def backward_all(full, made, lat, media, hot, hotc, bias, shards, n_z):
    width = 512
    queries_n, model = lat.shape
    media_rows = media.shape[0]
    key_rows = queries_n + media_rows
    hidden_n = shards[2].shape[1]
    plan, count = number(backward_plan(shards, model, width))
    q, k, v, dpre, mid, new, lse, p_keys, p_lat, p_att, p_hid, p_act, p_cot = made
    given = dict(f_qkv=full[0], f_out=full[1], f_up=full[2], f_tiny=full[4], dpre=dpre, p_keys=p_keys, p_lat=p_lat, p_att=p_att, p_hid=p_hid, p_act=p_act, p_cot=p_cot,
                 media=media, q=q, keys=k, v=v, mid=mid, lse=lse, lat=lat, hot=hot, hotc=hotc, bias=bias)
    bf, f32 = jnp.bfloat16, jnp.float32
    grads = [((s.shape[0], s.shape[1]), f32) for s in shards]
    outs = dict(g_qkv=grads[0], g_out=grads[1], g_up=grads[2], g_down=grads[3], g_tiny=grads[4], d_lat=((queries_n, model), f32), norm=((8, 128), f32),
                x_dpre=((queries_n, hidden_n), bf), x_branch=((queries_n, model), bf), x_dq=((queries_n, model), bf), x_dk=((key_rows, model), bf), x_dv=((key_rows, model), bf),
                x_tiny=((2, n_z, 2, 48, 128), bf))
    W, S = width, SLOTS
    vm = dict(s0=((2 * S, 2, n_z, 2, 48, W), bf), r1x=((S, 2, n_z, 48, W), bf), r1y=((S, n_z, 2, 48, W), bf), s1x=((S, 2, n_z, 48, W), bf), s1y=((S, n_z, 2, 48, W), bf),
          r2=((2 * S, n_z, 48, W), bf), s2=((2 * S, n_z, 48, W), bf), r3=((2 * S, n_z - 1, 48, W), bf), o=((2 * S, 48, W), f32),
          sq=((48, W), f32), n=((6, 8, 128), f32), nz=((n_z, 8, 128), f32),
          wbuf=((3, n_z, 2, 48, model), bf), dpart=((queries_n, model), bf), dmid=((queries_n, model), f32), dbranch=((queries_n, model), bf), datt=((queries_n, model), bf),
          dq=((queries_n, model), bf), k=((key_rows, model), bf), dk=((key_rows, model), bf), dv=((key_rows, model), bf), tiny=((2, 2, n_z, 2, 48, 128), bf), tiny_t=((128, model), f32),
          gsmall=((128, model), f32), gblocks=((2, 2, n_z, 2, 48, 128), bf), tiny2=((2, n_z, 2, 48, 128), bf), mrows=((media_rows // 3, model), bf),
          lt=(p_act.shape, bf), ltk=(p_keys.shape, bf), rhs=((2, 2, queries_n, W), bf), rhsk=((2, key_rows, W), bf))
    sem = pltpu.SemaphoreType.DMA
    in_vmem, in_any = pl.BlockSpec(memory_space=pltpu.VMEM), pl.BlockSpec(memory_space=ANY)
    resident = tuple(id(a) for a in (q, v, mid, lse, lat, hot, hotc, bias))
    n_copies = count * (n_z + 1)
    res = pl.pallas_call(
        functools.partial(backward_kernel, n_z, plan, (*given, *outs, *vm)),
        out_shape=[jax.ShapeDtypeStruct(*o) for o in outs.values()],
        in_specs=[in_vmem if id(a) in resident else in_any for a in given.values()],
        out_specs=[in_vmem if o is outs["norm"] else in_any for o in outs.values()],
        scratch_shapes=[pltpu.VMEM(*m) for m in vm.values()] + [sem((n_copies,)), sem((n_copies,)), sem((2 * S,)), sem((n_z + 2,)), sem((n_z + 2,)), sem((5,)), sem((8,)), sem((8,)), sem((1,)), sem((2, 2)), sem((2,))],
        name="backward_and_scatter",
        compiler_params=pltpu.CompilerParams(collective_id=1, has_side_effects=True, vmem_limit_bytes=62 * 2**20),
    )(*given.values())
    return types.SimpleNamespace(**dict(zip(outs, res)))


def out_copies(pairs, sems, at, running):
    for src, dst in pairs:
        d = pltpu.make_async_copy(src, dst, sems.at[len(running)])
        d.start()
        running.append(d)


def dot(a, b, contract=((1,), (0,))):
    return lax.dot_general(a, b, (contract, ((), ())), preferred_element_type=jnp.float32)


def head_windows(head):
    group = 128 // math.gcd(head, 128)
    out = []
    for j in range(group):
        first, last = j * head // 128, ((j + 1) * head - 1) // 128
        out.append((first, last + 1, j * head - first * 128))
    return out, group * head


def lanes_of(rows, tiles, start, head):
    lane = lax.broadcasted_iota(jnp.int32, (rows, tiles * 128), 1)
    return (lane >= start) & (lane < start + head)


def normed(rows_in, gain):
    centered = rows_in - jnp.mean(rows_in, axis=-1, keepdims=True)
    var_row = jnp.mean(centered * centered, axis=-1, keepdims=True)
    return centered * lax.rsqrt(var_row + norm_eps) * gain


def forward_kernel(n_z, plan, needs, *refs):
    (sh, (lat, media, cot, hot, bias), full, outs, scratch) = refs[:5], refs[5:10], refs[10:15], refs[15:27], refs[27:]
    o_q, o_k, o_v, o_dpre, o_mid, o_new, o_lse, p_keys, p_lat, p_att, p_hid, p_act = outs[:12]
    p_cot, *scratch = scratch
    keys, q, k, v, att, hid, act, slope, dact, mid, new, tiny, tiny_t, lse, wbuf, wdown, flip, flip_keys, ss, rs, ls, os_, ws, ps, pr, pl_ = scratch
    f_qkv, f_out, f_up, f_down, f_tiny = full
    place = Place(n_z)
    greet(place)
    queries_n, model = lat.shape
    media_rows = media.shape[0]
    key_rows = media_rows + queries_n
    hidden_n = act.shape[1]
    head = model // HEADS
    windows, group_width = head_windows(head)
    scale = 1.0 / head**0.5
    written = []
    given = []
    core = place.at["c"]

    def give(src, dst, theirs):
        n = len(given)
        if theirs:
            d = pltpu.make_async_remote_copy(src_ref=src, dst_ref=dst, send_sem=ps.at[n], recv_sem=pr.at[n], device_id=place.other("c"), device_id_type=MESH)
        else:
            d = pltpu.make_async_copy(src, dst, pl_.at[n])
        d.start()
        given.append([d, theirs, False])
        return n

    def gone(n):
        d, theirs, done = given[n]
        if not done:
            d.wait_send() if theirs else d.wait()
            given[n][2] = True

    def turn(a, dst, slot, x, wide, before=()):
        made = []
        for n in before:
            gone(n)
        for theirs in (False, True):
            who = 1 - core if theirs else core
            for m in range(wide // 384):
                cols = pl.ds(pl.multiple_of((x * 2 + who) * wide + m * 384, 128), 384)
                flip[slot] = a[:, cols].T.reshape(8, 48, queries_n)
                made.append(give(flip.at[slot], dst.at[core, x, pl.ds(m * 8, 8)], theirs))
                slot += 1
        return made

    def load(src, dst):
        d = pltpu.make_async_copy(src, dst, ws.at[0])
        d.start()
        d.wait()

    def write(*pairs):
        out_copies(pairs, os_, 0, written)

    def norms():
        load(f_tiny, tiny)
        tiny_t[...] = tiny[...].reshape(model, 128).astype(jnp.float32).T
        give(cot, p_cot.at[core], False)
        give(cot, p_cot.at[core], True)
        hid[...] = normed(lat[...].astype(jnp.float32), tiny_t[9:10, :]).astype(jnp.bfloat16)
        keys[media_rows:key_rows, :] = hid[...]
        for x in range(2):
            turn(hid, p_lat, 2 * x, x, 384)

        def frame(i, carry):
            rows = pl.ds(pl.multiple_of(i * 48, 48), 48)
            mixed = media[rows, :].astype(jnp.float32) + dot(hot[rows, :], tiny_t[...].astype(jnp.bfloat16))
            keys[rows, :] = normed(mixed, tiny_t[8:9, :]).astype(jnp.bfloat16)
            return carry

        lax.fori_loop(0, media_rows // 48, frame, 0)

    key_turns = []

    def turn_keys(x):
        for n in key_turns:
            gone(n)
        for theirs in (False, True):
            who = 1 - core if theirs else core
            cols = pl.ds(pl.multiple_of((x * 2 + who) * 384, 128), 384)
            flip_keys[int(theirs)] = keys[:, cols].T.reshape(8, 48, key_rows)
            key_turns.append(give(flip_keys.at[int(theirs)], p_keys.at[core, x], theirs))

    def project(i, dst, first):
        load(f_qkv.at[:, :, :, :, :, pl.ds(i * model, model)], wbuf)

        def tile(n, carry):
            cols = pl.ds(pl.multiple_of(n * 256, 256), 256)
            w = wbuf[:, :, :, :, :, cols].reshape(model, 256)
            dst[:, cols] = dot(keys[first:key_rows, :], w).astype(jnp.bfloat16)
            return carry

        lax.fori_loop(0, model // 256, tile, 0)

    def project_q():
        project(0, q, media_rows)
        write((q, o_q))

    def project_k():
        project(1, k, 0)
        write((k, o_k))

    def project_v():
        project(2, v, 0)
        write((v, o_v))

    def attend(g):
        base = g * group_width
        tiles = [jnp.zeros((queries_n, 128), jnp.float32) for _ in range(group_width // 128)]
        for j, (t0, t1, start) in enumerate(windows):
            cols = slice(base + t0 * 128, base + t1 * 128)
            qh = q[:, cols]
            qh = jnp.where(lanes_of(queries_n, t1 - t0, start, head), qh, jnp.zeros_like(qh))
            s = dot(k[:, cols], qh, ((1,), (1,))) * scale + bias[...]
            top = jnp.max(s, axis=0, keepdims=True)
            e = jnp.exp(s - top)
            total = jnp.sum(e, axis=0, keepdims=True)
            p = (e * (1.0 / total)).astype(jnp.bfloat16)
            lse[g * len(windows) + j : g * len(windows) + j + 1, :] = top + jnp.log(total)
            vh = v[:, cols]
            vh = jnp.where(lanes_of(key_rows, t1 - t0, start, head), vh, jnp.zeros_like(vh))
            got = dot(p, vh, ((0,), (0,)))
            for t in range(t0, t1):
                tiles[t] = tiles[t] + got[:, (t - t0) * 128 : (t - t0 + 1) * 128]
        for t, tile in enumerate(tiles):
            att[:, base + t * 128 : base + (t + 1) * 128] = tile.astype(jnp.bfloat16)

    def project_out():
        write((lse, o_lse))
        for x in range(2):
            turn(att, p_att, 4 + 2 * x, x, 384)
        load(f_out, wbuf)

        def tile(n, carry):
            cols = pl.ds(pl.multiple_of(n * 256, 256), 256)
            w = wbuf[:, :, :, :, :, cols].reshape(model, 256)
            mid[:, cols] = lat[:, cols].astype(jnp.float32) + dot(att[...], w)
            return carry

        lax.fori_loop(0, model // 256, tile, 0)
        hid[...] = normed(mid[...], tiny_t[10:11, :]).astype(jnp.bfloat16)
        write((mid, o_mid))
        for x in range(2):
            hid_turns.extend(turn(hid, p_hid, 8 + 2 * x, x, 384))

    hid_turns = []
    act_turns = []

    def up(i):
        load(f_up.at[:, :, :, :, :, pl.ds(i * model, model)], wbuf)

        def tile(n, carry):
            cols = pl.ds(pl.multiple_of(n * 256, 256), 256)
            into = pl.ds(pl.multiple_of(i * model + n * 256, 256), 256)
            w = wbuf[:, :, :, :, :, cols].reshape(model, 256)
            x = dot(hid[...], w)
            cdf = 0.5 + 0.5 * lax.erf(x * 0.7071067811865476)
            act[:, into] = (x * cdf).astype(jnp.bfloat16)
            slope[:, into] = cdf + x * (jnp.exp(-0.5 * x * x) * 0.3989422804014327)
            return carry

        lax.fori_loop(0, model // 256, tile, 0)
        if i % 2 == 1:
            before = list(range(len(given))) if i == 1 else act_turns
            act_turns.extend(turn(act, p_act, 0, i // 2, model, before))

    def down(i, width):
        cols = slice(i * width, (i + 1) * width)
        load(f_down.at[:, :, :, :, :, pl.ds(i * width, width)], wdown)
        per = hidden_n // 4
        got = jnp.zeros((queries_n, width), jnp.float32)
        for b in range(4):
            w = wdown[b // 2, b % 2].reshape(per, width)
            got = got + dot(act[:, b * per : (b + 1) * per], w)
            back = dot(cot[:, cols], w, ((1,), (1,)))
            if i == 0:
                dact[:, b * per : (b + 1) * per] = back
            else:
                dact[:, b * per : (b + 1) * per] += back
        new[:, cols] = (mid[:, cols] + got).astype(jnp.bfloat16)

    def finish():
        def tile(n, carry):
            cols = pl.ds(pl.multiple_of(n * 512, 512), 512)
            act[:, cols] = (dact[:, cols] * slope[:, cols]).astype(jnp.bfloat16)
            return carry

        lax.fori_loop(0, hidden_n // 512, tile, 0)
        write((act, o_dpre), (new, o_new))
        for d in written:
            d.wait()
        for n, (d, theirs, done) in enumerate(given):
            gone(n)
            if theirs:
                d.wait_recv()

    work = [(needs["tiny"], 8, norms), (needs["q"], 4, project_q), (needs["k"], 8, project_k), (needs["v"], 8, project_v)]
    work[2:2] = [(needs["q"], 3, functools.partial(turn_keys, x)) for x in range(2)]
    work += [(needs["v"], 7, functools.partial(attend, g)) for g in range(model // group_width)]
    work += [(needs["out"], 5, project_out)]
    work += [(s, 6, functools.partial(up, i)) for i, s in enumerate(needs["up"])]
    work += [(s, 5, functools.partial(down, i, model // len(needs["down"]))) for i, s in enumerate(needs["down"])]
    work += [(needs["down"][-1], 5, finish)]
    locals_ = []
    for i in range(5):
        d = pltpu.make_async_copy(sh[i], full[i].at[block_index(place, ())], ls.at[i])
        d.start()
        locals_.append(d)
    stages = [[Gather(place, sh[w], full[w], rows, cols, order, (ss, rs), j * n_sems(n_z)) for (j, w, rows, cols, order) in stage] for stage in plan]
    waited = set()
    total, steps = len(stages), 4
    for t in range(total + steps):
        for back in range(steps + 1):
            u = t - back
            if not 0 <= u < total:
                continue
            for g, (j, w, *_) in zip(stages[u], plan[u]):
                if back == 1 and w not in waited:
                    locals_[w].wait()
                    waited.add(w)
                if back > 0:
                    g.arrive(back - 1)
                if back < steps:
                    g.start(back)
        room = 14
        while work and work[0][0] <= t - steps and (room > 0 or t == total + steps - 1):
            need, cost, piece = work.pop(0)
            room -= cost
            piece()
    for st in stages:
        for g in st:
            g.finish()


def forward_plan(shards, model):
    two = lambda w, rows, first, width: [(w, (0, rows), (first, width), ZYX), (w, (0, rows), (first + width, width), ZXY)]
    rows, half = shards[1].shape[0], model // 2
    stages, needs = [[(4, (0, rows), (0, 128), ZYX)]], {"tiny": 0}
    for i, name in enumerate("qkv"):
        needs[name] = len(stages)
        stages.append(two(0, rows, i * model, half))
    needs["out"] = len(stages)
    stages.append(two(1, rows, 0, half))
    needs["up"], needs["down"] = [], []
    for i in range(shards[2].shape[1] // model):
        needs["up"].append(len(stages))
        stages.append(two(2, rows, i * model, half))
    for i in range(model // 256):
        needs["down"].append(len(stages))
        stages.append(two(3, shards[3].shape[0], i * 256, 128))
    return stages, needs


def forward_all(shards, lat, media, cot, hot, bias, n_z):
    model, hidden_n = lat.shape[1], shards[2].shape[1]
    stages, needs = forward_plan(shards, model)
    plan, count = number(stages)
    queries_n, media_rows = lat.shape[0], media.shape[0]
    key_rows = queries_n + media_rows
    bf, f32 = jnp.bfloat16, jnp.float32
    rows = shards[1].shape[0]
    part = (2, 2, 2 * n_z, 48)
    made = [((queries_n, model), bf), ((key_rows, model), bf), ((key_rows, model), bf), ((queries_n, hidden_n), bf), ((queries_n, model), f32), ((queries_n, model), bf), ((HEADS, queries_n), f32),
            (part + (key_rows,), bf), (part + (queries_n,), bf), (part + (queries_n,), bf), (part + (queries_n,), bf), ((2, 2, 2 * n_z * hidden_n // model, 48, queries_n), bf), ((2, queries_n, model), bf)]
    vm = [((key_rows, model), bf), ((queries_n, model), bf), ((key_rows, model), bf), ((key_rows, model), bf), ((queries_n, model), bf), ((queries_n, model), bf), ((queries_n, hidden_n), bf),
          ((queries_n, hidden_n), f32), ((queries_n, hidden_n), f32), ((queries_n, model), f32), ((queries_n, model), bf),
                     ((2, 2, n_z, 2, rows, 128), bf), ((128, model), f32), ((HEADS, queries_n), f32), ((2, 2, n_z, 2, rows, model), bf), ((2, 2, n_z, 2, shards[3].shape[0], 256), bf),
                     ((12, 8, 48, queries_n), bf), ((2, 8, 48, key_rows), bf)]
    sem = pltpu.SemaphoreType.DMA
    in_vmem, in_any = pl.BlockSpec(memory_space=pltpu.VMEM), pl.BlockSpec(memory_space=ANY)
    out = pl.pallas_call(
        functools.partial(forward_kernel, n_z, plan, needs),
        out_shape=[jax.ShapeDtypeStruct((2, 2, n_z, 2) + s.shape, s.dtype) for s in shards] + [jax.ShapeDtypeStruct(*m) for m in made],
        in_specs=[in_vmem] * 10,
        out_specs=[in_any] * (5 + len(made)),
        scratch_shapes=[pltpu.VMEM(*m) for m in vm] + [sem((count * n_sems(n_z),)), sem((count * n_sems(n_z),)), sem((5,)), sem((16,)), sem((1,)), sem((48,)), sem((48,)), sem((48,))],
        name="gather_and_forward",
        compiler_params=pltpu.CompilerParams(collective_id=0, has_side_effects=True, vmem_limit_bytes=60 * 2**20),
    )(*shards, lat, media, cot, hot, bias)
    return out[:5], out[5:]


def layer_norm(values_in, gain):
    mean_row = jnp.mean(values_in, axis=-1, keepdims=True)
    centered = values_in - mean_row
    var_row = jnp.mean(centered * centered, axis=-1, keepdims=True)
    return centered * lax.rsqrt(var_row + norm_eps) * gain


def exact_gelu(values_in):
    return jax.nn.gelu(values_in, approximate=False)


def frame_tables(counts, frame_slots, time_len):
    slot_total = counts.shape[0]
    order = jnp.arange(slot_total, dtype=jnp.int32)
    slot_ends = jnp.sum(jnp.where(order[None, :] <= order[:, None], counts[None, :], 0), axis=1)
    slot_starts = slot_ends - counts
    frame_ids = jnp.arange(frame_slots, dtype=jnp.int32)
    frame_owner = jnp.sum((frame_ids[:, None] >= slot_ends[None, :]).astype(jnp.int32), axis=1)
    slot_ids = jnp.arange(slot_total, dtype=jnp.int32)
    start_of = jnp.sum(
        jnp.where(frame_owner[:, None] == slot_ids[None, :], slot_starts[None, :], 0), axis=1
    )
    time_index = frame_ids - start_of
    live_frame = frame_owner < slot_total
    time_ids = jnp.arange(time_len, dtype=jnp.int32)
    time_hot = ((time_index[:, None] == time_ids[None, :]) & live_frame[:, None]).astype(
        jnp.float32
    )
    return (frame_owner, time_hot)


def gather_params(part_qkv, part_out, part_up, part_down, part_time, part_gains):
    inner_part = (
        lax.all_gather(part_qkv, FSDP, axis=0, tiled=True),
        lax.all_gather(part_out, FSDP, axis=0, tiled=True),
        lax.all_gather(part_up, FSDP, axis=0, tiled=True),
        lax.all_gather(part_down, FSDP, axis=0, tiled=True),
        lax.all_gather(part_time, FSDP, axis=0, tiled=True),
        lax.all_gather(part_gains, FSDP, axis=0, tiled=True),
    )
    return (
        lax.all_gather(inner_part[0], DP, axis=0, tiled=True),
        lax.all_gather(inner_part[1], DP, axis=0, tiled=True),
        lax.all_gather(inner_part[2], DP, axis=0, tiled=True),
        lax.all_gather(inner_part[3], DP, axis=0, tiled=True),
        lax.all_gather(inner_part[4], DP, axis=0, tiled=True),
        lax.all_gather(inner_part[5], DP, axis=0, tiled=True),
    )


def reduce_grads(grad_qkv, grad_out, grad_up, grad_down, grad_time, grad_gains):
    outer_part = (
        lax.psum_scatter(
            grad_qkv.astype(jnp.bfloat16), DP, scatter_dimension=0, tiled=True
        ).astype(jnp.float32),
        lax.psum_scatter(
            grad_out.astype(jnp.bfloat16), DP, scatter_dimension=0, tiled=True
        ).astype(jnp.float32),
        lax.psum_scatter(
            grad_up.astype(jnp.bfloat16), DP, scatter_dimension=0, tiled=True
        ).astype(jnp.float32),
        lax.psum_scatter(
            grad_down.astype(jnp.bfloat16), DP, scatter_dimension=0, tiled=True
        ).astype(jnp.float32),
        lax.psum_scatter(
            grad_time.astype(jnp.bfloat16), DP, scatter_dimension=0, tiled=True
        ).astype(jnp.float32),
        lax.psum_scatter(
            grad_gains.astype(jnp.bfloat16), DP, scatter_dimension=0, tiled=True
        ).astype(jnp.float32),
    )
    return (
        lax.psum_scatter(
            outer_part[0].astype(jnp.bfloat16), FSDP, scatter_dimension=0, tiled=True
        ).astype(jnp.float32),
        lax.psum_scatter(
            outer_part[1].astype(jnp.bfloat16), FSDP, scatter_dimension=0, tiled=True
        ).astype(jnp.float32),
        lax.psum_scatter(
            outer_part[2].astype(jnp.bfloat16), FSDP, scatter_dimension=0, tiled=True
        ).astype(jnp.float32),
        lax.psum_scatter(
            outer_part[3].astype(jnp.bfloat16), FSDP, scatter_dimension=0, tiled=True
        ).astype(jnp.float32),
        lax.psum_scatter(
            outer_part[4].astype(jnp.bfloat16), FSDP, scatter_dimension=0, tiled=True
        ).astype(jnp.float32),
        lax.psum_scatter(
            outer_part[5].astype(jnp.bfloat16), FSDP, scatter_dimension=0, tiled=True
        ).astype(jnp.float32),
    )


def masked_scores(q_heads, k_heads, allowed, score_scale):
    scores = (
        jnp.einsum("qhe,khe->hqk", q_heads, k_heads, preferred_element_type=jnp.float32)
        * score_scale
    )
    return jnp.where(allowed[None, :, :], scores, -1e30)


def adamw_step(weight, first, second, grad, factor, rate):
    clipped = grad * factor
    first_new = beta_one * first + (1.0 - beta_one) * clipped
    second_new = beta_two * second + (1.0 - beta_two) * clipped * clipped
    first_hat = first_new / (1.0 - beta_one**STEP)
    second_hat = second_new / (1.0 - beta_two**STEP)
    weight_new = weight - rate * (
        first_hat / (jnp.sqrt(second_hat) + adam_eps) + decay_rate * weight
    )
    return (weight_new, first_new, second_new)


def on_device(
    latents,
    media,
    frame_counts,
    cotangent,
    w_qkv,
    m_qkv,
    v_qkv,
    w_out,
    m_out,
    v_out,
    w_up,
    m_up,
    v_up,
    w_down,
    m_down,
    v_down,
    time_table,
    m_time,
    v_time,
    gains,
    m_gains,
    v_gains,
):
    low_qkv = w_qkv.astype(jnp.bfloat16)
    low_out = w_out.astype(jnp.bfloat16)
    low_up = w_up.astype(jnp.bfloat16)
    low_down = w_down.astype(jnp.bfloat16)
    low_time = time_table.astype(jnp.bfloat16)
    low_gains = gains.astype(jnp.bfloat16)
    n_dp, n_fsdp = lax.axis_size(DP), lax.axis_size(FSDP)
    own_rows = w_qkv.shape[0]
    item_slots, lat_count, model_width = latents.shape
    frame_slots, patch_rows, _ = media.shape
    queries_n, media_rows = item_slots * lat_count, frame_slots * patch_rows
    frame_owner, time_hot = frame_tables(frame_counts, frame_slots, time_table.shape[1])
    query_owner = jnp.arange(queries_n, dtype=jnp.int32) // lat_count
    key_owner = jnp.concatenate([jnp.repeat(frame_owner, patch_rows), query_owner], axis=0)
    allowed = query_owner[:, None] == key_owner[None, :]
    lows = (low_qkv, low_out, low_up, low_down, low_time, low_gains)
    if fits_kernels(n_dp, n_fsdp, w_qkv, w_up, w_down, queries_n, frame_slots, patch_rows):
        new_latents, d_latents, grad_norm, reduced = by_kernels(lows, latents, media, cotangent, time_hot, allowed, n_fsdp // 2)
    else:
        new_latents, d_latents, grad_norm, reduced = by_collectives(lows, latents, media, cotangent, time_hot, allowed)
    factor = jnp.minimum(1.0, clip_limit / (grad_norm + 1e-06))
    masters = (w_qkv, w_out, w_up, w_down, time_table, gains)
    firsts = (m_qkv, m_out, m_up, m_down, m_time, m_gains)
    seconds = (v_qkv, v_out, v_up, v_down, v_time, v_gains)
    rates = (0.02, 0.1, 0.02, 0.01, 0.2, 0.5)
    updated = []
    for index in range(6):
        updated.extend(adamw_step(masters[index], firsts[index], seconds[index], reduced[index], factor, rates[index]))
    return (new_latents, d_latents, grad_norm, *updated)


def fits_kernels(n_dp, n_fsdp, w_qkv, w_up, w_down, queries_n, frame_slots, patch_rows):
    rows, _, model = w_qkv.shape
    return (
        n_dp == 4 and n_fsdp == 8 and rows == 48 and model == 1536 and w_up.shape[1] == 4 * model and w_down.shape[0] == 192
        and queries_n == 256 and patch_rows == 48 and frame_slots % 3 == 0
    )


def by_kernels(lows, latents, media, cotangent, time_hot, allowed, n_z):
    low_qkv, low_out, low_up, low_down, low_time, low_gains = lows
    own_rows, _, model = low_qkv.shape
    time_len = low_time.shape[1]
    queries_n = allowed.shape[0]
    frame_slots, patch_rows, _ = media.shape
    tiny = jnp.concatenate([low_time, low_gains], axis=1)
    shards = [low_qkv.reshape(own_rows, -1), low_out, low_up, low_down, jnp.pad(tiny, ((0, 0), (0, 128 - tiny.shape[1])))]
    hot = jnp.pad(jnp.repeat(time_hot, patch_rows, axis=0), ((0, 0), (0, 128 - time_len))).astype(jnp.bfloat16)
    hotc = jnp.broadcast_to(time_hot[:, :, None], time_hot.shape + (128,))
    bias = jnp.where(allowed.T, 0.0, -1e30).astype(jnp.float32)
    lat = latents.reshape(queries_n, model)
    med = media.reshape(frame_slots * patch_rows, model)
    full, made = forward_all(shards, lat, med, cotangent.reshape(queries_n, model), hot, bias, n_z)
    own = backward_all(full, made, lat, med, hot, hotc, bias, shards, n_z)
    small = own.g_tiny
    reduced = (
        own.g_qkv.reshape(low_qkv.shape), own.g_out, own.g_up, own.g_down, small[:, :time_len], small[:, time_len : time_len + 3]
    )
    return made[5].reshape(latents.shape), own.d_lat.reshape(latents.shape), jnp.sqrt(jnp.sum(own.norm)), reduced


def by_collectives(lows, latents, media, cotangent, time_hot, allowed):
    full_qkv, full_out, full_up, full_down, full_time, full_gains = gather_params(*lows)
    item_slots, lat_count, model_width = latents.shape
    frame_slots, patch_rows, unused_width = media.shape
    queries_n = item_slots * lat_count
    media_rows = frame_slots * patch_rows
    head_size = model_width // HEADS
    score_scale = 1.0 / head_size**0.5
    time_f32 = full_time.astype(jnp.float32)
    gains_f32 = full_gains.astype(jnp.float32)
    frame_time = jnp.dot(time_hot, time_f32.T, precision=highest)
    mixed = media.astype(jnp.float32) + frame_time[:, None, :]
    media_norm, media_back = jax.vjp(layer_norm, mixed, gains_f32[:, 0])
    media_low = media_norm.astype(jnp.bfloat16).reshape(media_rows, model_width)
    lat_rows = latents.reshape(queries_n, model_width).astype(jnp.float32)
    lat_norm, lat_back = jax.vjp(layer_norm, lat_rows, gains_f32[:, 1])
    lat_low = lat_norm.astype(jnp.bfloat16)
    keys_in = jnp.concatenate([media_low, lat_low], axis=0)
    key_rows = keys_in.shape[0]
    qkv_flat = full_qkv.reshape(model_width, 3 * model_width)
    queries = jnp.dot(
        lat_low, qkv_flat[:, :model_width], preferred_element_type=jnp.float32
    ).astype(jnp.bfloat16)
    key_value = jnp.dot(
        keys_in, qkv_flat[:, model_width:], preferred_element_type=jnp.float32
    ).astype(jnp.bfloat16)
    q_heads = queries.reshape(queries_n, HEADS, head_size)
    k_heads = key_value[:, :model_width].reshape(key_rows, HEADS, head_size)
    v_heads = key_value[:, model_width:].reshape(key_rows, HEADS, head_size)
    scores = masked_scores(q_heads, k_heads, allowed, score_scale)
    row_top = jnp.max(scores, axis=-1, keepdims=True)
    row_total = jnp.sum(jnp.exp(scores - row_top), axis=-1, keepdims=True)
    log_total = row_top + jnp.log(row_total)
    probs_low = jnp.exp(scores - log_total).astype(jnp.bfloat16)
    attended = jnp.einsum("hqk,khe->qhe", probs_low, v_heads, preferred_element_type=jnp.float32)
    attended = attended.reshape(queries_n, model_width).astype(jnp.bfloat16)
    middle = lat_rows + jnp.dot(attended, full_out, preferred_element_type=jnp.float32)
    hidden, ffn_back = jax.vjp(layer_norm, middle, gains_f32[:, 2])
    hidden_low = hidden.astype(jnp.bfloat16)
    pre_act = jnp.dot(hidden_low, full_up, preferred_element_type=jnp.float32)
    activated, gelu_back = jax.vjp(exact_gelu, pre_act)
    act_low = activated.astype(jnp.bfloat16)
    result = middle + jnp.dot(act_low, full_down, preferred_element_type=jnp.float32)
    new_latents = result.astype(jnp.bfloat16).reshape(item_slots, lat_count, model_width)
    d_result = cotangent.reshape(queries_n, model_width)
    g_down = jnp.einsum("qf,qd->fd", act_low, d_result, preferred_element_type=jnp.float32)
    d_act = jnp.einsum("qd,fd->qf", d_result, full_down, preferred_element_type=jnp.float32)
    d_pre = gelu_back(d_act)[0].astype(jnp.bfloat16)
    g_up = jnp.einsum("qd,qf->df", hidden_low, d_pre, preferred_element_type=jnp.float32)
    d_hidden = jnp.einsum("qf,df->qd", d_pre, full_up, preferred_element_type=jnp.float32)
    d_middle_ln, g_gain_ffn = ffn_back(d_hidden)
    d_middle = d_result.astype(jnp.float32) + d_middle_ln
    d_branch = d_middle.astype(jnp.bfloat16)
    g_out = jnp.einsum("qe,qd->ed", attended, d_branch, preferred_element_type=jnp.float32)
    d_attended = jnp.einsum(
        "qd,ed->qe", d_branch, full_out, preferred_element_type=jnp.float32
    ).astype(jnp.bfloat16)
    scores_again = masked_scores(q_heads, k_heads, allowed, score_scale)
    probs = jnp.exp(scores_again - log_total)
    probs_again = probs.astype(jnp.bfloat16)
    d_att_heads = d_attended.reshape(queries_n, HEADS, head_size)
    d_probs = jnp.einsum("qhe,khe->hqk", d_att_heads, v_heads, preferred_element_type=jnp.float32)
    row_dot = jnp.sum(probs * d_probs, axis=-1, keepdims=True)
    d_scores = (probs * (d_probs - row_dot)).astype(jnp.bfloat16)
    d_queries = (
        (
            jnp.einsum("hqk,khe->qhe", d_scores, k_heads, preferred_element_type=jnp.float32)
            * score_scale
        )
        .reshape(queries_n, model_width)
        .astype(jnp.bfloat16)
    )
    d_keys = (
        (
            jnp.einsum("hqk,qhe->khe", d_scores, q_heads, preferred_element_type=jnp.float32)
            * score_scale
        )
        .reshape(key_rows, model_width)
        .astype(jnp.bfloat16)
    )
    d_values = (
        jnp.einsum("hqk,qhe->khe", probs_again, d_att_heads, preferred_element_type=jnp.float32)
        .reshape(key_rows, model_width)
        .astype(jnp.bfloat16)
    )
    g_query = jnp.einsum("qd,qe->de", lat_low, d_queries, preferred_element_type=jnp.float32)
    d_key_value = jnp.concatenate([d_keys, d_values], axis=1)
    g_key_value = jnp.einsum("kd,kx->dx", keys_in, d_key_value, preferred_element_type=jnp.float32)
    g_qkv = jnp.concatenate([g_query, g_key_value], axis=1).reshape(model_width, 3, model_width)
    back_flat = full_qkv.reshape(model_width, 3 * model_width)
    d_keys_in = jnp.einsum(
        "kx,dx->kd", d_key_value, back_flat[:, model_width:], preferred_element_type=jnp.float32
    )
    d_lat_norm = (
        jnp.einsum(
            "qe,de->qd", d_queries, back_flat[:, :model_width], preferred_element_type=jnp.float32
        )
        + d_keys_in[media_rows:]
    )
    d_lat_ln, g_gain_lat = lat_back(d_lat_norm)
    d_latents = (d_middle + d_lat_ln).reshape(item_slots, lat_count, model_width)
    d_mixed, g_gain_media = media_back(
        d_keys_in[:media_rows].reshape(frame_slots, patch_rows, model_width)
    )
    frame_grad = jnp.sum(d_mixed, axis=1)
    g_time = jnp.einsum("fd,ft->dt", frame_grad, time_hot, precision=highest)
    g_gains = jnp.stack([g_gain_media, g_gain_lat, g_gain_ffn], axis=1)
    reduced = reduce_grads(g_qkv, g_out, g_up, g_down, g_time, g_gains)
    local_sq = jnp.zeros((), jnp.float32)
    for grad in reduced:
        local_sq = local_sq + jnp.sum(grad * grad)
    grad_norm = jnp.sqrt(lax.psum(local_sq, (DP, FSDP)))
    return new_latents, d_latents, grad_norm, reduced


def solution(mesh):
    both = (DP, FSDP)
    one, two, three = P(both), P(both, None), P(both, None, None)
    updated = (three,) * 3 + (two,) * 15
    placed = (three, three, one, three, *updated)
    return jax.shard_map(
        on_device,
        mesh=mesh,
        in_specs=placed,
        out_specs=(three, three, P(), *updated),
        check_vma=False,
    )
```

time: 795 us -> 602 us (0.76)
  matrix products: 132 us -> 0 us
  other arithmetic: 64.9 us -> 18.5 us
  local copies, waits for them, and re-layouts: 32.2 us -> 12.4 us
  Pallas kernels: 553 us -> 562 us
    dot_general x16 -> x0, matrix products: 132 us -> none  [the longest x1 19.1 us: on_device(): jnp.einsum('kd,kx->dx', keys_in, d_key_value, preferred_element_type=jnp....]
    convert_element_type x4 -> x1, other arithmetic: 17.1 us -> 0.08 us  [frame_tables(): ((time_index[:, None] == time_ids[None, :]) & live_frame[:, None]).astype...]
    reduce_sum x11 -> x1, other arithmetic: 15.7 us -> 1.28 us  [by_kernels(): jnp.sum(own.norm)]
    pallas_call x3 -> x0, local copies, waits for them, and re-layouts: 13.7 us -> none  [forward_all(): pl.pallas_call(functools.partial(forward_kernel, n_z, plan, needs), out_s...]
    concatenate x2 -> x1, other arithmetic: 10.7 us -> 0.01 us  [by_kernels(): tiny = jnp.concatenate([low_time, low_gains], axis=1)]
where the time goes in v3:
time: 602 us; the launch traced here: 596 us
  Pallas kernels  562 us (93%)
  other arithmetic  18.5 us (3%)
  local copies, waits for them, and re-layouts  12.4 us (2%)
    pallas_call x1, Pallas kernels, backward_all(): pl.pallas_call(functools.partial(backward_kernel, n_z, plan, (*given, *ou...  283 us
    pallas_call x1, Pallas kernels, forward_all(): pl.pallas_call(functools.partial(forward_kernel, n_z, plan, needs), out_s...  278 us

profile of v3, /device:TPU:0, one launch (start us, length us, event | category | flops | bytes accessed | tf_op | source)
XLA Modules:
  0.0 595.5 jit_solution(18323732371262844428)
XLA Ops:
  0.7 0.9 select_reduce_fusion.1
  1.6 0.7 sub.36
  2.5 0.7 pad.10.refs_8_.refs_18_
  3.5 1.2 compare_select_fusion.refs_9_.refs_20_
  5.5 0.8 copy.195
  6.3 0.9 convert_element_type.35.refs_2_
  7.2 0.9 convert_element_type.36.refs_3_
  8.2 0.7 convert_element_type.34.refs_1_
  8.8 278.5 %gather_and_forward.1 = (bf16[2,2,4,2,48,4608]{5,4,3,2,1,0:T(8,128)(2,1)}, bf16[2,2,4,2,48,1536]{5,4,3,2,1,0:T(8,128)(2,1)}, bf16[2,2,4,2,48,6144]{5,4,3,2,1,0:T...) custom-call(bf16[48,4608]{1,0:T(8,128)(2,1)} %bitcast.22, ...), custom_call_target="tpu_custom_call" | custom-call | tf_op jit(solution)/shard_map/gather_and_forward/pallas_call | solution.py:878
  287.3 0.7 broadcast_in_dim.65.refs_19_
  288.0 283.2 %backward_and_scatter.1 = (f32[48,4608]{1,0:T(8,128)}, f32[48,1536]{1,0:T(8,128)}, f32[48,6144]{1,0:T(8,128)}, f32[192,1536]{1,0:T(8,128)}, f32[48,128]{1,0:T(8,...) custom-call(bf16[2,2,4,2,48,4608]{5,4,3,2,1,0:T(8,128)(2,1)} %get-tu, ...), custom_call_target="tpu_custom_call" | custom-call | tf_op jit(solution)/shard_map/backward_and_scatter/pallas_call | solution.py:563
  571.2 1.3 reduce_sum.39
  573.4 0.8 sqrt_add_fusion
  576.9 0.8 multiply_subtract_fusion.4
  577.7 0.7 copy.188
  578.4 0.7 copy.189
  579.0 0.7 copy.190
  579.7 4.5 multiply_subtract_fusion
  584.3 2.4 multiply_subtract_fusion.1
  586.7 1.1 multiply_subtract_fusion.3
  589.4 2.0 multiply_subtract_fusion.2
  591.3 0.9 copy.202
  592.2 0.8 copy-done.5
  593.0 1.1 copy.203
  (81 shorter events, 5.9 us)
Async XLA Ops:
  0.7 4.0 copy-start.18
  0.7 4.0 copy-start.17
  0.7 4.8 copy-start.3
  4.7 1.6 copy-start.1
  5.5 1.7 copy-start
  7.2 1.0 copy-start.6
  288.0 285.2 %copy-start.21 = (f32[48,3]{0,1:T(4,128)S(1)}, f32[48,3]{0,1:T(4,128)}, u32[]{:S(2)}) copy-start(f32[48,3]{0,1:T(4,128)} %param.42) | copy-start | bytes 1732
  288.0 285.3 %copy-start.22 = (f32[48,3]{0,1:T(4,128)S(1)}, f32[48,3]{0,1:T(4,128)}, u32[]{:S(2)}) copy-start(f32[48,3]{0,1:T(4,128)} %param.43) | copy-start | bytes 1732
  288.0 288.7 %copy-start.19 = (f32[48,8]{0,1:T(8,128)S(1)}, f32[48,8]{0,1:T(8,128)}, u32[]{:S(2)}) copy-start(f32[48,8]{0,1:T(8,128)} %param.39) | copy-start | bytes 4612
  288.0 288.7 %copy-start.20 = (f32[48,8]{0,1:T(8,128)S(1)}, f32[48,8]{0,1:T(8,128)}, u32[]{:S(2)}) copy-start(f32[48,8]{0,1:T(8,128)} %param.40) | copy-start | bytes 4612
  579.7 4.6 copy-start.2
  579.7 4.6 copy-start.7
  579.7 4.6 copy-start.8
  579.7 4.6 copy-start.9
  584.3 2.4 copy-start.14
  584.3 2.4 copy-start.15
  584.3 2.4 copy-start.16
  586.7 1.5 copy-start.12
  586.7 1.7 copy-start.11
  587.8 1.3 copy-start.4
  587.8 1.6 copy-start.10
  589.3 2.0 copy-start.13
  591.3 1.7 copy-start.5

commit v4 on v3

--- a/solution.py
+++ b/solution.py
@@ -47,8 +47,9 @@
         pl.semaphore_signal(bar, inc=1, device_id=d, device_id_type=MESH)
     pl.semaphore_wait(bar, len(others))
 
-def block_index(place, held):
-    return tuple(slice(None) if ax in held else place.at[ax] for ax in "xczy")
+def block_index(place, held, **at):
+    where = {**place.at, **at}
+    return tuple(slice(None) if ax in held else where[ax] for ax in "xczy")
 
 class Gather:
     def __init__(self, place, src, dst, rows, cols, order, sems, base):
@@ -56,29 +57,64 @@
         self.sl = (pl.ds(*rows), pl.ds(*cols))
         self.order, self.sems, self.base = order, sems, base
         self.copies = {}
-    def region(self, held):
-        return self.dst.at[block_index(self.place, held) + self.sl]
+
+    def region(self, held, **at):
+        return self.dst.at[block_index(self.place, held, **at) + self.sl]
+
+    def copy(self, src, dst, n, to):
+        ss, rs = self.sems
+        n += self.base
+        return pltpu.make_async_remote_copy(src_ref=src, dst_ref=dst, send_sem=ss.at[n], recv_sem=rs.at[n], device_id=to, device_id_type=MESH)
+
     def start(self, step):
-        p = self.place; ax = self.order[step]; held = self.order[:step]
-        ss, rs = self.sems
-        made = []
-        n = self.base
-        for s in range(step):
-            n += p.n_z - 1 if self.order[s] == "z" else 1
-        src = self.src.at[self.sl] if step == 0 else self.region(held)
-        dst = self.region(held)
-        for k in (range(1, p.n_z) if ax == "z" else (0,)):
-            to = p.along_z(k) if ax == "z" else p.other(ax)
-            d = pltpu.make_async_remote_copy(src_ref=src, dst_ref=dst, send_sem=ss.at[n], recv_sem=rs.at[n], device_id=to, device_id_type=MESH)
-            d.start(); made.append(d); n += 1
-        self.copies[step] = made
+        ax, held, p = self.order[step], self.order[:step], self.place
+        if ax == "z":
+            self.line(step, 1)
+            return
+        d = self.copy(self.src.at[self.sl] if step == 0 else self.region(held), self.region(held), "xyc".index(ax), p.other(ax))
+        d.start()
+        self.copies[step] = d
+
+    def line(self, step, k):
+        p, held = self.place, self.order[:step]
+        z, last = p.at["z"], p.n_z - 1
+        for side, from_z, to_z in ((0, z - (k - 1), z + 1), (1, z + (k - 1), z - 1)):
+            ok = (from_z >= 0) & (to_z <= last) if side == 0 else (from_z <= last) & (to_z >= 0)
+            at = jnp.clip(from_z, 0, last)
+            dst = self.region(held, z=at)
+            src = self.src.at[self.sl] if step == 0 and k == 1 else dst
+            d = self.copy(src, dst, 3 + 2 * (k - 1) + side, p.dev(z=jnp.clip(to_z, 0, last)))
+            pl.when(ok)(d.start)
+            came = z >= k if side == 0 else z + k <= last
+            self.copies[step, k, side] = (d, ok, came)
+
+    def came(self, step, k):
+        for side in range(2):
+            d, _, came = self.copies[step, k, side]
+            pl.when(came)(d.wait_recv)
+
+    def advance(self, step, k):
+        if self.order[step] == "z":
+            self.came(step, k)
+            self.line(step, k + 1)
+
     def arrive(self, step):
-        for d in self.copies[step]: d.wait_recv()
+        if self.order[step] == "z":
+            self.came(step, self.place.n_z - 1)
+        else:
+            self.copies[step].wait_recv()
+
     def finish(self):
-        for made in self.copies.values():
-            for d in made: d.wait_send()
-
-def n_sems(n_z): return n_z + 2
+        for key, d in self.copies.items():
+            if isinstance(key, tuple):
+                pl.when(d[1])(d[0].wait_send)
+            else:
+                d.wait_send()
+
+
+def n_sems(n_z):
+    return 3 + 2 * (n_z - 1)
+
 
 def number(plan):
     j, out = 0, []
@@ -89,28 +125,33 @@
         out.append(new)
     return out, j
 
-ZYX, ZXY = ("z", "y", "x", "c"), ("z", "x", "y", "c")
-
-SLOTS = 4
+ZYX, ZXY, XYZ, YXZ = ("z", "y", "x", "c"), ("z", "x", "y", "c"), ("x", "y", "z", "c"), ("y", "x", "z", "c")
+
+BACK_LAG, SEND_SLOTS, LAND_SLOTS = 2, 3, 6
+ROOM_B = 4
+FINE_B = 0
 
 
 class Scatter:
-    def __init__(self, place, out, rows, cols, order, piece, part, turn, sems, bufs):
+    def __init__(self, place, out, rows, cols, order, piece, turn, sems, bufs, total_sq):
         self.p, self.out, self.order, self.piece = place, out, order, piece
         self.rows, self.cols, self.width = pl.ds(*rows), pl.ds(*cols), cols[1]
         self.ss, self.rs, self.ls = sems
-        self.part, self.b = part, bufs
-        self.here = (turn % SLOTS) * 2 + part
-        self.sent = {}
+        self.b, self.sq = bufs, total_sq
+        self.turn, self.h, self.n = turn, turn % SEND_SLOTS, turn % LAND_SLOTS
+        self.sent, self.moves = {}, {}
 
     def v(self, ref, *lead):
         return ref.at[lead + (slice(None), pl.ds(0, self.width))]
 
-    def send(self, src, dst, to, n):
-        n += self.piece * (self.p.n_z + 1)
-        d = pltpu.make_async_remote_copy(src_ref=src, dst_ref=dst, send_sem=self.ss.at[n], recv_sem=self.rs.at[n], device_id=to, device_id_type=MESH)
-        d.start()
-        return d
+    def copy(self, src, dst, to, n):
+        n += self.piece * n_sems(self.p.n_z)
+        return pltpu.make_async_remote_copy(src_ref=src, dst_ref=dst, send_sem=self.ss.at[n], recv_sem=self.rs.at[n], device_id=to, device_id_type=MESH)
+
+    def send(self, step, src, dst, ax):
+        d = self.copy(src, dst, self.p.other(ax), "xyc".index(ax))
+        d.start()
+        self.sent[step] = d
 
     def add(self, count, dst, a, b):
         w = slice(0, self.width)
@@ -120,62 +161,134 @@
             da[di + (slice(None), w)] = aa[ai + (slice(None), w)] + ba[bi + (slice(None), w)]
             return carry
 
-        lax.fori_loop(0, count, one, 0)
+        if count == 1:
+            one(0, 0)
+        else:
+            lax.fori_loop(0, count, one, 0)
+
+    def row(self, d):
+        if self.order[0] == "z":
+            return self.v(self.b.s0, self.h, slice(None), d, slice(None))
+        return self.v(self.b.s2, self.h, d)
+
+    def land(self, side, k):
+        if self.order[0] == "z":
+            return self.v(self.b.rz, self.n, side, k - 1, slice(None), slice(None))
+        return self.v(self.b.rz, self.n, side, k - 1)
+
+    def add_landed(self, d, side, k):
+        b, h, n = self.b, self.h, self.n
+        if self.order[0] == "z":
+            mine = lambda i: (b.s0, (h, i // 2, d, i % 2))
+            self.add(4, mine, mine, lambda i: (b.rz, (n, side, k - 1, i // 2, i % 2)))
+        else:
+            mine = lambda i: (b.s2, (h, d))
+            self.add(1, mine, mine, lambda i: (b.rz, (n, side, k - 1)))
+
+    def line(self, step, k):
+        p = self.p
+        z, last = p.at["z"], p.n_z - 1
+        for side, d, to in ((0, p.n_z - k + z, z + 1), (1, z - (p.n_z - k), z - 1)):
+            ok = d <= last if side == 0 else d >= 0
+            at = jnp.clip(d, 0, last)
+            if k > 1:
+                got, _, came = self.moves[step, k - 1, side]
+
+                def forward(got=got, at=at, side=side):
+                    got.wait_recv()
+                    self.add_landed(at, side, k - 1)
+
+                pl.when(came)(forward)
+            c = self.copy(self.row(at), self.land(side, k), p.dev(z=jnp.clip(to, 0, last)), 3 + 2 * (k - 1) + side)
+            pl.when(ok)(c.start)
+            came = z <= k if side == 0 else z >= last - k
+            came = came & (z > 0 if side == 0 else z < last)
+            self.moves[step, k, side] = (c, ok, came)
+
+    def last_move(self, step):
+        p = self.p
+        z, k = p.at["z"], p.n_z - 1
+        for side in range(2):
+            c, _, came = self.moves[step, k, side]
+
+            def end(c=c, side=side):
+                c.wait_recv()
+                self.add_landed(z, side, k)
+
+            pl.when(came)(end)
+
+    def advance(self, step, k):
+        if self.order[step] == "z":
+            self.line(step, k + 1)
 
     def free(self, step):
-        for d in self.sent.pop(step, ()):
-            d.wait_send() if step < 3 else d.wait()
-
-    def step0(self, fill):
-        p, b, A, h = self.p, self.b, slice(None), self.here
-        fill(b.s0, h, self)
-        ax = self.order[0]
-        o = 1 - p.at[ax]
-        if ax == "x":
-            pair = self.v(b.s0, h, o, A, A), self.v(b.r1y, h // 2, A, A)
+        if step == 3:
+            self.sent.pop(3).wait()
+        elif self.order[step] == "z":
+            for k in range(1, self.p.n_z):
+                for side in range(2):
+                    c, ok, _ = self.moves.pop((step, k, side))
+                    pl.when(ok)(c.wait_send)
         else:
-            pair = self.v(b.s0, h, A, A, o), self.v(b.r1x, h // 2, A, A)
-        self.sent[0] = [self.send(*pair, p.other(ax), 0)]
-
-    def step1(self):
-        p, b, A, h, nz = self.p, self.b, slice(None), self.here, self.p.n_z
-        for d in self.sent[0]:
-            d.wait_recv()
-        ax, nxt = self.order[0], self.order[1]
-        m, o = p.at[ax], 1 - p.at[nxt]
-        if ax == "x":
-            at = lambda i: (i // 2, i % 2)
-            self.add(2 * nz, lambda i: (b.s1y, (h // 2,) + at(i)), lambda i: (b.s0, (h, m) + at(i)), lambda i: (b.r1y, (h // 2,) + at(i)))
-            src = self.v(b.s1y, h // 2, A, o)
+            self.sent.pop(step).wait_send()
+
+    def start(self, step):
+        p, b, A, h, n, nz = self.p, self.b, slice(None), self.h, self.n, self.p.n_z
+        at = p.at
+        if step < 3 and self.order[step] == "z":
+            if step == 2:
+                first, nxt = self.order[:2]
+                mine = (lambda i: (b.s1, (h, i, at[nxt]))) if first == "x" else (lambda i: (b.s1, (h, at[nxt], i)))
+                self.sent[1].wait_recv()
+                self.add(nz, lambda i: (b.s2, (h, i)), mine, lambda i: (b.r2, (n, i)))
+            self.line(step, 1)
+            return
+        first = self.order[0]
+        if step == 0:
+            o = 1 - at[first]
+            src = self.v(b.s0, h, o, A, A) if first == "x" else self.v(b.s0, h, A, A, o)
+            self.send(0, src, self.v(b.r1, n, A, A), first)
+        elif step == 1 and first == "z":
+            self.last_move(0)
+            for x in range(2):
+                b.s1[h, x] = b.s0[h, x, at["z"]]
+            self.send(1, self.v(b.s1, h, 1 - at["x"], A), self.v(b.r1, n, A), "x")
+        elif step == 1:
+            self.sent[0].wait_recv()
+            o = 1 - at[self.order[1]]
+            i0, i1 = (lambda i: i // 2), (lambda i: i % 2)
+            if first == "y":
+                i0, i1 = (lambda i: i // nz), (lambda i: i % nz)
+                mine = lambda i: (b.s0, (h, i0(i), i1(i), at["y"]))
+            else:
+                mine = lambda i: (b.s0, (h, at["x"], i0(i), i1(i)))
+            self.add(2 * nz, lambda i: (b.s1, (h, i0(i), i1(i))), mine, lambda i: (b.r1, (n, i0(i), i1(i))))
+            src = self.v(b.s1, h, A, o) if first == "x" else self.v(b.s1, h, o, A)
+            self.send(1, src, self.v(b.r2, n, A), self.order[1])
+        elif step == 2:
+            self.sent[1].wait_recv()
+            self.add(2, lambda i: (b.s2, (h, i)), lambda i: (b.s1, (h, at["x"], i)), lambda i: (b.r1, (n, i)))
+            self.send(2, self.v(b.s2, h, 1 - at["y"]), self.v(b.r2, n), "y")
         else:
-            at = lambda i: (i // nz, i % nz)
-            self.add(2 * nz, lambda i: (b.s1x, (h // 2,) + at(i)), lambda i: (b.s0, (h,) + at(i) + (m,)), lambda i: (b.r1x, (h // 2,) + at(i)))
-            src = self.v(b.s1x, h // 2, o, A)
-        self.sent[1] = [self.send(src, self.v(b.r2, h, A), p.other(nxt), 1)]
-
-    def step2(self):
-        p, b, h, nz = self.p, self.b, self.here, self.p.n_z
-        for d in self.sent[1]:
-            d.wait_recv()
-        m = p.at[self.order[1]]
-        mine = (lambda i: (b.s1y, (h // 2, i, m))) if self.order[0] == "x" else (lambda i: (b.s1x, (h // 2, m, i)))
-        self.add(nz, lambda i: (b.s2, (h, i)), mine, lambda i: (b.r2, (h, i)))
-        self.sent[2] = [
-            self.send(self.v(b.s2, h, (p.at["z"] + k) % nz), self.v(b.r3, h, k - 1), p.along_z(k), 1 + k) for k in range(1, nz)
-        ]
-
-    def step3(self):
-        p, b, h, nz, w = self.p, self.b, self.here, self.p.n_z, self.width
-        for d in self.sent[2]:
-            d.wait_recv()
-        total = b.s2[h, p.at["z"], :, 0:w].astype(jnp.float32)
-        for k in range(nz - 1):
-            total = total + b.r3[h, k, :, 0:w].astype(jnp.float32)
-        b.o[h, :, 0:w] = total
-        b.sq[:, 0:w] += total * total
-        d = pltpu.make_async_copy(self.v(b.o, h), self.out.at[self.rows, self.cols], self.ls.at[h])
-        d.start()
-        self.sent[3] = [d]
+            w = slice(0, self.width)
+            if first == "z":
+                self.sent[2].wait_recv()
+                total = b.s2[h, at["y"], :, w].astype(jnp.float32) + b.r2[n, :, w].astype(jnp.float32)
+            else:
+                p_last = nz - 1
+                for side in range(2):
+                    c, _, came = self.moves[2, p_last, side]
+                    pl.when(came)(c.wait_recv)
+                total = b.s2[h, at["z"], :, w].astype(jnp.float32)
+                for side in range(2):
+                    came = self.moves[2, p_last, side][2]
+                    landed = b.rz[n, side, p_last - 1, :, w].astype(jnp.float32)
+                    total = total + jnp.where(came, landed, 0.0)
+            b.o[h, :, w] = total
+            self.sq[:, w] += total * total
+            d = pltpu.make_async_copy(self.v(b.o, h), self.out.at[self.rows, self.cols], self.ls.at[self.piece])
+            d.start()
+            self.sent[3] = d
 
 
 def sum_squares(place, n_z, bufs, sems, out):
@@ -257,12 +370,12 @@
             use(i, wbuf[i % 2].reshape(384, model))
 
     def hidden_part(i):
-        d = pltpu.make_async_copy(b.dpre.at[:, pl.ds(i * model, model)], b.dpart, ws.at[4])
+        d = pltpu.make_async_copy(b.dpre.at[:, pl.ds(i * model, model)], b.datt, ws.at[4])
         d.start()
         d.wait()
 
         def use(n, w):
-            got_ = dot(b.dpart[...], w, ((1,), (1,)))
+            got_ = dot(b.datt[...], w, ((1,), (1,)))
             cols = slice(n * 384, (n + 1) * 384)
             if i == 0:
                 b.dmid[:, cols] = got_
@@ -372,7 +485,7 @@
     late = []
 
     def media_back(part):
-        step = media_rows // 3
+        step = media_rows // parts
         frames = step // 48
         d = pltpu.make_async_copy(b.media.at[pl.ds(part * step, step)], b.mrows, ws.at[3])
         d.start()
@@ -390,8 +503,8 @@
         lax.fori_loop(0, frames, frame, 0)
 
     def small():
-        b.gblocks[...] = b.gsmall[...].T.astype(bf).reshape(b.gblocks.shape)
-        give(b.gblocks.at[:, 1 - core], b.x_tiny)
+        b.tiny[...] = b.gsmall[...].T.astype(bf).reshape(b.tiny.shape)
+        give(b.tiny.at[:, 1 - core], b.x_tiny)
 
     held = [None]
 
@@ -409,114 +522,131 @@
         d.start()
         d.wait()
 
-    def right(own, sibling, cols, part):
-        made = [pltpu.make_async_copy(r.at[:, pl.ds(*cols)], b.rhs.at[part, i], rhs_sem.at[part, i]) for i, r in enumerate((own, sibling))]
+    coming = {}
+
+    def sources(w, first):
+        if w == 3:
+            return b.p_cot.at[core], b.p_cot.at[1 - core], first
+        if w == 2:
+            return b.dpre, b.x_dpre, first
+        if w == 1:
+            return b.dbranch, b.x_branch, first
+        return (b.dq, b.dk, b.dv)[first // model], (b.x_dq, b.x_dk, b.x_dv)[first // model], first % model
+
+    def right(t):
+        w, first, width = plan_of[t]
+        if w == 4 or t in coming:
+            return
+        mine, theirs, at = sources(w, first)
+        if w != 3:
+            if id(theirs) not in given:
+                return
+            got(theirs)
+        cols = pl.ds(at, width)
+        made = []
+        if w in (2, 3):
+            made.append(pltpu.make_async_copy(mine.at[:, cols], b.rhs.at[t % 2, 0, :, pl.ds(0, width)], rhs_sem.at[t % 2, 0]))
+        into = b.rhsk.at[:, pl.ds(0, width)] if w == 0 and first >= model else b.rhs.at[t % 2, 1, :, pl.ds(0, width)]
+        made.append(pltpu.make_async_copy(theirs.at[:, cols], into, rhs_sem.at[t % 2, 1]))
         for d in made:
             d.start()
-        for d in made:
-            d.wait()
+        coming[t] = made
 
     def blocks(x, k, group):
         if group == 1:
             return [b.lt[s, x, 0 : 2 * n_z].reshape(96 * n_z, queries_n) for s in (core, 1 - core)]
         return [jnp.concatenate([b.lt[s, x, i * group + k] for i in range(2 * n_z)], axis=0) for s in (core, 1 - core)]
 
-    def filler(w, rows, cols):
-        first, width = cols
-        wide = pl.ds(first, width)
-
-        def fill(dst, here, g):
-            if w == 4:
-                got(b.x_tiny)
-                d = pltpu.make_async_copy(b.x_tiny, b.tiny2, ws.at[3])
-                d.start()
-                d.wait()
-
-                def one(i, carry):
-                    x, z, y = i // (2 * n_z), (i // 2) % n_z, i % 2
-                    dst[here, x, z, y, :, 0:width] = b.gblocks[x, core, z, y] + b.tiny2[x, z, y]
-                    return carry
-
-                lax.fori_loop(0, 4 * n_z, one, 0)
-                return
-            keyed = w == 0 and first >= model
+    def fill(t, pieces):
+        w, first, width = plan_of[t]
+        h = pieces[0].h
+        if w == 4:
+            got(b.x_tiny)
+            d = pltpu.make_async_copy(b.x_tiny, b.tiny2, ws.at[3])
+            d.start()
+            d.wait()
+
+            def one(i, carry):
+                x, z, y = i // (2 * n_z), (i // 2) % n_z, i % 2
+                pieces[0].b.s0[h, x, z, y, :, 0:128] = b.tiny[x, core, z, y] + b.tiny2[x, z, y]
+                return carry
+
+            lax.fori_loop(0, 4 * n_z, one, 0)
+            return
+        right(t)
+        for d in coming.pop(t):
+            d.wait()
+        mine, _, at = sources(w, first)
+        keyed = w == 0 and first >= model
+        left((b.p_keys if keyed else b.p_lat, b.p_att, b.p_hid, b.p_act)[w])
+        r = [b.rhs[t % 2, 0, :, 0:width] if w in (2, 3) else mine[:, pl.ds(at, width)], b.rhsk[:, 0:width] if keyed else b.rhs[t % 2, 1, :, 0:width]]
+        for x in range(2):
             if keyed:
-                left(b.p_keys)
-                mine, theirs = (b.dk, b.x_dk) if first < 2 * model else (b.dv, b.x_dv)
-                got(theirs)
-                at = pl.ds(first % model, width)
-                d = pltpu.make_async_copy(theirs.at[:, at], b.rhsk.at[g.part], rhs_sem.at[g.part, 0])
-                d.start()
-                d.wait()
-                r = [mine[:, at], b.rhsk[g.part]]
-            elif w == 3:
-                left(b.p_act)
-                right(b.p_cot.at[core], b.p_cot.at[1 - core], cols, g.part)
-            elif w == 2:
-                left(b.p_hid)
-                got(b.x_dpre)
-                right(b.dpre, b.x_dpre, cols, g.part)
+                l = [b.ltk[s, x].reshape(96 * n_z, key_rows) for s in (core, 1 - core)]
             else:
-                mine, theirs, act = (b.dbranch, b.x_branch, b.p_att) if w == 1 else (b.dq, b.x_dq, b.p_lat)
-                left(act)
-                got(theirs)
-                at = pl.ds(first % model, width)
-                d = pltpu.make_async_copy(theirs.at[:, at], b.rhs.at[g.part, 1], rhs_sem.at[g.part, 1])
-                d.start()
-                d.wait()
-            if w in (2, 3):
-                r = [b.rhs[g.part, 0], b.rhs[g.part, 1]]
-            elif not keyed:
-                r = [mine[:, at], b.rhs[g.part, 1]]
-            for x in range(2):
-                if keyed:
-                    l = [b.ltk[s, x].reshape(96 * n_z, key_rows) for s in (core, 1 - core)]
-                else:
-                    l = blocks(x, rows[0] // 48, 4 if w == 3 else 1)
-                total = dot(l[0], r[0]) + dot(l[1], r[1])
-                dst[here, x, :, :, :, 0:width] = total.astype(bf).reshape(n_z, 2, 48, width)
-
-        return fill
-
-    parts = 3
+                l = blocks(x, rows_of[t] // 48, 4 if w == 3 else 1)
+            sums = (dot(l[0], r[0]) + dot(l[1], r[1])).astype(bf)
+            start = 0
+            for g in pieces:
+                g.b.s0[h, x, :, :, :, 0 : g.width] = sums[:, start : start + g.width].reshape(n_z, 2, 48, g.width)
+                start += g.width
+        if t + 1 < total_stages:
+            right(t + 1)
+
+    parts = 6
     work = [(3, 5, functools.partial(hidden_part, i)) for i in range(hidden_n // model)] + [(0, 3, ffn_norm), (0, 4, attended_back)]
     work += [(0, 9, functools.partial(attend_back, g)) for g in range(model // group_width)]
     work += [(0, 5, functools.partial(keys_back, n)) for n in range(4)] + [(0, 3, latents_back)]
-    work += [(0, 4, functools.partial(media_back, i)) for i in range(parts)] + [(0, 2, small)]
+    work += [(0, 2, functools.partial(media_back, i)) for i in range(parts)] + [(0, 2, small)]
 
     def run_until(dst):
         while id(dst) not in given:
             work.pop(0)[2]()
 
+    kinds = [types.SimpleNamespace(**{n: getattr(b, n + k) for n in NAMES}) for k in SETS]
+    plan_of = [(st[0][1], st[0][3][0], sum(p[3][1] for p in st)) for st in plan]
+    rows_of = [st[0][2][0] for st in plan]
+    total_stages = len(plan)
     stages = [
-        [Scatter(place, own_grads[w], rows, cols, order, j, part, t, (ss, rs, ls), b) for part, (j, w, rows, cols, order) in enumerate(stage)]
+        [Scatter(place, own_grads[w], rows, cols, order, j, t, (ss, rs, ls), kinds[part], b.sq) for part, (j, w, rows, cols, order) in enumerate(stage)]
         for t, stage in enumerate(plan)
     ]
-    total = len(stages)
-    for t in range(total + 3):
+    ticks = total_stages + 3 * BACK_LAG
+
+    def moves(t, k):
+        for back in range(3):
+            u = t - BACK_LAG * back - 1
+            if 0 <= u < total_stages:
+                for g in stages[u]:
+                    g.advance(back, k)
+
+    for t in range(ticks):
+        moves(t, 1)
         for back in range(4):
-            u = t - back
-            if not 0 <= u < total:
+            u = t - BACK_LAG * back
+            if not 0 <= u < total_stages:
                 continue
-            if u >= SLOTS:
-                for g in stages[u - SLOTS]:
-                    g.free(back)
-            for g, (j, w, rows, cols, order) in zip(stages[u], plan[u]):
-                if back == 0:
-                    need = (b.x_dv, b.x_branch, b.x_dpre, b.x_dpre, b.x_tiny)[w]
-                    run_until(need)
-                    g.step0(filler(w, rows, cols))
-                else:
-                    (g.step1, g.step2, g.step3)[back - 1]()
-        room = 9
+            if u >= SEND_SLOTS:
+                for g in stages[u - SEND_SLOTS]:
+                    if back == 3 or g.order[back] == "z" or back in g.sent:
+                        g.free(back)
+            if back == 0:
+                w = plan_of[u][0]
+                run_until((b.x_dv, b.x_branch, b.x_dpre, b.x_dpre, b.x_tiny)[w])
+                fill(u, stages[u])
+            for g in stages[u]:
+                g.start(back)
+        for k in range(2, n_z - 1):
+            moves(t, k)
+        room = ROOM_B
         while work and room > 0:
             _, cost, piece = work.pop(0)
             room -= cost
             piece()
-    for st in stages:
+    for st in stages[-SEND_SLOTS:]:
         for g in st:
-            for k in range(4):
-                g.free(k)
+            for back in range(4):
+                g.free(back)
     for d, done in given.values():
         d.wait_send()
     for d in late:
@@ -524,22 +654,39 @@
     sum_squares(place, n_z, b, (ns, nr), b.norm)
 
 
-def backward_plan(shards, model, width):
-    orders = (("x", "y", "z"), ("y", "x", "z"))
-    pieces = [(3, (k, 48), (c, width)) for k in range(0, shards[3].shape[0], 48) for c in range(0, model, width)]
-    pieces += [(2, (0, 48), (c, width)) for c in range(0, shards[2].shape[1], width)]
-    pieces += [(1, (0, 48), (c, width)) for c in range(0, model, width)] + [(4, (0, 48), (0, 128))]
-    pieces += [(0, (0, 48), (c, width)) for c in range(0, 3 * model, width)]
-    return [[p + (orders[i],) for i, p in enumerate(pieces[n : n + 2])] for n in range(0, len(pieces), 2)]
+SETS = "abc"
+NAMES = ("s0", "r1", "s1", "r2", "s2", "rz", "o")
+
+
+def backward_plan(shards, model):
+    tile = 128
+    stages = []
+
+    def split(w, row, first, widths=None):
+        widths = widths or ((3, 2, 1), (2, 3, 1))[len(stages) % 2]
+        at, pieces = first, []
+        for width, order in zip(widths, (("x", "y", "z"), ("y", "x", "z"), ("z", "x", "y"))):
+            pieces.append((w, (row, 48), (at, width * tile), order))
+            at += width * tile
+        stages.append(pieces)
+
+    for row in range(0, shards[3].shape[0], 48):
+        for first in range(0, model, 768):
+            split(3, row, first)
+    for w, cols in ((2, shards[2].shape[1]), (1, model), (0, 3 * model)):
+        for first in range(0, cols - FINE_B * 768 * (w == 0), 768):
+            split(w, 0, first)
+    for first in range(3 * model - FINE_B * 768, 3 * model, 384):
+        split(0, 0, first, (1, 1, 1))
+    return stages + [[(4, (0, 48), (0, 128), ("x", "y", "z"))]]
 
 
 def backward_all(full, made, lat, media, hot, hotc, bias, shards, n_z):
-    width = 512
     queries_n, model = lat.shape
     media_rows = media.shape[0]
     key_rows = queries_n + media_rows
     hidden_n = shards[2].shape[1]
-    plan, count = number(backward_plan(shards, model, width))
+    plan, count = number(backward_plan(shards, model))
     q, k, v, dpre, mid, new, lse, p_keys, p_lat, p_att, p_hid, p_act, p_cot = made
     given = dict(f_qkv=full[0], f_out=full[1], f_up=full[2], f_tiny=full[4], dpre=dpre, p_keys=p_keys, p_lat=p_lat, p_att=p_att, p_hid=p_hid, p_act=p_act, p_cot=p_cot,
                  media=media, q=q, keys=k, v=v, mid=mid, lse=lse, lat=lat, hot=hot, hotc=hotc, bias=bias)
@@ -548,24 +695,25 @@
     outs = dict(g_qkv=grads[0], g_out=grads[1], g_up=grads[2], g_down=grads[3], g_tiny=grads[4], d_lat=((queries_n, model), f32), norm=((8, 128), f32),
                 x_dpre=((queries_n, hidden_n), bf), x_branch=((queries_n, model), bf), x_dq=((queries_n, model), bf), x_dk=((key_rows, model), bf), x_dv=((key_rows, model), bf),
                 x_tiny=((2, n_z, 2, 48, 128), bf))
-    W, S = width, SLOTS
-    vm = dict(s0=((2 * S, 2, n_z, 2, 48, W), bf), r1x=((S, 2, n_z, 48, W), bf), r1y=((S, n_z, 2, 48, W), bf), s1x=((S, 2, n_z, 48, W), bf), s1y=((S, n_z, 2, 48, W), bf),
-          r2=((2 * S, n_z, 48, W), bf), s2=((2 * S, n_z, 48, W), bf), r3=((2 * S, n_z - 1, 48, W), bf), o=((2 * S, 48, W), f32),
+    W, S, L = 384, SEND_SLOTS, LAND_SLOTS
+    vm = dict(s0a=((S, 2, n_z, 2, 48, W), bf), r1a=((L, n_z, 2, 48, W), bf), s1a=((S, n_z, 2, 48, W), bf), r2a=((L, n_z, 48, W), bf), s2a=((S, n_z, 48, W), bf), rza=((L, 2, n_z - 1, 48, W), bf), oa=((S, 48, W), f32),
+              s0b=((S, 2, n_z, 2, 48, W), bf), r1b=((L, 2, n_z, 48, W), bf), s1b=((S, 2, n_z, 48, W), bf), r2b=((L, n_z, 48, W), bf), s2b=((S, n_z, 48, W), bf), rzb=((L, 2, n_z - 1, 48, W), bf), ob=((S, 48, W), f32),
+              s0c=((S, 2, n_z, 2, 48, 128), bf), rzc=((L, 2, n_z - 1, 2, 2, 48, 128), bf), r1c=((L, 2, 48, 128), bf), s1c=((S, 2, 2, 48, 128), bf), s2c=((S, 2, 48, 128), bf), r2c=((L, 48, 128), bf), oc=((S, 48, 128), f32),
           sq=((48, W), f32), n=((6, 8, 128), f32), nz=((n_z, 8, 128), f32),
-          wbuf=((3, n_z, 2, 48, model), bf), dpart=((queries_n, model), bf), dmid=((queries_n, model), f32), dbranch=((queries_n, model), bf), datt=((queries_n, model), bf),
+          wbuf=((3, n_z, 2, 48, model), bf), dmid=((queries_n, model), f32), dbranch=((queries_n, model), bf), datt=((queries_n, model), bf),
           dq=((queries_n, model), bf), k=((key_rows, model), bf), dk=((key_rows, model), bf), dv=((key_rows, model), bf), tiny=((2, 2, n_z, 2, 48, 128), bf), tiny_t=((128, model), f32),
-          gsmall=((128, model), f32), gblocks=((2, 2, n_z, 2, 48, 128), bf), tiny2=((2, n_z, 2, 48, 128), bf), mrows=((media_rows // 3, model), bf),
-          lt=(p_act.shape, bf), ltk=(p_keys.shape, bf), rhs=((2, 2, queries_n, W), bf), rhsk=((2, key_rows, W), bf))
+          gsmall=((128, model), f32), tiny2=((2, n_z, 2, 48, 128), bf), mrows=((media_rows // 6, model), bf),
+          lt=(p_act.shape, bf), ltk=(p_keys.shape, bf), rhs=((2, 2, queries_n, 768), bf), rhsk=((key_rows, 768), bf))
     sem = pltpu.SemaphoreType.DMA
     in_vmem, in_any = pl.BlockSpec(memory_space=pltpu.VMEM), pl.BlockSpec(memory_space=ANY)
     resident = tuple(id(a) for a in (q, v, mid, lse, lat, hot, hotc, bias))
-    n_copies = count * (n_z + 1)
+    n_copies = count * n_sems(n_z)
     res = pl.pallas_call(
         functools.partial(backward_kernel, n_z, plan, (*given, *outs, *vm)),
         out_shape=[jax.ShapeDtypeStruct(*o) for o in outs.values()],
         in_specs=[in_vmem if id(a) in resident else in_any for a in given.values()],
         out_specs=[in_vmem if o is outs["norm"] else in_any for o in outs.values()],
-        scratch_shapes=[pltpu.VMEM(*m) for m in vm.values()] + [sem((n_copies,)), sem((n_copies,)), sem((2 * S,)), sem((n_z + 2,)), sem((n_z + 2,)), sem((5,)), sem((8,)), sem((8,)), sem((1,)), sem((2, 2)), sem((2,))],
+        scratch_shapes=[pltpu.VMEM(*m) for m in vm.values()] + [sem((n_copies,)), sem((n_copies,)), sem((count,)), sem((n_z + 2,)), sem((n_z + 2,)), sem((5,)), sem((8,)), sem((8,)), sem((1,)), sem((2, 2)), sem((2,))],
         name="backward_and_scatter",
         compiler_params=pltpu.CompilerParams(collective_id=1, has_side_effects=True, vmem_limit_bytes=62 * 2**20),
     )(*given.values())
@@ -816,9 +964,15 @@
     stages = [[Gather(place, sh[w], full[w], rows, cols, order, (ss, rs), j * n_sems(n_z)) for (j, w, rows, cols, order) in stage] for stage in plan]
     waited = set()
     total, steps = len(stages), 4
-    for t in range(total + steps):
+    ticks = total + LAG * steps
+    for t in range(ticks):
+        for back in range(steps):
+            u = t - LAG * back - 1
+            if LAG > 1 and 0 <= u < total:
+                for g in stages[u]:
+                    g.advance(back, 1)
         for back in range(steps + 1):
-            u = t - back
+            u = t - LAG * back
             if not 0 <= u < total:
                 continue
             for g, (j, w, *_) in zip(stages[u], plan[u]):
@@ -829,8 +983,14 @@
                     g.arrive(back - 1)
                 if back < steps:
                     g.start(back)
-        room = 14
-        while work and work[0][0] <= t - steps and (room > 0 or t == total + steps - 1):
+        for move in range(1 if LAG == 1 else 2, n_z - 1):
+            for back in range(steps):
+                u = t - LAG * back - (LAG > 1)
+                if 0 <= u < total:
+                    for g in stages[u]:
+                        g.advance(back, move)
+        room = ROOM_A
+        while work and work[0][0] <= t - LAG * steps and (room > 0 or t == ticks - 1):
             need, cost, piece = work.pop(0)
             room -= cost
             piece()
@@ -839,22 +999,43 @@
             g.finish()
 
 
+ROOM_A = 12
+LAG = 2
+FINE = 1
+Z_DOWN = (1,)
+
+
 def forward_plan(shards, model):
-    two = lambda w, rows, first, width: [(w, (0, rows), (first, width), ZYX), (w, (0, rows), (first + width, width), ZXY)]
-    rows, half = shards[1].shape[0], model // 2
+    def split(w, rows, first, widths, last):
+        at, pieces = first, []
+        for width, order in zip(widths, (ZYX, ZXY, last)):
+            pieces.append((w, (0, rows), (at, width), order))
+            at += width
+        return pieces
+
+    rows = shards[1].shape[0]
     stages, needs = [[(4, (0, rows), (0, 128), ZYX)]], {"tiny": 0}
+    wide = model * 5 // 12, model * 5 // 12, model // 6
     for i, name in enumerate("qkv"):
         needs[name] = len(stages)
-        stages.append(two(0, rows, i * model, half))
+        stages.append(split(0, rows, i * model, wide, (XYZ, YXZ)[i % 2]))
     needs["out"] = len(stages)
-    stages.append(two(1, rows, 0, half))
+    stages.append(split(1, rows, 0, wide, YXZ))
     needs["up"], needs["down"] = [], []
     for i in range(shards[2].shape[1] // model):
         needs["up"].append(len(stages))
-        stages.append(two(2, rows, i * model, half))
-    for i in range(model // 256):
-        needs["down"].append(len(stages))
-        stages.append(two(3, shards[3].shape[0], i * 256, 128))
+        stages.append(split(2, rows, i * model, wide, (XYZ, YXZ)[i % 2]))
+    groups = model // 256
+    deep = shards[3].shape[0]
+    for i in range(groups):
+        if i >= groups - FINE:
+            for half in range(2):
+                cols = (i * 256 + half * 128, 128)
+                stages.append([(3, (0, deep // 2), cols, ZYX), (3, (deep // 2, deep // 2), cols, ZXY)])
+        else:
+            pair = (XYZ, YXZ) if i in Z_DOWN else (ZYX, ZXY)
+            stages.append([(3, (0, deep), (i * 256 + n * 128, 128), pair[n]) for n in range(2)])
+        needs["down"].append(len(stages) - 1)
     return stages, needs
 
 

time: 602 us -> 550 us (0.914)
  Pallas kernels: 562 us -> 509 us
    pallas_call x1, Pallas kernels: 278 us -> 248 us  [forward_all(): pl.pallas_call(functools.partial(forward_kernel, n_z, plan, needs), out_s...]
    pallas_call x1, Pallas kernels: 283 us -> 261 us  [backward_all(): pl.pallas_call(functools.partial(backward_kernel, n_z, plan, (*given, *ou...]
where the time goes in v4:
time: 550 us; the launch traced here: 543 us
  Pallas kernels  509 us (93%)
  other arithmetic  18.5 us (3%)
  local copies, waits for them, and re-layouts  12.4 us (2%)
    pallas_call x1, Pallas kernels, backward_all(): pl.pallas_call(functools.partial(backward_kernel, n_z, plan, (*given, *ou...  261 us
    pallas_call x1, Pallas kernels, forward_all(): pl.pallas_call(functools.partial(forward_kernel, n_z, plan, needs), out_s...  248 us

profile of v4, /device:TPU:0, one launch (start us, length us, event | category | flops | bytes accessed | tf_op | source)
XLA Modules:
  0.0 542.8 jit_solution(6147448117811250500)
XLA Ops:
  0.7 0.9 select_reduce_fusion.1
  1.6 0.7 sub.36
  2.5 0.7 pad.10.refs_8_.refs_18_
  3.5 1.2 compare_select_fusion.refs_9_.refs_20_
  5.5 0.8 copy.195
  6.3 0.9 convert_element_type.35.refs_2_
  7.2 0.9 convert_element_type.36.refs_3_
  8.2 0.7 convert_element_type.34.refs_1_
  8.8 248.3 %gather_and_forward.1 = (bf16[2,2,4,2,48,4608]{5,4,3,2,1,0:T(8,128)(2,1)}, bf16[2,2,4,2,48,1536]{5,4,3,2,1,0:T(8,128)(2,1)}, bf16[2,2,4,2,48,6144]{5,4,3,2,1,0:T...) custom-call(bf16[48,4608]{1,0:T(8,128)(2,1)} %bitcast.22, ...), custom_call_target="tpu_custom_call" | custom-call | tf_op jit(solution)/shard_map/gather_and_forward/pallas_call | solution.py:1059
  257.2 0.7 broadcast_in_dim.65.refs_19_
  257.9 260.6 %backward_and_scatter.1 = (f32[48,4608]{1,0:T(8,128)}, f32[48,1536]{1,0:T(8,128)}, f32[48,6144]{1,0:T(8,128)}, f32[192,1536]{1,0:T(8,128)}, f32[48,128]{1,0:T(8,...) custom-call(bf16[2,2,4,2,48,4608]{5,4,3,2,1,0:T(8,128)(2,1)} %get-tu, ...), custom_call_target="tpu_custom_call" | custom-call | tf_op jit(solution)/shard_map/backward_and_scatter/pallas_call | solution.py:711
  518.5 1.3 reduce_sum.39
  520.8 0.8 sqrt_add_fusion
  524.3 0.8 multiply_subtract_fusion.4
  525.0 0.7 copy.188
  525.7 0.7 copy.189
  526.4 0.7 copy.190
  527.0 4.5 multiply_subtract_fusion
  531.6 2.4 multiply_subtract_fusion.1
  534.0 1.1 multiply_subtract_fusion.3
  536.7 2.0 multiply_subtract_fusion.2
  538.6 0.9 copy.202
  539.5 0.8 copy-done.5
  540.3 1.1 copy.203
  (81 shorter events, 5.9 us)
Async XLA Ops:
  0.7 4.0 copy-start.18
  0.7 4.0 copy-start.17
  0.7 4.8 copy-start.3
  4.7 1.6 copy-start.1
  5.5 1.7 copy-start
  7.2 1.0 copy-start.6
  257.9 262.7 %copy-start.21 = (f32[48,3]{0,1:T(4,128)S(1)}, f32[48,3]{0,1:T(4,128)}, u32[]{:S(2)}) copy-start(f32[48,3]{0,1:T(4,128)} %param.42) | copy-start | bytes 1732
  257.9 262.8 %copy-start.22 = (f32[48,3]{0,1:T(4,128)S(1)}, f32[48,3]{0,1:T(4,128)}, u32[]{:S(2)}) copy-start(f32[48,3]{0,1:T(4,128)} %param.43) | copy-start | bytes 1732
  257.9 266.1 %copy-start.19 = (f32[48,8]{0,1:T(8,128)S(1)}, f32[48,8]{0,1:T(8,128)}, u32[]{:S(2)}) copy-start(f32[48,8]{0,1:T(8,128)} %param.39) | copy-start | bytes 4612
  257.9 266.2 %copy-start.20 = (f32[48,8]{0,1:T(8,128)S(1)}, f32[48,8]{0,1:T(8,128)}, u32[]{:S(2)}) copy-start(f32[48,8]{0,1:T(8,128)} %param.40) | copy-start | bytes 4612
  527.0 4.6 copy-start.2
  527.0 4.6 copy-start.7
  527.0 4.6 copy-start.8
  527.0 4.6 copy-start.9
  531.6 2.4 copy-start.14
  531.6 2.4 copy-start.15
  531.6 2.4 copy-start.16
  534.0 1.5 copy-start.12
  534.0 1.7 copy-start.11
  535.1 1.3 copy-start.4
  535.1 1.6 copy-start.10
  536.7 2.0 copy-start.13
  538.6 1.7 copy-start.5

commit v5 on v4

--- a/solution.py
+++ b/solution.py
@@ -37,12 +37,15 @@
         return self.dev(**{ax: 1 - self.at[ax]})
     def along_z(self, k):
         return self.dev(z=(self.at["z"] + k) % self.n_z)
+    def level(self):
+        flip = lambda ax, by: 1 - self.at[ax] if by else self.at[ax]
+        return [self.dev(x=flip("x", n & 4), c=flip("c", n & 2), y=flip("y", n & 1)) for n in range(1, 8)]
     def partners(self):
         return [self.other(a) for a in "cxy"] + [self.along_z(k) for k in range(1, self.n_z)]
 
-def greet(place):
+def greet(place, wide=False):
     bar = pltpu.get_barrier_semaphore()
-    others = place.partners()
+    others = place.level() + place.partners()[3:] if wide else place.partners()
     for d in others:
         pl.semaphore_signal(bar, inc=1, device_id=d, device_id_type=MESH)
     pl.semaphore_wait(bar, len(others))
@@ -134,8 +137,9 @@
 
 class Scatter:
     def __init__(self, place, out, rows, cols, order, piece, turn, sems, bufs, total_sq):
-        self.p, self.out, self.order, self.piece = place, out, order, piece
-        self.rows, self.cols, self.width = pl.ds(*rows), pl.ds(*cols), cols[1]
+        self.p, self.order, self.piece, self.width = place, order, piece, cols[1]
+        model = out.shape[-1]
+        self.out = out.at[cols[0] // model, pl.ds(*rows), pl.ds(cols[0] % model, cols[1])] if len(out.shape) == 3 else out.at[pl.ds(*rows), pl.ds(*cols)]
         self.ss, self.rs, self.ls = sems
         self.b, self.sq = bufs, total_sq
         self.turn, self.h, self.n = turn, turn % SEND_SLOTS, turn % LAND_SLOTS
@@ -286,7 +290,7 @@
                     total = total + jnp.where(came, landed, 0.0)
             b.o[h, :, w] = total
             self.sq[:, w] += total * total
-            d = pltpu.make_async_copy(self.v(b.o, h), self.out.at[self.rows, self.cols], self.ls.at[self.piece])
+            d = pltpu.make_async_copy(self.v(b.o, h), self.out, self.ls.at[self.piece])
             d.start()
             self.sent[3] = d
 
@@ -298,17 +302,24 @@
     for i in range(sq.shape[0] // 8):
         for j in range(sq.shape[1] // 128):
             acc = acc + sq[i * 8 : (i + 1) * 8, j * 128 : (j + 1) * 128]
-    for n, ax in enumerate("cxy"):
-        part[2 * n] = acc
-        d = pltpu.make_async_remote_copy(src_ref=part.at[2 * n], dst_ref=part.at[2 * n + 1], send_sem=ns.at[n], recv_sem=nr.at[n], device_id=place.other(ax), device_id_type=MESH)
+    at = place.at
+    me = at["x"] * 4 + at["c"] * 2 + at["y"]
+    part[me] = acc
+    made = []
+    for n, d in enumerate(place.level()):
+        made.append(pltpu.make_async_remote_copy(src_ref=part.at[me], dst_ref=part.at[me], send_sem=ns.at[n], recv_sem=nr.at[n], device_id=d, device_id_type=MESH))
+    for d in made:
         d.start()
+    for d in made:
         d.wait()
-        acc = part[2 * n] + part[2 * n + 1]
-    z = place.at["z"]
+    acc = part[0]
+    for n in range(1, 8):
+        acc = acc + part[n]
+    z = at["z"]
     zs[z] = acc
     made = []
     for k in range(1, n_z):
-        d = pltpu.make_async_remote_copy(src_ref=zs.at[z], dst_ref=zs.at[z], send_sem=ns.at[2 + k], recv_sem=nr.at[2 + k], device_id=place.along_z(k), device_id_type=MESH)
+        d = pltpu.make_async_remote_copy(src_ref=zs.at[z], dst_ref=zs.at[z], send_sem=ns.at[6 + k], recv_sem=nr.at[6 + k], device_id=place.along_z(k), device_id_type=MESH)
         d.start()
         made.append(d)
     for d in made:
@@ -316,7 +327,7 @@
     total = zs[0]
     for k in range(1, n_z):
         total = total + zs[k]
-    out[...] = total
+    out[...] = jnp.broadcast_to(jnp.sqrt(jnp.sum(total, keepdims=True)), out.shape)
 
 
 def backward_kernel(n_z, plan, names, *refs):
@@ -324,7 +335,7 @@
     ss, rs, ls, ns, nr, ws, ps, pr, lt_sem, rhs_sem, out_sem = refs[len(names) :]
     own_grads = (b.g_qkv, b.g_out, b.g_up, b.g_down, b.g_tiny)
     place = Place(n_z)
-    greet(place)
+    greet(place, True)
     core, A = place.at["c"], slice(None)
     queries_n, model = b.q.shape
     key_rows = b.keys.shape[0]
@@ -423,6 +434,7 @@
     def attend_back(g):
         if g == 0:
             keys_in.wait()
+            b.bias[...] = own_keys(b.counts, media_rows, queries_n, 48)
         base = g * group_width
         n_tiles = group_width // 128
         last = {t: max(j for j, (t0, t1, _) in enumerate(windows) if t0 <= t < t1) for t in range(n_tiles)}
@@ -489,6 +501,8 @@
         frames = step // 48
         d = pltpu.make_async_copy(b.media.at[pl.ds(part * step, step)], b.mrows, ws.at[3])
         d.start()
+        if part == 0:
+            b.hot[...] = time_table_rows(b.counts, media_rows, 48, 128, 8)
         d.wait()
 
         def frame(i, carry):
@@ -497,7 +511,14 @@
             mixed = b.mrows[at, :].astype(f32) + dot(b.hot[whole, :], b.tiny_t[...].astype(bf))
             back, gain = norm_back(mixed, b.k[whole, :].astype(f32), b.tiny_t[8:9, :])
             b.gsmall[8:9, :] += gain
-            b.gsmall[0:8, :] += b.hotc[part * frames + i][:, 0:1] * jnp.sum(back, axis=0, keepdims=True)
+            f = part * frames + i
+            ends = frame_ends(b.counts)
+            time = f
+            for s, end in enumerate(ends):
+                time = time - jnp.where(f >= end, b.counts[s], 0)
+            time = jnp.where(f < ends[-1], time, -1)
+            at_time = jnp.where(lax.broadcasted_iota(jnp.int32, (8, 1), 0) == time, 1.0, 0.0)
+            b.gsmall[0:8, :] += at_time * jnp.sum(back, axis=0, keepdims=True)
             return carry
 
         lax.fori_loop(0, frames, frame, 0)
@@ -681,17 +702,19 @@
     return stages + [[(4, (0, 48), (0, 128), ("x", "y", "z"))]]
 
 
-def backward_all(full, made, lat, media, hot, hotc, bias, shards, n_z):
+def backward_all(full, made, lat, media, counts, n_z):
     queries_n, model = lat.shape
     media_rows = media.shape[0]
     key_rows = queries_n + media_rows
+    shards = [jax.ShapeDtypeStruct(f.shape[4:], f.dtype) for f in full]
     hidden_n = shards[2].shape[1]
     plan, count = number(backward_plan(shards, model))
     q, k, v, dpre, mid, new, lse, p_keys, p_lat, p_att, p_hid, p_act, p_cot = made
     given = dict(f_qkv=full[0], f_out=full[1], f_up=full[2], f_tiny=full[4], dpre=dpre, p_keys=p_keys, p_lat=p_lat, p_att=p_att, p_hid=p_hid, p_act=p_act, p_cot=p_cot,
-                 media=media, q=q, keys=k, v=v, mid=mid, lse=lse, lat=lat, hot=hot, hotc=hotc, bias=bias)
+                 media=media, q=q, keys=k, v=v, mid=mid, lse=lse, lat=lat, counts=counts)
     bf, f32 = jnp.bfloat16, jnp.float32
-    grads = [((s.shape[0], s.shape[1]), f32) for s in shards]
+    grads = [(s.shape, f32) for s in shards]
+    grads[0] = ((3, shards[1].shape[0], model), f32)
     outs = dict(g_qkv=grads[0], g_out=grads[1], g_up=grads[2], g_down=grads[3], g_tiny=grads[4], d_lat=((queries_n, model), f32), norm=((8, 128), f32),
                 x_dpre=((queries_n, hidden_n), bf), x_branch=((queries_n, model), bf), x_dq=((queries_n, model), bf), x_dk=((key_rows, model), bf), x_dv=((key_rows, model), bf),
                 x_tiny=((2, n_z, 2, 48, 128), bf))
@@ -699,25 +722,66 @@
     vm = dict(s0a=((S, 2, n_z, 2, 48, W), bf), r1a=((L, n_z, 2, 48, W), bf), s1a=((S, n_z, 2, 48, W), bf), r2a=((L, n_z, 48, W), bf), s2a=((S, n_z, 48, W), bf), rza=((L, 2, n_z - 1, 48, W), bf), oa=((S, 48, W), f32),
               s0b=((S, 2, n_z, 2, 48, W), bf), r1b=((L, 2, n_z, 48, W), bf), s1b=((S, 2, n_z, 48, W), bf), r2b=((L, n_z, 48, W), bf), s2b=((S, n_z, 48, W), bf), rzb=((L, 2, n_z - 1, 48, W), bf), ob=((S, 48, W), f32),
               s0c=((S, 2, n_z, 2, 48, 128), bf), rzc=((L, 2, n_z - 1, 2, 2, 48, 128), bf), r1c=((L, 2, 48, 128), bf), s1c=((S, 2, 2, 48, 128), bf), s2c=((S, 2, 48, 128), bf), r2c=((L, 48, 128), bf), oc=((S, 48, 128), f32),
-          sq=((48, W), f32), n=((6, 8, 128), f32), nz=((n_z, 8, 128), f32),
+          sq=((48, W), f32), n=((8, 8, 128), f32), nz=((n_z, 8, 128), f32),
           wbuf=((3, n_z, 2, 48, model), bf), dmid=((queries_n, model), f32), dbranch=((queries_n, model), bf), datt=((queries_n, model), bf),
-          dq=((queries_n, model), bf), k=((key_rows, model), bf), dk=((key_rows, model), bf), dv=((key_rows, model), bf), tiny=((2, 2, n_z, 2, 48, 128), bf), tiny_t=((128, model), f32),
+          bias=((key_rows, queries_n), f32), hot=((media_rows, 128), bf), dq=((queries_n, model), bf), k=((key_rows, model), bf), dk=((key_rows, model), bf), dv=((key_rows, model), bf), tiny=((2, 2, n_z, 2, 48, 128), bf), tiny_t=((128, model), f32),
           gsmall=((128, model), f32), tiny2=((2, n_z, 2, 48, 128), bf), mrows=((media_rows // 6, model), bf),
           lt=(p_act.shape, bf), ltk=(p_keys.shape, bf), rhs=((2, 2, queries_n, 768), bf), rhsk=((key_rows, 768), bf))
     sem = pltpu.SemaphoreType.DMA
     in_vmem, in_any = pl.BlockSpec(memory_space=pltpu.VMEM), pl.BlockSpec(memory_space=ANY)
-    resident = tuple(id(a) for a in (q, v, mid, lse, lat, hot, hotc, bias))
+    resident = tuple(id(a) for a in (q, v, mid, lse, lat))
     n_copies = count * n_sems(n_z)
     res = pl.pallas_call(
         functools.partial(backward_kernel, n_z, plan, (*given, *outs, *vm)),
         out_shape=[jax.ShapeDtypeStruct(*o) for o in outs.values()],
-        in_specs=[in_vmem if id(a) in resident else in_any for a in given.values()],
+        in_specs=[pl.BlockSpec(memory_space=pltpu.SMEM) if a is counts else in_vmem if id(a) in resident else in_any for a in given.values()],
         out_specs=[in_vmem if o is outs["norm"] else in_any for o in outs.values()],
-        scratch_shapes=[pltpu.VMEM(*m) for m in vm.values()] + [sem((n_copies,)), sem((n_copies,)), sem((count,)), sem((n_z + 2,)), sem((n_z + 2,)), sem((5,)), sem((8,)), sem((8,)), sem((1,)), sem((2, 2)), sem((2,))],
+        scratch_shapes=[pltpu.VMEM(*m) for m in vm.values()] + [sem((n_copies,)), sem((n_copies,)), sem((count,)), sem((n_z + 6,)), sem((n_z + 6,)), sem((5,)), sem((8,)), sem((8,)), sem((1,)), sem((2, 2)), sem((2,))],
         name="backward_and_scatter",
         compiler_params=pltpu.CompilerParams(collective_id=1, has_side_effects=True, vmem_limit_bytes=62 * 2**20),
     )(*given.values())
     return types.SimpleNamespace(**dict(zip(outs, res)))
+
+
+def update_kernel(rates, norm, *refs):
+    factor = jnp.minimum(1.0, clip_limit / (norm[0:1, 0:1] + 1e-06))
+    n = len(rates)
+    ws, ms, vs, gs, rows, outs = refs[:n], refs[n : 2 * n], refs[2 * n : 3 * n], refs[3 * n : 4 * n - 1], refs[4 * n - 1 : 4 * n + 1], refs[4 * n + 1 :]
+    for row, o in zip(rows, outs[3 * n :]):
+        o[...] = row[...]
+    outs[-1][...] = norm[0:1, 0:1]
+    small = gs[4][...].T
+    steps = ws[4].shape[0]
+    grads = [g[...] for g in gs[:4]] + [small[0:steps, :], small[steps : steps + 3, :]]
+    for i, g in enumerate(grads):
+        new = adamw_step(ws[i][...], ms[i][...], vs[i][...], g, factor if g.ndim == 2 else factor[None], rates[i])
+        for o, value in zip(outs[3 * i : 3 * i + 3], new):
+            o[...] = value
+
+
+def update_all(norm, masters, firsts, seconds, grads, rows, rates):
+    steps = masters[1].shape[0] // 8
+
+    def spec(a):
+        if a.ndim == 3:
+            return pl.BlockSpec((3, 8, a.shape[2]), lambda i: (0, i, 0))
+        if any(a is r for r in rows):
+            return pl.BlockSpec((64, a.shape[1]), lambda i: (jnp.minimum(i, a.shape[0] // 64 - 1), 0))
+        if a.shape[1] > 128:
+            return pl.BlockSpec((a.shape[0] // steps, a.shape[1]), lambda i: (i, 0))
+        return pl.BlockSpec(a.shape, lambda i: (0, 0))
+
+    args = [norm, *masters, *firsts, *seconds, *grads, *rows]
+    outs = [a for w in masters for a in (w, w, w)] + list(rows) + [jax.ShapeDtypeStruct((1, 1), jnp.float32)]
+    return pl.pallas_call(
+        functools.partial(update_kernel, rates),
+        grid=(steps,),
+        out_shape=[jax.ShapeDtypeStruct(a.shape, a.dtype) for a in outs],
+        in_specs=[spec(a) for a in args],
+        out_specs=[spec(a) for a in outs],
+        name="adamw",
+        compiler_params=pltpu.CompilerParams(vmem_limit_bytes=62 * 2**20),
+    )(*args)
 
 
 def out_copies(pairs, sems, at, running):
@@ -751,15 +815,63 @@
     return centered * lax.rsqrt(var_row + norm_eps) * gain
 
 
+def frame_ends(counts):
+    ends, total = [], 0
+    for s in range(counts.shape[0]):
+        total = total + counts[s]
+        ends.append(total)
+    return ends
+
+
+def time_table_rows(counts, rows, patch, lanes, time_len):
+    row = lax.broadcasted_iota(jnp.int32, (rows, lanes), 0)
+    lane = lax.broadcasted_iota(jnp.int32, (rows, lanes), 1)
+    ends = frame_ends(counts)
+    start = jnp.zeros((rows, lanes), jnp.int32)
+    for s, end in enumerate(ends):
+        start = start + jnp.where(row >= end * patch, counts[s] * patch, 0)
+    off = row - start - lane * patch
+    live = (off >= 0) & (off < patch) & (row < ends[-1] * patch) & (lane < time_len)
+    return jnp.where(live, 1.0, 0.0).astype(jnp.bfloat16)
+
+
+def own_keys(counts, media_rows, queries_n, patch):
+    slots = counts.shape[0]
+    each = queries_n // slots
+    shape = (media_rows + queries_n, queries_n)
+    row = lax.broadcasted_iota(jnp.int32, shape, 0)
+    lane = lax.broadcasted_iota(jnp.int32, shape, 1)
+    owner, asks = jnp.zeros(shape, jnp.int32), jnp.zeros(shape, jnp.int32)
+    for s, end in enumerate(frame_ends(counts)):
+        owner = owner + jnp.where(row >= end * patch, 1, 0)
+        if s + 1 < slots:
+            asks = asks + jnp.where(lane >= (s + 1) * each, 1, 0)
+    mine = jnp.zeros(shape, jnp.int32)
+    for s in range(1, slots):
+        mine = mine + jnp.where(row >= media_rows + s * each, 1, 0)
+    owner = jnp.where(row >= media_rows, mine, owner)
+    return jnp.where(owner == asks, 0.0, -1e30)
+
+
 def forward_kernel(n_z, plan, needs, *refs):
-    (sh, (lat, media, cot, hot, bias), full, outs, scratch) = refs[:5], refs[5:10], refs[10:15], refs[15:27], refs[27:]
+    (w_qkv, w_out, w_up, w_down, w_time, w_gains, lat, media, cot, counts), full, outs, scratch = refs[:10], refs[10:15], refs[15:27], refs[27:]
     o_q, o_k, o_v, o_dpre, o_mid, o_new, o_lse, p_keys, p_lat, p_att, p_hid, p_act = outs[:12]
     p_cot, *scratch = scratch
-    keys, q, k, v, att, hid, act, slope, dact, mid, new, tiny, tiny_t, lse, wbuf, wdown, flip, flip_keys, ss, rs, ls, os_, ws, ps, pr, pl_ = scratch
+    *sh, small, hot, bias = scratch[:8]
+    keys, q, k, v, att, hid, act, slope, dact, mid, new, tiny, tiny_t, lse, wbuf, wdown, flip, flip_keys, ss, rs, ls, os_, ws, ps, pr, pl_ = scratch[8:]
     f_qkv, f_out, f_up, f_down, f_tiny = full
     place = Place(n_z)
+    queries_n, model = lat.shape
+    for i in range(3):
+        sh[0][:, i * model : (i + 1) * model] = w_qkv[i].astype(jnp.bfloat16)
+    for low, w in zip(sh[1:4], (w_out, w_up, w_down)):
+        low[...] = w[...].astype(jnp.bfloat16)
+    time_len = w_time.shape[0]
+    small[...] = jnp.zeros_like(small)
+    small[0:time_len, :] = w_time[...]
+    small[time_len : time_len + 3, :] = w_gains[...]
+    sh[4][...] = small[...].T.astype(jnp.bfloat16)
     greet(place)
-    queries_n, model = lat.shape
     media_rows = media.shape[0]
     key_rows = media_rows + queries_n
     hidden_n = act.shape[1]
@@ -808,6 +920,7 @@
         out_copies(pairs, os_, 0, written)
 
     def norms():
+        hot[...] = time_table_rows(counts, media_rows, 48, hot.shape[1], time_len)
         load(f_tiny, tiny)
         tiny_t[...] = tiny[...].reshape(model, 128).astype(jnp.float32).T
         give(cot, p_cot.at[core], False)
@@ -860,6 +973,8 @@
         write((v, o_v))
 
     def attend(g):
+        if g == 0:
+            bias[...] = own_keys(counts, media_rows, queries_n, 48)
         base = g * group_width
         tiles = [jnp.zeros((queries_n, 128), jnp.float32) for _ in range(group_width // 128)]
         for j, (t0, t1, start) in enumerate(windows):
@@ -1039,18 +1154,20 @@
     return stages, needs
 
 
-def forward_all(shards, lat, media, cot, hot, bias, n_z):
-    model, hidden_n = lat.shape[1], shards[2].shape[1]
+def forward_all(weights, lat, media, cot, counts, n_z):
+    bf, f32 = jnp.bfloat16, jnp.float32
+    rows, model = weights[1].shape
+    hidden_n = weights[2].shape[1]
+    shards = [jax.ShapeDtypeStruct(s, bf) for s in ((rows, 3 * model), weights[1].shape, weights[2].shape, weights[3].shape, (rows, 128))]
     stages, needs = forward_plan(shards, model)
     plan, count = number(stages)
     queries_n, media_rows = lat.shape[0], media.shape[0]
     key_rows = queries_n + media_rows
-    bf, f32 = jnp.bfloat16, jnp.float32
-    rows = shards[1].shape[0]
     part = (2, 2, 2 * n_z, 48)
     made = [((queries_n, model), bf), ((key_rows, model), bf), ((key_rows, model), bf), ((queries_n, hidden_n), bf), ((queries_n, model), f32), ((queries_n, model), bf), ((HEADS, queries_n), f32),
             (part + (key_rows,), bf), (part + (queries_n,), bf), (part + (queries_n,), bf), (part + (queries_n,), bf), ((2, 2, 2 * n_z * hidden_n // model, 48, queries_n), bf), ((2, queries_n, model), bf)]
-    vm = [((key_rows, model), bf), ((queries_n, model), bf), ((key_rows, model), bf), ((key_rows, model), bf), ((queries_n, model), bf), ((queries_n, model), bf), ((queries_n, hidden_n), bf),
+    vm = [(s.shape, bf) for s in shards] + [((128, rows), f32), ((media_rows, 128), bf), ((key_rows, queries_n), f32)]
+    vm += [((key_rows, model), bf), ((queries_n, model), bf), ((key_rows, model), bf), ((key_rows, model), bf), ((queries_n, model), bf), ((queries_n, model), bf), ((queries_n, hidden_n), bf),
           ((queries_n, hidden_n), f32), ((queries_n, hidden_n), f32), ((queries_n, model), f32), ((queries_n, model), bf),
                      ((2, 2, n_z, 2, rows, 128), bf), ((128, model), f32), ((HEADS, queries_n), f32), ((2, 2, n_z, 2, rows, model), bf), ((2, 2, n_z, 2, shards[3].shape[0], 256), bf),
                      ((12, 8, 48, queries_n), bf), ((2, 8, 48, key_rows), bf)]
@@ -1059,12 +1176,12 @@
     out = pl.pallas_call(
         functools.partial(forward_kernel, n_z, plan, needs),
         out_shape=[jax.ShapeDtypeStruct((2, 2, n_z, 2) + s.shape, s.dtype) for s in shards] + [jax.ShapeDtypeStruct(*m) for m in made],
-        in_specs=[in_vmem] * 10,
+        in_specs=[in_vmem] * 9 + [pl.BlockSpec(memory_space=pltpu.SMEM)],
         out_specs=[in_any] * (5 + len(made)),
         scratch_shapes=[pltpu.VMEM(*m) for m in vm] + [sem((count * n_sems(n_z),)), sem((count * n_sems(n_z),)), sem((5,)), sem((16,)), sem((1,)), sem((48,)), sem((48,)), sem((48,))],
         name="gather_and_forward",
         compiler_params=pltpu.CompilerParams(collective_id=0, has_side_effects=True, vmem_limit_bytes=60 * 2**20),
-    )(*shards, lat, media, cot, hot, bias)
+    )(*weights, lat, media, cot, counts)
     return out[:5], out[5:]
 
 
@@ -1205,35 +1322,35 @@
     m_gains,
     v_gains,
 ):
-    low_qkv = w_qkv.astype(jnp.bfloat16)
-    low_out = w_out.astype(jnp.bfloat16)
-    low_up = w_up.astype(jnp.bfloat16)
-    low_down = w_down.astype(jnp.bfloat16)
-    low_time = time_table.astype(jnp.bfloat16)
-    low_gains = gains.astype(jnp.bfloat16)
     n_dp, n_fsdp = lax.axis_size(DP), lax.axis_size(FSDP)
-    own_rows = w_qkv.shape[0]
-    item_slots, lat_count, model_width = latents.shape
-    frame_slots, patch_rows, _ = media.shape
-    queries_n, media_rows = item_slots * lat_count, frame_slots * patch_rows
-    frame_owner, time_hot = frame_tables(frame_counts, frame_slots, time_table.shape[1])
-    query_owner = jnp.arange(queries_n, dtype=jnp.int32) // lat_count
-    key_owner = jnp.concatenate([jnp.repeat(frame_owner, patch_rows), query_owner], axis=0)
-    allowed = query_owner[:, None] == key_owner[None, :]
-    lows = (low_qkv, low_out, low_up, low_down, low_time, low_gains)
-    if fits_kernels(n_dp, n_fsdp, w_qkv, w_up, w_down, queries_n, frame_slots, patch_rows):
-        new_latents, d_latents, grad_norm, reduced = by_kernels(lows, latents, media, cotangent, time_hot, allowed, n_fsdp // 2)
-    else:
-        new_latents, d_latents, grad_norm, reduced = by_collectives(lows, latents, media, cotangent, time_hot, allowed)
-    factor = jnp.minimum(1.0, clip_limit / (grad_norm + 1e-06))
     masters = (w_qkv, w_out, w_up, w_down, time_table, gains)
     firsts = (m_qkv, m_out, m_up, m_down, m_time, m_gains)
     seconds = (v_qkv, v_out, v_up, v_down, v_time, v_gains)
     rates = (0.02, 0.1, 0.02, 0.01, 0.2, 0.5)
-    updated = []
-    for index in range(6):
-        updated.extend(adamw_step(masters[index], firsts[index], seconds[index], reduced[index], factor, rates[index]))
+    item_slots, lat_count, _ = latents.shape
+    frame_slots, patch_rows, _ = media.shape
+    queries_n = item_slots * lat_count
+    if fits_kernels(n_dp, n_fsdp, w_qkv, w_up, w_down, queries_n, frame_slots, patch_rows):
+        new_latents, d_latents, grad_norm, updated = by_kernels(
+            turned(masters), turned(firsts), turned(seconds), rates, latents, media, cotangent, frame_counts, n_fsdp // 2
+        )
+    else:
+        frame_owner, time_hot = frame_tables(frame_counts, frame_slots, time_table.shape[1])
+        query_owner = jnp.arange(queries_n, dtype=jnp.int32) // lat_count
+        key_owner = jnp.concatenate([jnp.repeat(frame_owner, patch_rows), query_owner], axis=0)
+        allowed = query_owner[:, None] == key_owner[None, :]
+        lows = tuple(w.astype(jnp.bfloat16) for w in masters)
+        new_latents, d_latents, grad_norm, reduced = by_collectives(lows, latents, media, cotangent, time_hot, allowed)
+        factor = jnp.minimum(1.0, clip_limit / (grad_norm + 1e-06))
+        updated = []
+        for index in range(6):
+            updated.extend(adamw_step(masters[index], firsts[index], seconds[index], reduced[index], factor, rates[index]))
     return (new_latents, d_latents, grad_norm, *updated)
+
+
+def turned(arrays):
+    qkv, out, up, down, time, gain = arrays
+    return qkv.transpose(1, 0, 2), out, up, down, time.T, gain.T
 
 
 def fits_kernels(n_dp, n_fsdp, w_qkv, w_up, w_down, queries_n, frame_slots, patch_rows):
@@ -1244,26 +1361,16 @@
     )
 
 
-def by_kernels(lows, latents, media, cotangent, time_hot, allowed, n_z):
-    low_qkv, low_out, low_up, low_down, low_time, low_gains = lows
-    own_rows, _, model = low_qkv.shape
-    time_len = low_time.shape[1]
-    queries_n = allowed.shape[0]
-    frame_slots, patch_rows, _ = media.shape
-    tiny = jnp.concatenate([low_time, low_gains], axis=1)
-    shards = [low_qkv.reshape(own_rows, -1), low_out, low_up, low_down, jnp.pad(tiny, ((0, 0), (0, 128 - tiny.shape[1])))]
-    hot = jnp.pad(jnp.repeat(time_hot, patch_rows, axis=0), ((0, 0), (0, 128 - time_len))).astype(jnp.bfloat16)
-    hotc = jnp.broadcast_to(time_hot[:, :, None], time_hot.shape + (128,))
-    bias = jnp.where(allowed.T, 0.0, -1e30).astype(jnp.float32)
-    lat = latents.reshape(queries_n, model)
-    med = media.reshape(frame_slots * patch_rows, model)
-    full, made = forward_all(shards, lat, med, cotangent.reshape(queries_n, model), hot, bias, n_z)
-    own = backward_all(full, made, lat, med, hot, hotc, bias, shards, n_z)
-    small = own.g_tiny
-    reduced = (
-        own.g_qkv.reshape(low_qkv.shape), own.g_out, own.g_up, own.g_down, small[:, :time_len], small[:, time_len : time_len + 3]
-    )
-    return made[5].reshape(latents.shape), own.d_lat.reshape(latents.shape), jnp.sqrt(jnp.sum(own.norm)), reduced
+def by_kernels(masters, firsts, seconds, rates, latents, media, cotangent, counts, n_z):
+    model = latents.shape[2]
+    lat, med, cot = (a.reshape(-1, model) for a in (latents, media, cotangent))
+    full, made = forward_all(masters, lat, med, cot, counts, n_z)
+    own = backward_all(full, made, lat, med, counts, n_z)
+    grads = [own.g_qkv, own.g_out, own.g_up, own.g_down, own.g_tiny]
+    *new, new_rows, d_rows, norm = update_all(own.norm, masters, firsts, seconds, grads, (made[5], own.d_lat), rates)
+    kinds = [turned(new[n::3]) for n in range(3)]
+    updated = [kinds[n][i] for i in range(6) for n in range(3)]
+    return new_rows.reshape(latents.shape), d_rows.reshape(latents.shape), norm.reshape(()), updated
 
 
 def by_collectives(lows, latents, media, cotangent, time_hot, allowed):

time: 550 us -> 527 us (0.958)
  other arithmetic: 18.5 us -> 0 us
  local copies, waits for them, and re-layouts: 12.4 us -> 0 us
  Pallas kernels: 509 us -> 520 us
    pallas_call x0 -> x1, Pallas kernels: none -> 12.1 us  [update_all(): pl.pallas_call(functools.partial(update_kernel, rates), grid=(steps,), ou...]
    sub x8 -> x0, other arithmetic: 11.4 us -> none  [the longest x6 10.8 us: adamw_step(): weight - rate * (first_hat / (jnp.sqrt(second_hat) + adam_eps) + decay_ra...]
    unnamed x56 -> x0, local copies, waits for them, and re-layouts: 8.63 us -> none
where the time goes in v5:
time: 527 us; the launch traced here: 521 us
  Pallas kernels  520 us (99%)
    pallas_call x1, Pallas kernels, backward_all(): pl.pallas_call(functools.partial(backward_kernel, n_z, plan, (*given, *ou...  259 us
    pallas_call x1, Pallas kernels, forward_all(): pl.pallas_call(functools.partial(forward_kernel, n_z, plan, needs), out_s...  249 us
    pallas_call x1, Pallas kernels, update_all(): pl.pallas_call(functools.partial(update_kernel, rates), grid=(steps,), ou...  12.1 us

profile of v5, /device:TPU:0, one launch (start us, length us, event | category | flops | bytes accessed | tf_op | source)
XLA Modules:
  0.0 520.6 jit_solution(12831025963831421172)
XLA Ops:
  0.7 248.7 %gather_and_forward.1 = (bf16[2,2,4,2,48,4608]{5,4,3,2,1,0:T(8,128)(2,1)}, bf16[2,2,4,2,48,1536]{5,4,3,2,1,0:T(8,128)(2,1)}, bf16[2,2,4,2,48,6144]{5,4,3,2,1,0:T...) custom-call(f32[3,48,1536]{2,1,0:T(8,128)} %bitcast.26, ...), custom_call_target="tpu_custom_call" | custom-call | tf_op jit(solution)/shard_map/gather_and_forward/pallas_call | solution.py:1176
  249.4 259.0 %backward_and_scatter.1 = (f32[3,48,1536]{2,1,0:T(8,128)}, f32[48,1536]{1,0:T(8,128)}, f32[48,6144]{1,0:T(8,128)}, f32[192,1536]{1,0:T(8,128)}, f32[48,128]{1,0:...) custom-call(bf16[2,2,4,2,48,4608]{5,4,3,2,1,0:T(8,128)(2,1)} %get-tu, ...), custom_call_target="tpu_custom_call" | custom-call | tf_op jit(solution)/shard_map/backward_and_scatter/pallas_call | solution.py:734
  508.3 12.1 %adamw.1 = (f32[3,48,1536]{2,1,0:T(8,128)}, f32[3,48,1536]{2,1,0:T(8,128)}, f32[3,48,1536]{2,1,0:T(8,128)}, f32[48,1536]{1,0:T(8,128)}, f32[48,1536]{1,0:T(8,128...) custom-call(f32[8,128]{1,0:T(8,128)} %get-tuple-element.82.norm, ...), custom_call_target="tpu_custom_call" | custom-call | tf_op jit(solution)/shard_map/adamw/pallas_call | solution.py:776

commit v6 on v5

--- a/solution.py
+++ b/solution.py
@@ -131,8 +131,9 @@
 ZYX, ZXY, XYZ, YXZ = ("z", "y", "x", "c"), ("z", "x", "y", "c"), ("x", "y", "z", "c"), ("y", "x", "z", "c")
 
 BACK_LAG, SEND_SLOTS, LAND_SLOTS = 2, 3, 6
-ROOM_B = 4
+ROOM_B = 3
 FINE_B = 0
+WIDE_B = ((3, 2, 1), (2, 3, 1), (2, 2, 2))
 
 
 class Scatter:
@@ -255,7 +256,7 @@
         elif step == 1 and first == "z":
             self.last_move(0)
             for x in range(2):
-                b.s1[h, x] = b.s0[h, x, at["z"]]
+                b.s1[h, x, :, :, 0 : self.width] = b.s0[h, x, at["z"], :, :, 0 : self.width]
             self.send(1, self.v(b.s1, h, 1 - at["x"], A), self.v(b.r1, n, A), "x")
         elif step == 1:
             self.sent[0].wait_recv()
@@ -334,10 +335,21 @@
     b = types.SimpleNamespace(**dict(zip(names, refs)))
     ss, rs, ls, ns, nr, ws, ps, pr, lt_sem, rhs_sem, out_sem = refs[len(names) :]
     own_grads = (b.g_qkv, b.g_out, b.g_up, b.g_down, b.g_tiny)
+    early = [
+        pltpu.make_async_copy(src, dst, out_sem.at[1 + n])
+        for n, (src, dst) in enumerate(((b.p_act, b.lt), (b.mid_in, b.mid), (b.q_in, b.q), (b.keys, b.k), (b.v_in, b.v), (b.lat_in, b.lat)))
+    ]
+    for d in early:
+        d.start()
+
+    def here(*which):
+        for n in which:
+            early[n].wait()
+
     place = Place(n_z)
     greet(place, True)
     core, A = place.at["c"], slice(None)
-    queries_n, model = b.q.shape
+    queries_n, model = b.q_in.shape
     key_rows = b.keys.shape[0]
     media_rows = key_rows - queries_n
     hidden_n = b.dpre.shape[1]
@@ -361,8 +373,6 @@
             held_copy[1] = True
 
     give(b.dpre, b.x_dpre)
-    keys_in = pltpu.make_async_copy(b.keys, b.k, out_sem.at[1])
-    keys_in.start()
 
     wbuf = b.wbuf
 
@@ -410,6 +420,7 @@
         e.start()
         d.wait()
         e.wait()
+        here(1)
         b.tiny_t[...] = b.tiny[...].reshape(model, 128).astype(f32).T
         b.gsmall[...] = jnp.zeros_like(b.gsmall)
 
@@ -433,7 +444,7 @@
 
     def attend_back(g):
         if g == 0:
-            keys_in.wait()
+            here(2, 3, 4)
             b.bias[...] = own_keys(b.counts, media_rows, queries_n, 48)
         base = g * group_width
         n_tiles = group_width // 128
@@ -481,6 +492,8 @@
             b.k[rows, cols] = (dot(b.dk[rows, :], w[1], ((1,), (1,))) + dot(b.dv[rows, :], w[2], ((1,), (1,)))).astype(bf)
 
     def latents_back():
+        here(5)
+
         def rows(i, carry):
             at = pl.ds(pl.multiple_of(i * 64, 64), 64)
             grad = b.k[pl.ds(pl.multiple_of(media_rows + i * 64, 16), 64), :].astype(f32)
@@ -531,6 +544,10 @@
 
     def left(src):
         if held[0] is src:
+            return
+        if held[0] is None:
+            here(0)
+            held[0] = src
             return
         held[0] = src
         if src is b.p_keys:
@@ -684,7 +701,7 @@
     stages = []
 
     def split(w, row, first, widths=None):
-        widths = widths or ((3, 2, 1), (2, 3, 1))[len(stages) % 2]
+        widths = widths or WIDE_B[len(stages) % len(WIDE_B)]
         at, pieces = first, []
         for width, order in zip(widths, (("x", "y", "z"), ("y", "x", "z"), ("z", "x", "y"))):
             pieces.append((w, (row, 48), (at, width * tile), order))
@@ -711,7 +728,7 @@
     plan, count = number(backward_plan(shards, model))
     q, k, v, dpre, mid, new, lse, p_keys, p_lat, p_att, p_hid, p_act, p_cot = made
     given = dict(f_qkv=full[0], f_out=full[1], f_up=full[2], f_tiny=full[4], dpre=dpre, p_keys=p_keys, p_lat=p_lat, p_att=p_att, p_hid=p_hid, p_act=p_act, p_cot=p_cot,
-                 media=media, q=q, keys=k, v=v, mid=mid, lse=lse, lat=lat, counts=counts)
+                 media=media, q_in=q, keys=k, v_in=v, mid_in=mid, lse=lse, lat_in=lat, counts=counts)
     bf, f32 = jnp.bfloat16, jnp.float32
     grads = [(s.shape, f32) for s in shards]
     grads[0] = ((3, shards[1].shape[0], model), f32)
@@ -719,24 +736,25 @@
                 x_dpre=((queries_n, hidden_n), bf), x_branch=((queries_n, model), bf), x_dq=((queries_n, model), bf), x_dk=((key_rows, model), bf), x_dv=((key_rows, model), bf),
                 x_tiny=((2, n_z, 2, 48, 128), bf))
     W, S, L = 384, SEND_SLOTS, LAND_SLOTS
+    N = max(w[2] for w in WIDE_B) * 128
     vm = dict(s0a=((S, 2, n_z, 2, 48, W), bf), r1a=((L, n_z, 2, 48, W), bf), s1a=((S, n_z, 2, 48, W), bf), r2a=((L, n_z, 48, W), bf), s2a=((S, n_z, 48, W), bf), rza=((L, 2, n_z - 1, 48, W), bf), oa=((S, 48, W), f32),
               s0b=((S, 2, n_z, 2, 48, W), bf), r1b=((L, 2, n_z, 48, W), bf), s1b=((S, 2, n_z, 48, W), bf), r2b=((L, n_z, 48, W), bf), s2b=((S, n_z, 48, W), bf), rzb=((L, 2, n_z - 1, 48, W), bf), ob=((S, 48, W), f32),
-              s0c=((S, 2, n_z, 2, 48, 128), bf), rzc=((L, 2, n_z - 1, 2, 2, 48, 128), bf), r1c=((L, 2, 48, 128), bf), s1c=((S, 2, 2, 48, 128), bf), s2c=((S, 2, 48, 128), bf), r2c=((L, 48, 128), bf), oc=((S, 48, 128), f32),
+              s0c=((S, 2, n_z, 2, 48, N), bf), rzc=((L, 2, n_z - 1, 2, 2, 48, N), bf), r1c=((L, 2, 48, N), bf), s1c=((S, 2, 2, 48, N), bf), s2c=((S, 2, 48, N), bf), r2c=((L, 48, N), bf), oc=((S, 48, N), f32),
           sq=((48, W), f32), n=((8, 8, 128), f32), nz=((n_z, 8, 128), f32),
           wbuf=((3, n_z, 2, 48, model), bf), dmid=((queries_n, model), f32), dbranch=((queries_n, model), bf), datt=((queries_n, model), bf),
-          bias=((key_rows, queries_n), f32), hot=((media_rows, 128), bf), dq=((queries_n, model), bf), k=((key_rows, model), bf), dk=((key_rows, model), bf), dv=((key_rows, model), bf), tiny=((2, 2, n_z, 2, 48, 128), bf), tiny_t=((128, model), f32),
+          q=(q.shape, bf), v=(v.shape, bf), mid=(mid.shape, f32), lat=(lat.shape, bf), bias=((key_rows, queries_n), f32), hot=((media_rows, 128), bf), dq=((queries_n, model), bf), k=((key_rows, model), bf), dk=((key_rows, model), bf), dv=((key_rows, model), bf), tiny=((2, 2, n_z, 2, 48, 128), bf), tiny_t=((128, model), f32),
           gsmall=((128, model), f32), tiny2=((2, n_z, 2, 48, 128), bf), mrows=((media_rows // 6, model), bf),
           lt=(p_act.shape, bf), ltk=(p_keys.shape, bf), rhs=((2, 2, queries_n, 768), bf), rhsk=((key_rows, 768), bf))
     sem = pltpu.SemaphoreType.DMA
     in_vmem, in_any = pl.BlockSpec(memory_space=pltpu.VMEM), pl.BlockSpec(memory_space=ANY)
-    resident = tuple(id(a) for a in (q, v, mid, lse, lat))
+    resident = tuple(id(a) for a in (lse,))
     n_copies = count * n_sems(n_z)
     res = pl.pallas_call(
         functools.partial(backward_kernel, n_z, plan, (*given, *outs, *vm)),
         out_shape=[jax.ShapeDtypeStruct(*o) for o in outs.values()],
         in_specs=[pl.BlockSpec(memory_space=pltpu.SMEM) if a is counts else in_vmem if id(a) in resident else in_any for a in given.values()],
         out_specs=[in_vmem if o is outs["norm"] else in_any for o in outs.values()],
-        scratch_shapes=[pltpu.VMEM(*m) for m in vm.values()] + [sem((n_copies,)), sem((n_copies,)), sem((count,)), sem((n_z + 6,)), sem((n_z + 6,)), sem((5,)), sem((8,)), sem((8,)), sem((1,)), sem((2, 2)), sem((2,))],
+        scratch_shapes=[pltpu.VMEM(*m) for m in vm.values()] + [sem((n_copies,)), sem((n_copies,)), sem((count,)), sem((n_z + 6,)), sem((n_z + 6,)), sem((5,)), sem((8,)), sem((8,)), sem((1,)), sem((2, 2)), sem((7,))],
         name="backward_and_scatter",
         compiler_params=pltpu.CompilerParams(collective_id=1, has_side_effects=True, vmem_limit_bytes=62 * 2**20),
     )(*given.values())
@@ -854,14 +872,17 @@
 
 
 def forward_kernel(n_z, plan, needs, *refs):
-    (w_qkv, w_out, w_up, w_down, w_time, w_gains, lat, media, cot, counts), full, outs, scratch = refs[:10], refs[10:15], refs[15:27], refs[27:]
+    (w_qkv, w_out, w_up, w_down, w_time, w_gains, lat_in, media_in, cot_in, counts), full, outs, scratch = refs[:10], refs[10:15], refs[15:27], refs[27:]
     o_q, o_k, o_v, o_dpre, o_mid, o_new, o_lse, p_keys, p_lat, p_att, p_hid, p_act = outs[:12]
     p_cot, *scratch = scratch
-    *sh, small, hot, bias = scratch[:8]
-    keys, q, k, v, att, hid, act, slope, dact, mid, new, tiny, tiny_t, lse, wbuf, wdown, flip, flip_keys, ss, rs, ls, os_, ws, ps, pr, pl_ = scratch[8:]
+    *sh, small, hot, bias, lat, media, cot = scratch[:11]
+    keys, q, k, v, att, hid, act, slope, dact, mid, new, tiny, tiny_t, lse, wbuf, wdown, flip, flip_keys, ss, rs, ls, os_, ws, ps, pr, pl_, ins = scratch[11:]
     f_qkv, f_out, f_up, f_down, f_tiny = full
     place = Place(n_z)
     queries_n, model = lat.shape
+    coming = [pltpu.make_async_copy(src, dst, ins.at[n]) for n, (src, dst) in enumerate(((lat_in, lat), (cot_in, cot), (media_in, media)))]
+    for d in coming:
+        d.start()
     for i in range(3):
         sh[0][:, i * model : (i + 1) * model] = w_qkv[i].astype(jnp.bfloat16)
     for low, w in zip(sh[1:4], (w_out, w_up, w_down)):
@@ -920,6 +941,8 @@
         out_copies(pairs, os_, 0, written)
 
     def norms():
+        for d in coming:
+            d.wait()
         hot[...] = time_table_rows(counts, media_rows, 48, hot.shape[1], time_len)
         load(f_tiny, tiny)
         tiny_t[...] = tiny[...].reshape(model, 128).astype(jnp.float32).T
@@ -1116,7 +1139,8 @@
 
 ROOM_A = 12
 LAG = 2
-FINE = 1
+FINE = 2
+WIDE_A = ((5, 5, 2), (5, 4, 3), (5, 5, 2), (4, 5, 3))
 Z_DOWN = (1,)
 
 
@@ -1130,16 +1154,17 @@
 
     rows = shards[1].shape[0]
     stages, needs = [[(4, (0, rows), (0, 128), ZYX)]], {"tiny": 0}
-    wide = model * 5 // 12, model * 5 // 12, model // 6
+    twelfth = model // 12
+    widths = [tuple(n * twelfth for n in WIDE_A[i % len(WIDE_A)]) for i in range(4 + shards[2].shape[1] // model)]
     for i, name in enumerate("qkv"):
         needs[name] = len(stages)
-        stages.append(split(0, rows, i * model, wide, (XYZ, YXZ)[i % 2]))
+        stages.append(split(0, rows, i * model, widths[i], (XYZ, YXZ)[i % 2]))
     needs["out"] = len(stages)
-    stages.append(split(1, rows, 0, wide, YXZ))
+    stages.append(split(1, rows, 0, widths[3], YXZ))
     needs["up"], needs["down"] = [], []
     for i in range(shards[2].shape[1] // model):
         needs["up"].append(len(stages))
-        stages.append(split(2, rows, i * model, wide, (XYZ, YXZ)[i % 2]))
+        stages.append(split(2, rows, i * model, widths[4 + i], (XYZ, YXZ)[i % 2]))
     groups = model // 256
     deep = shards[3].shape[0]
     for i in range(groups):
@@ -1166,7 +1191,7 @@
     part = (2, 2, 2 * n_z, 48)
     made = [((queries_n, model), bf), ((key_rows, model), bf), ((key_rows, model), bf), ((queries_n, hidden_n), bf), ((queries_n, model), f32), ((queries_n, model), bf), ((HEADS, queries_n), f32),
             (part + (key_rows,), bf), (part + (queries_n,), bf), (part + (queries_n,), bf), (part + (queries_n,), bf), ((2, 2, 2 * n_z * hidden_n // model, 48, queries_n), bf), ((2, queries_n, model), bf)]
-    vm = [(s.shape, bf) for s in shards] + [((128, rows), f32), ((media_rows, 128), bf), ((key_rows, queries_n), f32)]
+    vm = [(s.shape, bf) for s in shards] + [((128, rows), f32), ((media_rows, 128), bf), ((key_rows, queries_n), f32), (lat.shape, bf), (media.shape, bf), (cot.shape, bf)]
     vm += [((key_rows, model), bf), ((queries_n, model), bf), ((key_rows, model), bf), ((key_rows, model), bf), ((queries_n, model), bf), ((queries_n, model), bf), ((queries_n, hidden_n), bf),
           ((queries_n, hidden_n), f32), ((queries_n, hidden_n), f32), ((queries_n, model), f32), ((queries_n, model), bf),
                      ((2, 2, n_z, 2, rows, 128), bf), ((128, model), f32), ((HEADS, queries_n), f32), ((2, 2, n_z, 2, rows, model), bf), ((2, 2, n_z, 2, shards[3].shape[0], 256), bf),
@@ -1176,9 +1201,9 @@
     out = pl.pallas_call(
         functools.partial(forward_kernel, n_z, plan, needs),
         out_shape=[jax.ShapeDtypeStruct((2, 2, n_z, 2) + s.shape, s.dtype) for s in shards] + [jax.ShapeDtypeStruct(*m) for m in made],
-        in_specs=[in_vmem] * 9 + [pl.BlockSpec(memory_space=pltpu.SMEM)],
+        in_specs=[in_vmem] * 6 + [in_any] * 3 + [pl.BlockSpec(memory_space=pltpu.SMEM)],
         out_specs=[in_any] * (5 + len(made)),
-        scratch_shapes=[pltpu.VMEM(*m) for m in vm] + [sem((count * n_sems(n_z),)), sem((count * n_sems(n_z),)), sem((5,)), sem((16,)), sem((1,)), sem((48,)), sem((48,)), sem((48,))],
+        scratch_shapes=[pltpu.VMEM(*m) for m in vm] + [sem((count * n_sems(n_z),)), sem((count * n_sems(n_z),)), sem((5,)), sem((16,)), sem((1,)), sem((48,)), sem((48,)), sem((48,)), sem((3,))],
         name="gather_and_forward",
         compiler_params=pltpu.CompilerParams(collective_id=0, has_side_effects=True, vmem_limit_bytes=60 * 2**20),
     )(*weights, lat, media, cot, counts)

time: 527 us -> 515 us (0.977)
  Pallas kernels: 520 us -> 507 us
    pallas_call x1, Pallas kernels: 249 us -> 240 us  [forward_all(): pl.pallas_call(functools.partial(forward_kernel, n_z, plan, needs), out_s...]
where the time goes in v6:
time: 515 us; the launch traced here: 508 us
  Pallas kernels  507 us (98%)
    pallas_call x1, Pallas kernels, backward_all(): pl.pallas_call(functools.partial(backward_kernel, n_z, plan, (*given, *ou...  255 us
    pallas_call x1, Pallas kernels, forward_all(): pl.pallas_call(functools.partial(forward_kernel, n_z, plan, needs), out_s...  240 us
    pallas_call x1, Pallas kernels, update_all(): pl.pallas_call(functools.partial(update_kernel, rates), grid=(steps,), ou...  12.1 us

profile of v6, /device:TPU:0, one launch (start us, length us, event | category | flops | bytes accessed | tf_op | source)
XLA Modules:
  0.0 508.1 jit_solution(1912787038093919296)
XLA Ops:
  0.7 240.5 %gather_and_forward.1 = (bf16[2,2,4,2,48,4608]{5,4,3,2,1,0:T(8,128)(2,1)}, bf16[2,2,4,2,48,1536]{5,4,3,2,1,0:T(8,128)(2,1)}, bf16[2,2,4,2,48,6144]{5,4,3,2,1,0:T...) custom-call(f32[3,48,1536]{2,1,0:T(8,128)} %bitcast.26, ...), custom_call_target="tpu_custom_call" | custom-call | tf_op jit(solution)/shard_map/gather_and_forward/pallas_call | solution.py:1201
  241.1 254.7 %backward_and_scatter.1 = (f32[3,48,1536]{2,1,0:T(8,128)}, f32[48,1536]{1,0:T(8,128)}, f32[48,6144]{1,0:T(8,128)}, f32[192,1536]{1,0:T(8,128)}, f32[48,128]{1,0:...) custom-call(bf16[2,2,4,2,48,4608]{5,4,3,2,1,0:T(8,128)(2,1)} %get-tu, ...), custom_call_target="tpu_custom_call" | custom-call | tf_op jit(solution)/shard_map/backward_and_scatter/pallas_call | solution.py:752
  495.8 12.1 %adamw.1 = (f32[3,48,1536]{2,1,0:T(8,128)}, f32[3,48,1536]{2,1,0:T(8,128)}, f32[3,48,1536]{2,1,0:T(8,128)}, f32[48,1536]{1,0:T(8,128)}, f32[48,1536]{1,0:T(8,128...) custom-call(f32[8,128]{1,0:T(8,128)} %get-tuple-element.82.norm, ...), custom_call_target="tpu_custom_call" | custom-call | tf_op jit(solution)/shard_map/adamw/pallas_call | solution.py:794

commit v7 on v6

--- a/solution.py
+++ b/solution.py
@@ -1066,20 +1066,18 @@
             w = wdown[b // 2, b % 2].reshape(per, width)
             got = got + dot(act[:, b * per : (b + 1) * per], w)
             back = dot(cot[:, cols], w, ((1,), (1,)))
-            if i == 0:
+            part = slice(b * per, (b + 1) * per)
+            if (i + 1) * width == model:
+                act[:, part] = ((dact[:, part] + back) * slope[:, part]).astype(jnp.bfloat16)
+                write((act.at[:, part], o_dpre.at[:, part]))
+            elif i == 0:
                 dact[:, b * per : (b + 1) * per] = back
             else:
                 dact[:, b * per : (b + 1) * per] += back
         new[:, cols] = (mid[:, cols] + got).astype(jnp.bfloat16)
 
     def finish():
-        def tile(n, carry):
-            cols = pl.ds(pl.multiple_of(n * 512, 512), 512)
-            act[:, cols] = (dact[:, cols] * slope[:, cols]).astype(jnp.bfloat16)
-            return carry
-
-        lax.fori_loop(0, hidden_n // 512, tile, 0)
-        write((act, o_dpre), (new, o_new))
+        write((new, o_new))
         for d in written:
             d.wait()
         for n, (d, theirs, done) in enumerate(given):

time: 515 us -> 514 us (level)
  no operation moved by 1% of the time
where the time goes in v7:
time: 514 us; the launch traced here: 507 us
  Pallas kernels  506 us (98%)
    pallas_call x1, Pallas kernels, backward_all(): pl.pallas_call(functools.partial(backward_kernel, n_z, plan, (*given, *ou...  255 us
    pallas_call x1, Pallas kernels, forward_all(): pl.pallas_call(functools.partial(forward_kernel, n_z, plan, needs), out_s...  239 us
    pallas_call x1, Pallas kernels, update_all(): pl.pallas_call(functools.partial(update_kernel, rates), grid=(steps,), ou...  12.1 us

profile of v7, /device:TPU:0, one launch (start us, length us, event | category | flops | bytes accessed | tf_op | source)
XLA Modules:
  0.0 506.8 jit_solution(3377687706233260991)
XLA Ops:
  0.7 239.1 %gather_and_forward.1 = (bf16[2,2,4,2,48,4608]{5,4,3,2,1,0:T(8,128)(2,1)}, bf16[2,2,4,2,48,1536]{5,4,3,2,1,0:T(8,128)(2,1)}, bf16[2,2,4,2,48,6144]{5,4,3,2,1,0:T...) custom-call(f32[3,48,1536]{2,1,0:T(8,128)} %bitcast.26, ...), custom_call_target="tpu_custom_call" | custom-call | tf_op jit(solution)/shard_map/gather_and_forward/pallas_call | solution.py:1199
  239.8 254.7 %backward_and_scatter.1 = (f32[3,48,1536]{2,1,0:T(8,128)}, f32[48,1536]{1,0:T(8,128)}, f32[48,6144]{1,0:T(8,128)}, f32[192,1536]{1,0:T(8,128)}, f32[48,128]{1,0:...) custom-call(bf16[2,2,4,2,48,4608]{5,4,3,2,1,0:T(8,128)(2,1)} %get-tu, ...), custom_call_target="tpu_custom_call" | custom-call | tf_op jit(solution)/shard_map/backward_and_scatter/pallas_call | solution.py:752
  494.5 12.1 %adamw.1 = (f32[3,48,1536]{2,1,0:T(8,128)}, f32[3,48,1536]{2,1,0:T(8,128)}, f32[3,48,1536]{2,1,0:T(8,128)}, f32[48,1536]{1,0:T(8,128)}, f32[48,1536]{1,0:T(8,128...) custom-call(f32[8,128]{1,0:T(8,128)} %get-tuple-element.82.norm, ...), custom_call_target="tpu_custom_call" | custom-call | tf_op jit(solution)/shard_map/adamw/pallas_call | solution.py:794
